TPU v7x, 32 devices: a whole 2x2x4 slice. The times are simulated.
32 devices in a mesh: dp: 8 (over z, y), seq: 4 (over x, core).
Axes of the slice: x: 2, y: 2, z: 4, core: 2. Of those that a mesh axis runs over, the one named last changes fastest.
Arguments:
- tokens: bfloat16 [8192, 2048], P(('dp', 'seq')), may hold values from -6 to 6
- row_lengths: int32 [8, 4], P('dp'), may hold values from 1 to 1021, as said below
- branch_weight: bfloat16 [2048, 2560], P(('dp', 'seq')), may hold values from -0.125 to 0.125
- inner_weight: bfloat16 [2048, 2560], P(('dp', 'seq')), may hold values from -0.125 to 0.125
- output_weight: bfloat16 [2560, 2048], P(('dp', 'seq')), may hold values from -0.5 to 0.5
- rate_weight: bfloat16 [2560, 256], P(('dp', 'seq')), may hold values from -0.375 to 0.375
- entry_weight: bfloat16 [2560, 256], P(('dp', 'seq')), may hold values from -0.375 to 0.375
- rate_bias: bfloat16 [2560], P(('dp', 'seq')), may hold values from -3 to 3
- entry_bias: bfloat16 [2560], P(('dp', 'seq')), may hold values from -3 to 3
- conv_weight: bfloat16 [4, 2560], P(None, ('dp', 'seq')), may hold values from -3 to 3
- conv_bias: bfloat16 [2560], P(('dp', 'seq')), may hold values from -2 to 2
- recur_param: bfloat16 [2560], P(('dp', 'seq')), may hold values from 3.8 to 13
- norm_gain: bfloat16 [2048], P(('dp', 'seq')), may hold values from 0.5 to 1.5
- mlp_gain: bfloat16 [2048], P(('dp', 'seq')), may hold values from 0.5 to 1.5
- gate_weight: bfloat16 [2048, 6144], P(None, 'seq'), may hold values from -0.125 to 0.125
- up_weight: bfloat16 [2048, 6144], P(None, 'seq'), may hold values from -0.125 to 0.125
- down_weight: bfloat16 [6144, 2048], P('seq'), may hold values from -0.15625 to 0.15625
- cotangent: bfloat16 [8192, 2048], P(('dp', 'seq')), may hold values from -6 to 6
Outputs:
- result: bfloat16 [8192, 2048], P(('dp', 'seq'))
- grad_tokens: float32 [8192, 2048], P(('dp', 'seq'))
- grad_branch: float32 [2048, 2560], P(('dp', 'seq'))
- grad_inner: float32 [2048, 2560], P(('dp', 'seq'))
- grad_output: float32 [2560, 2048], P(('dp', 'seq'))
- grad_rate: float32 [2560, 256], P(('dp', 'seq'))
- grad_entry: float32 [2560, 256], P(('dp', 'seq'))
- grad_rate_bias: float32 [2560], P(('dp', 'seq'))
- grad_entry_bias: float32 [2560], P(('dp', 'seq'))
- grad_conv: float32 [4, 2560], P(None, ('dp', 'seq'))
- grad_conv_bias: float32 [2560], P(('dp', 'seq'))
- grad_recur: float32 [2560], P(('dp', 'seq'))
- grad_norm_gain: float32 [2048], P(('dp', 'seq'))
- grad_mlp_gain: float32 [2048], P(('dp', 'seq'))
- grad_gate: float32 [2048, 6144], P('dp', 'seq')
- grad_up: float32 [2048, 6144], P('dp', 'seq')
- grad_down: float32 [6144, 2048], P('seq', 'dp')
Inputs may be any that keep to these rules, and one draw needn't show every extreme that they name: `row_lengths`: each group's 4 lengths sum to 1024. In each group one row, at a place drawn from the seed, starts within the first 256 tokens and ends within the last 256; every other row has fewer than 64 tokens.
All inputs are finite; a program needn't handle non-finite values.
Results may differ from a plain program's by a relative error of at most 0.014.
Values may be sent and summed in bfloat16 or wider, within the bound.
A program may use at most 256 MiB of HBM per device.

v0:
```python
from functools import partial

import jax
import jax.numpy as jnp
from jax import lax
from jax.sharding import PartitionSpec as P

R = 2560
BLOCK = 256
WIDTH = 4
HEADS = 10


EPSILON = 1e-06


def shifted(block, axis, distance):
    devices = range(lax.axis_size(axis))
    route = [(i - distance, i) for i in devices if i - distance in devices]
    return lax.ppermute(block, axis, route)


def carried_in(part, axis, combine, identity, reverse):
    count = lax.axis_size(axis)
    place = lax.axis_index(axis)
    ahead = count - 1 - place if reverse else place
    gathered = jax.tree.map(lambda a: lax.all_gather(a, axis), part)
    state = jax.tree.map(lambda a, e: jnp.zeros_like(a) + jnp.asarray(e, a.dtype), part, identity)

    def one(step, state):
        source = count - 1 - step if reverse else step
        return combine(
            state, jax.tree.map(lambda a: lax.dynamic_index_in_dim(a, source, 0, False), gathered)
        )

    return lax.fori_loop(0, ahead, one, state)


def rms_norm(values, gain_vector):
    inv_scale = lax.rsqrt(jnp.mean(values * values, axis=-1, keepdims=True) + EPSILON)
    return values * inv_scale * gain_vector


def combine(earlier, latter):
    return (earlier[0] * latter[0], latter[0] * earlier[1] + latter[1])


def row_offsets(lengths, places):
    row_ends = jnp.cumsum(lengths)
    starts = row_ends - lengths
    row_begin = jnp.max(jnp.where(starts[None, :] <= places[:, None], starts[None, :], 0), axis=1)
    return places - row_begin


def lru_terms(keeping, pre_rate, pre_entry, conv_value, recur_value):
    rate_sig = jax.nn.sigmoid(pre_rate)
    entry_sig = jax.nn.sigmoid(pre_entry)
    decay_base = jnp.exp(-8.0 * rate_sig * jax.nn.softplus(-recur_value))
    sources = jnp.sqrt(1.0 - decay_base * decay_base) * entry_sig * conv_value
    return (decay_base * keeping, sources)


def contract_rows(left_side, right_side):
    return lax.dot_general(
        left_side, right_side, (((0,), (0,)), ((), ())), preferred_element_type=jnp.float32
    )


def contract_cols(left_side, right_side):
    return lax.dot_general(
        left_side, right_side, (((1,), (1,)), ((), ())), preferred_element_type=jnp.float32
    )


def shards(
    tokens,
    row_lengths,
    branch_weight,
    inner_weight,
    output_weight,
    rate_weight,
    entry_weight,
    rate_bias,
    entry_bias,
    conv_weight,
    conv_bias,
    recur_param,
    norm_gain,
    mlp_gain,
    gate_weight,
    up_weight,
    down_weight,
    cotangent,
):
    sharded = (
        branch_weight,
        inner_weight,
        output_weight,
        rate_weight,
        entry_weight,
        rate_bias,
        entry_bias,
        conv_weight,
        conv_bias,
        recur_param,
        norm_gain,
        mlp_gain,
    )
    gathered = (
        lax.all_gather(sharded[0], ("dp", "seq"), axis=0, tiled=True),
        lax.all_gather(sharded[1], ("dp", "seq"), axis=0, tiled=True),
        lax.all_gather(sharded[2], ("dp", "seq"), axis=0, tiled=True),
        lax.all_gather(sharded[3], ("dp", "seq"), axis=0, tiled=True),
        lax.all_gather(sharded[4], ("dp", "seq"), axis=0, tiled=True),
        lax.all_gather(sharded[5], ("dp", "seq"), axis=0, tiled=True),
        lax.all_gather(sharded[6], ("dp", "seq"), axis=0, tiled=True),
        lax.all_gather(sharded[7], ("dp", "seq"), axis=1, tiled=True),
        lax.all_gather(sharded[8], ("dp", "seq"), axis=0, tiled=True),
        lax.all_gather(sharded[9], ("dp", "seq"), axis=0, tiled=True),
        lax.all_gather(sharded[10], ("dp", "seq"), axis=0, tiled=True),
        lax.all_gather(sharded[11], ("dp", "seq"), axis=0, tiled=True),
    )
    tok_count = tokens.shape[0]
    seq_index = lax.axis_index("seq")
    places = seq_index * tok_count + jnp.arange(tok_count + WIDTH - 1, dtype=jnp.int32)
    offsets_all = row_offsets(row_lengths[0], places)
    offsets = offsets_all[:tok_count]
    identity = (jnp.ones((R,), jnp.float32), jnp.zeros((R,), jnp.float32))
    whole_x = tokens.astype(jnp.float32)
    normed_f, norm_pull = jax.vjp(rms_norm, whole_x, gathered[10].astype(jnp.float32))
    normed = normed_f.astype(jnp.bfloat16)
    branch_pre = jnp.dot(normed, gathered[0], preferred_element_type=jnp.float32)
    branch, branch_pull = jax.vjp(jax.nn.gelu, branch_pre)
    inner_low = jnp.dot(normed, gathered[1], preferred_element_type=jnp.float32).astype(
        jnp.bfloat16
    )
    rim = shifted(inner_low[tok_count - (WIDTH - 1) :], "seq", 1)
    padded = jnp.concatenate([rim, inner_low], axis=0)
    tap_values = gathered[7].astype(jnp.float32)
    conv_sum = jnp.zeros((tok_count, R), jnp.float32) + gathered[8].astype(jnp.float32)
    for tap_index in range(WIDTH):
        usable = (offsets >= tap_index).astype(jnp.float32)[:, None]
        window = padded[WIDTH - 1 - tap_index : WIDTH - 1 - tap_index + tok_count]
        conv_sum = conv_sum + tap_values[tap_index] * usable * window
    conv_low = conv_sum.astype(jnp.bfloat16)
    conv_value = conv_low.astype(jnp.float32)
    conv_heads = conv_low.reshape(tok_count, HEADS, BLOCK)
    pre_rate = jnp.einsum(
        "thc,hcd->thd",
        conv_heads,
        gathered[3].reshape(HEADS, BLOCK, BLOCK),
        preferred_element_type=jnp.float32,
    ).reshape(tok_count, R) + gathered[5].astype(jnp.float32)
    pre_entry = jnp.einsum(
        "thc,hcd->thd",
        conv_heads,
        gathered[4].reshape(HEADS, BLOCK, BLOCK),
        preferred_element_type=jnp.float32,
    ).reshape(tok_count, R) + gathered[6].astype(jnp.float32)
    keeping = (offsets > 0).astype(jnp.float32)[:, None]
    (decays, sources), lru_pull = jax.vjp(
        partial(lru_terms, keeping),
        pre_rate,
        pre_entry,
        conv_value,
        gathered[9].astype(jnp.float32),
    )
    prefix, local_state = lax.associative_scan(combine, (decays, sources))
    carried = carried_in((prefix[-1], local_state[-1]), "seq", combine, identity, False)
    incoming = carried[1]
    states = local_state + prefix * incoming
    mixed_low = (branch * states).astype(jnp.bfloat16)
    middle = whole_x + jnp.dot(mixed_low, gathered[2], preferred_element_type=jnp.float32)
    normed_mid_f, mid_pull = jax.vjp(rms_norm, middle, gathered[11].astype(jnp.float32))
    normed_mid = normed_mid_f.astype(jnp.bfloat16)
    group_rows = lax.all_gather(normed_mid, "seq", axis=0, tiled=True)
    gate_pre = jnp.dot(group_rows, gate_weight, preferred_element_type=jnp.float32)
    up_pre = jnp.dot(group_rows, up_weight, preferred_element_type=jnp.float32)
    gelu_gate, gelu_pull = jax.vjp(jax.nn.gelu, gate_pre)
    hidden = (gelu_gate * up_pre).astype(jnp.bfloat16)
    down_part = lax.psum_scatter(
        jnp.dot(hidden, down_weight, preferred_element_type=jnp.float32).astype(jnp.bfloat16),
        "seq",
        scatter_dimension=0,
        tiled=True,
    ).astype(jnp.float32)
    result = (middle + down_part).astype(jnp.bfloat16)
    upstream = cotangent.astype(jnp.float32)
    group_cot = lax.all_gather(cotangent, "seq", axis=0, tiled=True)
    back_hidden = contract_cols(group_cot, down_weight)
    grad_down_part = contract_rows(hidden, group_cot)
    back_gate = gelu_pull(back_hidden * up_pre)[0].astype(jnp.bfloat16)
    back_up = (back_hidden * gelu_gate).astype(jnp.bfloat16)
    grad_gate_part = contract_rows(group_rows, back_gate)
    grad_up_part = contract_rows(group_rows, back_up)
    back_mid = lax.psum_scatter(
        (contract_cols(back_gate, gate_weight) + contract_cols(back_up, up_weight)).astype(
            jnp.bfloat16
        ),
        "seq",
        scatter_dimension=0,
        tiled=True,
    ).astype(jnp.float32)
    grad_gate, grad_up, grad_down = (
        lax.psum_scatter(
            grad_gate_part.astype(jnp.bfloat16), "dp", scatter_dimension=0, tiled=True
        ).astype(jnp.float32),
        lax.psum_scatter(
            grad_up_part.astype(jnp.bfloat16), "dp", scatter_dimension=0, tiled=True
        ).astype(jnp.float32),
        lax.psum_scatter(
            grad_down_part.astype(jnp.bfloat16), "dp", scatter_dimension=1, tiled=True
        ).astype(jnp.float32),
    )
    back_mid_norm, grad_mlp_gain_part = mid_pull(back_mid)
    back_middle = upstream + back_mid_norm
    back_out = back_middle.astype(jnp.bfloat16)
    reused = (
        lax.all_gather(sharded[0], ("dp", "seq"), axis=0, tiled=True),
        lax.all_gather(sharded[1], ("dp", "seq"), axis=0, tiled=True),
        lax.all_gather(sharded[2], ("dp", "seq"), axis=0, tiled=True),
        lax.all_gather(sharded[3], ("dp", "seq"), axis=0, tiled=True),
        lax.all_gather(sharded[4], ("dp", "seq"), axis=0, tiled=True),
        lax.all_gather(sharded[5], ("dp", "seq"), axis=0, tiled=True),
        lax.all_gather(sharded[6], ("dp", "seq"), axis=0, tiled=True),
        lax.all_gather(sharded[7], ("dp", "seq"), axis=1, tiled=True),
        lax.all_gather(sharded[8], ("dp", "seq"), axis=0, tiled=True),
        lax.all_gather(sharded[9], ("dp", "seq"), axis=0, tiled=True),
        lax.all_gather(sharded[10], ("dp", "seq"), axis=0, tiled=True),
        lax.all_gather(sharded[11], ("dp", "seq"), axis=0, tiled=True),
    )
    back_mixed = contract_cols(back_out, reused[2])
    grad_output_part = contract_rows(mixed_low, back_out)
    back_branch = branch_pull(back_mixed * states)[0].astype(jnp.bfloat16)
    back_states = back_mixed * branch
    following = jnp.concatenate([decays[1:], jnp.ones((1, R), jnp.float32)], axis=0)
    later_prod, local_adjoint = lax.associative_scan(
        combine, (following, back_states), reverse=True
    )
    returned = carried_in(
        (prefix[-1], decays[0] * local_adjoint[0]), "seq", combine, identity, True
    )
    adjoint = local_adjoint + later_prod * returned[1]
    previous = jnp.concatenate([incoming[None, :], states[:-1]], axis=0)
    back_rate, back_entry, back_conv_direct, grad_recur_part = lru_pull(
        (adjoint * previous, adjoint)
    )
    grad_rate_bias_part = jnp.sum(back_rate, axis=0)
    grad_entry_bias_part = jnp.sum(back_entry, axis=0)
    rate_heads = back_rate.astype(jnp.bfloat16).reshape(tok_count, HEADS, BLOCK)
    entry_heads = back_entry.astype(jnp.bfloat16).reshape(tok_count, HEADS, BLOCK)
    back_conv = (
        back_conv_direct
        + jnp.einsum(
            "thd,hcd->thc",
            rate_heads,
            reused[3].reshape(HEADS, BLOCK, BLOCK),
            preferred_element_type=jnp.float32,
        ).reshape(tok_count, R)
        + jnp.einsum(
            "thd,hcd->thc",
            entry_heads,
            reused[4].reshape(HEADS, BLOCK, BLOCK),
            preferred_element_type=jnp.float32,
        ).reshape(tok_count, R)
    )
    grad_rate_part = jnp.einsum(
        "thc,thd->hcd", conv_heads, rate_heads, preferred_element_type=jnp.float32
    ).reshape(R, BLOCK)
    grad_entry_part = jnp.einsum(
        "thc,thd->hcd", conv_heads, entry_heads, preferred_element_type=jnp.float32
    ).reshape(R, BLOCK)
    rim_next = shifted(back_conv[: WIDTH - 1], "seq", -1)
    extended = jnp.concatenate([back_conv, rim_next], axis=0)
    tap_back = reused[7].astype(jnp.float32)
    back_inner_f = jnp.zeros((tok_count, R), jnp.float32)
    tap_grads = []
    for tap_index in range(WIDTH):
        usable_ext = (offsets_all >= tap_index).astype(jnp.float32)[:, None]
        masked = extended * usable_ext
        back_inner_f = (
            back_inner_f + tap_back[tap_index] * masked[tap_index : tap_index + tok_count]
        )
        window = padded[WIDTH - 1 - tap_index : WIDTH - 1 - tap_index + tok_count]
        tap_grads.append(jnp.sum(masked[:tok_count] * window, axis=0))
    grad_conv_part = jnp.stack(tap_grads, axis=0)
    grad_conv_bias_part = jnp.sum(back_conv, axis=0)
    back_inner = back_inner_f.astype(jnp.bfloat16)
    grad_inner_part = contract_rows(normed, back_inner)
    grad_branch_part = contract_rows(normed, back_branch)
    back_normed = contract_cols(back_inner, reused[1]) + contract_cols(back_branch, reused[0])
    back_x_norm, grad_norm_gain_part = norm_pull(back_normed)
    grad_tokens = back_middle + back_x_norm
    recur_grads = (
        lax.psum_scatter(grad_branch_part, ("dp", "seq"), scatter_dimension=0, tiled=True),
        lax.psum_scatter(grad_inner_part, ("dp", "seq"), scatter_dimension=0, tiled=True),
        lax.psum_scatter(grad_output_part, ("dp", "seq"), scatter_dimension=0, tiled=True),
        lax.psum_scatter(grad_rate_part, ("dp", "seq"), scatter_dimension=0, tiled=True),
        lax.psum_scatter(grad_entry_part, ("dp", "seq"), scatter_dimension=0, tiled=True),
        lax.psum_scatter(grad_rate_bias_part, ("dp", "seq"), scatter_dimension=0, tiled=True),
        lax.psum_scatter(grad_entry_bias_part, ("dp", "seq"), scatter_dimension=0, tiled=True),
        lax.psum_scatter(grad_conv_part, ("dp", "seq"), scatter_dimension=1, tiled=True),
        lax.psum_scatter(grad_conv_bias_part, ("dp", "seq"), scatter_dimension=0, tiled=True),
        lax.psum_scatter(grad_recur_part, ("dp", "seq"), scatter_dimension=0, tiled=True),
        lax.psum_scatter(grad_norm_gain_part, ("dp", "seq"), scatter_dimension=0, tiled=True),
        lax.psum_scatter(grad_mlp_gain_part, ("dp", "seq"), scatter_dimension=0, tiled=True),
    )
    return (
        result,
        grad_tokens,
        recur_grads[0],
        recur_grads[1],
        recur_grads[2],
        recur_grads[3],
        recur_grads[4],
        recur_grads[5],
        recur_grads[6],
        recur_grads[7],
        recur_grads[8],
        recur_grads[9],
        recur_grads[10],
        recur_grads[11],
        grad_gate,
        grad_up,
        grad_down,
    )


def solution(mesh):
    in_specs = (
        P(("dp", "seq"), None),
        P("dp", None),
        P(("dp", "seq"), None),
        P(("dp", "seq"), None),
        P(("dp", "seq"), None),
        P(("dp", "seq"), None),
        P(("dp", "seq"), None),
        P(("dp", "seq")),
        P(("dp", "seq")),
        P(None, ("dp", "seq")),
        P(("dp", "seq")),
        P(("dp", "seq")),
        P(("dp", "seq")),
        P(("dp", "seq")),
        P(None, "seq"),
        P(None, "seq"),
        P("seq", None),
        P(("dp", "seq"), None),
    )
    out_specs = (
        P(("dp", "seq"), None),
        P(("dp", "seq"), None),
        P(("dp", "seq"), None),
        P(("dp", "seq"), None),
        P(("dp", "seq"), None),
        P(("dp", "seq"), None),
        P(("dp", "seq"), None),
        P(("dp", "seq")),
        P(("dp", "seq")),
        P(None, ("dp", "seq")),
        P(("dp", "seq")),
        P(("dp", "seq")),
        P(("dp", "seq")),
        P(("dp", "seq")),
        P("dp", "seq"),
        P("dp", "seq"),
        P("seq", "dp"),
    )
    return jax.shard_map(shards, mesh=mesh, in_specs=in_specs, out_specs=out_specs, check_vma=False)
```

profile of v0, /device:TPU:19, one launch (start us, length us, event | category | flops | bytes accessed | tf_op | source)
XLA Modules:
  0.0 2449.9 jit_solution(2773360564935314899)
XLA Ops:
  15.7 40.6 %all-reduce.79 = (bf16[2560]{0:T(1024)(128)(2,1)S(1)}, bf16[2048]{0:T(1024)(128)(2,1)S(1)}, bf16[2560]{0:T(1024)(128)(2,1)S(1)}, bf16[2560]{0:T(1024)(128)(2,1)S...) all-reduce(bf16[2560]{0:T(1024)(128)(2,1)S(1)} %dynamic-update-slic, ...), channel_id=1, replica_groups=mesh['dp'=8,'seq'=4] {'dp','seq'}, use_global_device_ids=true, to_apply=%add.69 | all-reduce | flops 14336 | bytes 57344
  60.1 31.8 %all-gather = bf16[32,80,4]{1,2,0:T(4,128)(2,1)S(1)} all-gather(bf16[1,80,4]{1,2,0:T(4,128)(2,1)} %bitcast.112), channel_id=1, replica_groups=mesh['dp'=8,'seq'=4] {'dp','seq'}, dimensions={0}, use_global_device_ids=true | all-gather | bytes 21120 | tf_op jit(solution)/shard_map/all_gather | solution.py:117
  112.1 41.9 %all-gather.16.cloned.1.call-done = bf16[2560,256]{1,0:T(8,128)(2,1)} async-done(((bf16[80,256]{1,0:T(8,128)(2,1)}), bf16[2560,256]{1,0:T(8,128)(2,1)}) %all-gather.16.cloned.1.call-update) | async-done | bytes 1310736 | tf_op jit(solution)/shard_map/all_gather | solution.py:113
  159.5 50.6 %all-gather.18.cloned.1.call-done = bf16[2560,256]{1,0:T(8,128)(2,1)} async-done(((bf16[80,256]{1,0:T(8,128)(2,1)}), bf16[2560,256]{1,0:T(8,128)(2,1)}) %all-gather.18.cloned.1.call-update) | async-done | bytes 1310736 | tf_op jit(solution)/shard_map/all_gather | solution.py:114
  407.9 12.1 multiply_convert_fusion.2
  429.5 33.4 %all-gather.22.cloned.1.call-done = bf16[1024,2048]{1,0:T(8,128)(2,1)} async-done(((bf16[256,2048]{1,0:T(8,128)(2,1)}), bf16[1024,2048]{1,0:T(8,128)(2,1)}) %all-gather.22.cloned.1.call-update) | async-done | bytes 4194320 | tf_op jit(solution)/shard_map/all_gather | solution.py:176
  462.9 12.9 fusion.111
  486.2 12.8 all-gather.24.cloned.1.call-done
  499.0 18.0 multiply_convert_fusion
  528.0 11.3 add_convert_fusion
  606.7 24.2 reduce-scatter.14.cloned.1.call-done
  895.0 13.2 rev.9
  908.1 21.2 rev.8
  975.5 11.7 convolution_convert_fusion.2
  987.3 11.6 convolution_convert_fusion.1
  1071.1 42.7 %all-reduce.78 = (f32[2560]{0:T(1024)S(1)}, f32[2560]{0:T(1024)S(1)}, f32[2560]{0:T(1024)S(1)}, f32[2560]{0:T(1024)S(1)}, f32[2048]{0:T(1024)S(1)}, /*index=5*/f32[2048]{0:T(1024)S(1)}) all-reduce(f32[2560]{0:T(1024)S(1)} %get-tuple-element.148, ...), channel_id=9, replica_groups=mesh['dp'=8,'seq'=4] {'dp','seq'}, use_global_device_ids=true, to_apply=%region_18.19.clone | all-reduce | flops 14336 | bytes 114688
  1122.3 109.4 %reduce-scatter.28.cloned.1.call-done = bf16[256,1536]{1,0:T(8,128)(2,1)} async-done(((bf16[2048,1536]{1,0:T(8,128)(2,1)}), bf16[256,1536]{1,0:T(8,128)(2,1)}) %reduce-scatter.28.cloned.1.call-update) | async-done | bytes 786448 | tf_op jit(solution)/shard_map/reduce_scatter | solution.py:205
  1234.1 118.5 %reduce-scatter.30.cloned.1.call-done = bf16[256,1536]{1,0:T(8,128)(2,1)} async-done(((bf16[2048,1536]{1,0:T(8,128)(2,1)}), bf16[256,1536]{1,0:T(8,128)(2,1)}) %reduce-scatter.30.cloned.1.call-update) | async-done | bytes 786448 | tf_op jit(solution)/shard_map/reduce_scatter | solution.py:208
  1355.1 119.1 %reduce-scatter.32.cloned.1.call-done = bf16[1536,256]{1,0:T(8,128)(2,1)} async-done(((bf16[1536,2048]{1,0:T(8,128)(2,1)}), bf16[1536,256]{1,0:T(8,128)(2,1)}) %reduce-scatter.32.cloned.1.call-update) | async-done | bytes 786448 | tf_op jit(solution)/shard_map/reduce_scatter | solution.py:211
  1476.6 107.6 %reduce-scatter.24.cloned.1.call-done = f32[80,256]{1,0:T(8,128)} async-done(((f32[2560,256]{1,0:T(8,128)}), f32[80,256]{1,0:T(8,128)}) %reduce-scatter.24.cloned.1.call-update) | async-done | bytes 81936 | tf_op jit(solution)/shard_map/reduce_scatter | solution.py:298
  1584.2 136.8 %reduce-scatter.26.cloned.1.call-done = f32[80,256]{1,0:T(8,128)} async-done(((f32[2560,256]{1,0:T(8,128)}), f32[80,256]{1,0:T(8,128)}) %reduce-scatter.26.cloned.1.call-update) | async-done | bytes 81936 | tf_op jit(solution)/shard_map/reduce_scatter | solution.py:299
  1721.0 257.0 %reduce-scatter.22.cloned.1.call-done = f32[80,2048]{1,0:T(8,128)} async-done(((f32[2560,2048]{1,0:T(8,128)}), f32[80,2048]{1,0:T(8,128)}) %reduce-scatter.22.cloned.1.call-update) | async-done | bytes 655376 | tf_op jit(solution)/shard_map/reduce_scatter | solution.py:297
  1977.9 232.5 %reduce-scatter.18.cloned.1.call-done = f32[64,2560]{1,0:T(8,128)} async-done(((f32[2048,2560]{1,0:T(8,128)}), f32[64,2560]{1,0:T(8,128)}) %reduce-scatter.18.cloned.1.call-update) | async-done | bytes 655376 | tf_op jit(solution)/shard_map/reduce_scatter | solution.py:295
  2210.4 232.5 %reduce-scatter.20.cloned.1.call-done = f32[64,2560]{1,0:T(8,128)} async-done(((f32[2048,2560]{1,0:T(8,128)}), f32[64,2560]{1,0:T(8,128)}) %reduce-scatter.20.cloned.1.call-update) | async-done | bytes 655376 | tf_op jit(solution)/shard_map/reduce_scatter | solution.py:296
  (661 shorter events, 730.6 us)
Async XLA Ops:
  7.2 91.5 %all-gather.14.cloned.1.call-start = ((), (), s32[]{:S(2)}) async-start(), calls=%async_computation.12 | async-start | bytes 10813440 | tf_op jit(solution)/shard_map/all_gather | solution.py:111
  7.9 146.1 %all-gather.16.cloned.1.call-start = ((), (), s32[]{:S(2)}) async-start(), calls=%async_computation.13 | async-start | bytes 1351680 | tf_op jit(solution)/shard_map/all_gather | solution.py:113
  8.7 201.4 %all-gather.18.cloned.1.call-start = ((), (), s32[]{:S(2)}) async-start(), calls=%async_computation.14 | async-start | bytes 1351680 | tf_op jit(solution)/shard_map/all_gather | solution.py:114
  9.4 398.4 %all-gather.12.cloned.1.call-start = ((), (), s32[]{:S(2)}) async-start(), calls=%async_computation.11 | async-start | bytes 10813440 | tf_op jit(solution)/shard_map/all_gather | solution.py:110
  10.0 410.0 %all-gather.20.cloned.1.call-start = ((), (), s32[]{:S(2)}) async-start(), calls=%async_computation.15 | async-start | bytes 10813440 | tf_op jit(solution)/shard_map/all_gather | solution.py:112
  10.6 452.3 %all-gather.22.cloned.1.call-start = ((), (), s32[]{:S(2)}) async-start(), calls=%async_computation.16 | async-start | bytes 5242880 | tf_op jit(solution)/shard_map/all_gather | solution.py:176
  56.3 351.5 %copy-start.54 = (f32[2048]{0:T(1024)}, f32[2048]{0:T(1024)S(1)}, u32[]{:S(2)}) copy-start(f32[2048]{0:T(1024)S(1)} %convert_element_type.163) | copy-start | bytes 24580
  57.9 350.0 %copy-start.81 = (f32[256]{0:T(256)}, f32[256]{0:T(256)S(1)}, u32[]{:S(2)}) copy-start(f32[256]{0:T(256)S(1)} %fusion.84) | copy-start | bytes 3076
  60.1 157.1 %copy-start.118 = (f32[256]{0:T(256)}, f32[256]{0:T(256)S(1)}, u32[]{:S(2)}) copy-start(f32[256]{0:T(256)S(1)} %get-tuple-element.297) | copy-start | bytes 3076
  92.6 124.7 %copy-start.64 = (f32[2560]{0:T(1024)}, f32[2560]{0:T(1024)S(1)}, u32[]{:S(2)}) copy-start(f32[2560]{0:T(1024)S(1)} %get-tuple-element.290) | copy-start | bytes 30724
  106.0 3.1 collective-permute-start
  428.7 70.2 %all-gather.24.cloned.1.call-start = ((), (), s32[]{:S(2)}) async-start(), calls=%async_computation.18 | async-start | bytes 5242880 | tf_op jit(solution)/shard_map/all_gather | solution.py:189
  429.5 174.0 %reduce-scatter.16.cloned.1.call-start = ((), (), s32[]{:S(2)}) async-start(), calls=%async_computation.19 | async-start | bytes 5242880 | tf_op jit(solution)/shard_map/reduce_scatter | solution.py:196
  539.4 91.5 %reduce-scatter.14.cloned.1.call-start = ((), (), s32[]{:S(2)}) async-start(), calls=%async_computation.17 | async-start | bytes 5242880 | tf_op jit(solution)/shard_map/reduce_scatter | solution.py:181
  550.5 570.3 %reduce-scatter.34.cloned.1.call-start = ((), (), s32[]{:S(2)}) async-start(), calls=%async_computation.28 | async-start | bytes 1351680
  966.0 3.8 collective-permute-start.1
  975.5 256.2 %reduce-scatter.28.cloned.1.call-start = ((), (), s32[]{:S(2)}) async-start(), calls=%async_computation.25 | async-start | bytes 7077888 | tf_op jit(solution)/shard_map/reduce_scatter | solution.py:205
  987.2 365.4 %reduce-scatter.30.cloned.1.call-start = ((), (), s32[]{:S(2)}) async-start(), calls=%async_computation.26 | async-start | bytes 7077888 | tf_op jit(solution)/shard_map/reduce_scatter | solution.py:208
  998.9 475.4 %reduce-scatter.32.cloned.1.call-start = ((), (), s32[]{:S(2)}) async-start(), calls=%async_computation.27 | async-start | bytes 7077888 | tf_op jit(solution)/shard_map/reduce_scatter | solution.py:211
  1010.2 574.0 %reduce-scatter.24.cloned.1.call-start = ((), (), s32[]{:S(2)}) async-start(), calls=%async_computation.23 | async-start | bytes 2703360 | tf_op jit(solution)/shard_map/reduce_scatter | solution.py:298
  1013.9 707.0 %reduce-scatter.26.cloned.1.call-start = ((), (), s32[]{:S(2)}) async-start(), calls=%async_computation.24 | async-start | bytes 2703360 | tf_op jit(solution)/shard_map/reduce_scatter | solution.py:299
  1017.3 960.7 %reduce-scatter.22.cloned.1.call-start = ((), (), s32[]{:S(2)}) async-start(), calls=%async_computation.22 | async-start | bytes 21626880 | tf_op jit(solution)/shard_map/reduce_scatter | solution.py:297
  1029.1 1181.3 %reduce-scatter.18.cloned.1.call-start = ((), (), s32[]{:S(2)}) async-start(), calls=%async_computation.20 | async-start | bytes 21626880 | tf_op jit(solution)/shard_map/reduce_scatter | solution.py:295
  1039.5 1403.3 %reduce-scatter.20.cloned.1.call-start = ((), (), s32[]{:S(2)}) async-start(), calls=%async_computation.21 | async-start | bytes 21626880 | tf_op jit(solution)/shard_map/reduce_scatter | solution.py:296
  (122 other events, 1363.2 us)
Sparse Core Ops, SparseCore 0:
  10.9 87.7 all-gather.13
  101.5 52.3 all-gather.15
  156.8 53.2 all-gather.17
  212.8 86.3 all-gather.11
  301.9 85.2 all-gather.19
  428.9 33.9 all-gather.21
  464.4 34.4 all-gather.23
  539.5 44.1 reduce-scatter.15
  586.3 44.5 reduce-scatter.13
  975.6 108.4 reduce-scatter.33
  1088.1 143.5 reduce-scatter.27
  1235.5 117.0 reduce-scatter.29
  1356.7 117.5 reduce-scatter.31
  1477.0 107.1 reduce-scatter.23
  1587.0 133.9 reduce-scatter.25
  1723.8 254.0 reduce-scatter.21
  1980.8 229.5 reduce-scatter.17
  2213.2 229.5 reduce-scatter.19
where the time goes:
time: 2470 us; the launch traced here: 2450 us
  waiting for transfers between devices  1490 us (60%)
  local copies, waits for them, and re-layouts  458 us (19%)
  matrix products  207 us (8%)
  other arithmetic  144 us (6%)
  blocking collectives  131 us (5%)
    reduce_scatter x1, waiting for transfers between devices, shards(): lax.psum_scatter(grad_output_part, ('dp', 'seq'), scatter_dimension=0, ti...  257 us
    reduce_scatter x1, waiting for transfers between devices, shards(): lax.psum_scatter(grad_inner_part, ('dp', 'seq'), scatter_dimension=0, til...  232 us
    reduce_scatter x1, waiting for transfers between devices, shards(): lax.psum_scatter(grad_branch_part, ('dp', 'seq'), scatter_dimension=0, ti...  232 us
    slice x57, local copies, waits for them, and re-layouts, shards(): lax.associative_scan(combine, (following, back_states), reverse=True)  167 us
    reduce_scatter x1, waiting for transfers between devices, shards(): lax.psum_scatter(grad_entry_part, ('dp', 'seq'), scatter_dimension=0, til...  137 us
    reduce_scatter x1, waiting for transfers between devices, shards(): lax.psum_scatter(grad_down_part.astype(jnp.bfloat16), 'dp', scatter_dimen...  119 us
    reduce_scatter x1, waiting for transfers between devices, shards(): lax.psum_scatter(grad_up_part.astype(jnp.bfloat16), 'dp', scatter_dimensi...  119 us
    reduce_scatter x1, waiting for transfers between devices, shards(): lax.psum_scatter(grad_gate_part.astype(jnp.bfloat16), 'dp', scatter_dimen...  109 us
  transfers between devices with their start and end apart: 20, of which 16 were waited for; matrix products, arithmetic and copies ran while one was open for 17% of the time, Pallas kernels for 0%

commit v1 on v0

v1 whole, which is shorter than its diff:
```python
from functools import partial

import jax
import jax.numpy as jnp
from jax import lax
from jax.experimental import pallas as pl
from jax.experimental.pallas import tpu as pltpu
from jax.sharding import PartitionSpec as P

BLOCK = 256
WIDTH = 4
EPSILON = 1e-06
LANES = 128
VMEM_BYTES = 56 * 1024 * 1024
ENTRY_TILE = 256
MLP_TILE = 256
GRAD_TILE = 512
EXIT_TILE = 256
BOTH = ("dp", "seq")
F32 = jnp.float32
BF16 = jnp.bfloat16


def dot(left, right):
    return jnp.dot(left, right, preferred_element_type=F32)


def contract_rows(left, right):
    return lax.dot_general(left, right, (((0,), (0,)), ((), ())), preferred_element_type=F32)


def contract_cols(left, right):
    return lax.dot_general(left, right, (((1,), (1,)), ((), ())), preferred_element_type=F32)


class Place:
    def __init__(self):
        self.n_dp = lax.axis_size("dp")
        self.n_seq = lax.axis_size("seq")
        self.n_q = self.n_dp // 2
        self.n_x = self.n_seq // 2
        self.dp = lax.axis_index("dp")
        self.seq = lax.axis_index("seq")
        self.p = self.dp % 2
        self.q = self.dp // 2
        self.c = self.seq % 2
        self.x = self.seq // 2

    def swap_core(self, a):
        return lax.ppermute(a, "seq", [(i, i ^ 1) for i in range(self.n_seq)])

    def swap_pair(self, a):
        return lax.ppermute(a, "dp", [(i, i ^ 1) for i in range(self.n_dp)])

    def step_x(self, a, places, way):
        return lax.ppermute(
            a, "seq", [(2 * i + c, 2 * (i + way) + c) for i in places for c in range(2)]
        )

    def step_q(self, a, places, way):
        return lax.ppermute(
            a, "dp", [(2 * i + p, 2 * (i + way) + p) for i in places for p in range(2)]
        )


def add_low(*terms):
    total = terms[0].astype(F32)
    for term in terms[1:]:
        total = total + term.astype(F32)
    return total


def line_sum(block_of, count, here, step):
    if count == 1:
        return block_of(here).astype(F32)
    if count == 2:
        got = step(block_of(1 - here), [0, 1], None)
        return add_low(block_of(here), got)
    up = down = None
    for k in range(1, count):
        send_up = block_of(jnp.minimum(count - k + here, count - 1))
        if up is not None:
            send_up = add_low(send_up, up).astype(BF16)
        up = step(send_up, range(0, min(k, count - 1)), 1)
        send_down = block_of(jnp.maximum(k + here - count, 0))
        if down is not None:
            send_down = add_low(send_down, down).astype(BF16)
        down = step(send_down, range(max(count - k, 1), count), -1)
    return add_low(block_of(here), up, down)


def line_gather(block, count, here, step):
    if count == 1:
        return block[None]
    if count == 2:
        got = step(block, [0, 1], None)
        return jnp.where(here == 0, jnp.stack([block, got]), jnp.stack([got, block]))
    rows = jnp.zeros((count,) + block.shape, block.dtype)
    rows = lax.dynamic_update_index_in_dim(rows, block, here, 0)
    up = down = block
    for k in range(1, count):
        up = step(up, range(k - 1, count - 1), 1)
        down = step(down, range(1, count - k + 1), -1)
        from_up = lax.dynamic_update_index_in_dim(rows, up, jnp.maximum(here - k, 0), 0)
        rows = jnp.where(here - k >= 0, from_up, rows)
        from_down = lax.dynamic_update_index_in_dim(rows, down, jnp.minimum(here + k, count - 1), 0)
        rows = jnp.where(here + k < count, from_down, rows)
    return rows


def x_step(place):
    def step(a, places, way):
        if way is None:
            return lax.ppermute(a, "seq", [(i, i ^ 2) for i in range(place.n_seq)])
        return place.step_x(a, places, way)

    return step


def q_step(place):
    def step(a, places, way):
        if way is None:
            return lax.ppermute(a, "dp", [(i, i ^ 2) for i in range(place.n_dp)])
        return place.step_q(a, places, way)

    return step


def gather_seq(place, block):
    rows = line_gather(block, place.n_x, place.x, x_step(place))
    other = place.swap_core(rows)
    first = jnp.where(place.c == 0, rows, other)
    second = jnp.where(place.c == 0, other, rows)
    return jnp.stack([first, second], axis=1).reshape((place.n_seq,) + block.shape)


def scatter_seq(place, whole):
    view = whole.reshape((place.n_x, 2) + whole.shape[1:])
    mine = lax.dynamic_index_in_dim(view, place.c, 1, False)
    theirs = lax.dynamic_index_in_dim(view, 1 - place.c, 1, False)
    chip = add_low(mine, place.swap_core(theirs)).astype(BF16)
    return line_sum(
        lambda i: lax.dynamic_index_in_dim(chip, i, 0, False), place.n_x, place.x, x_step(place)
    )


def gather_plane(place, block):
    if place.n_x != 2:
        both = jnp.where(
            place.p == 0,
            jnp.stack([block, place.swap_pair(block)]),
            jnp.stack([place.swap_pair(block), block]),
        )
        rows = gather_seq(place, both)
        return jnp.swapaxes(rows, 0, 1)
    half = block.shape[0] // 2
    step = x_step(place)
    by_x = step(block, [0, 1], None)
    by_y = place.swap_pair(block)
    corner_low = step(by_y[:half], [0, 1], None)
    corner_high = place.swap_pair(by_x[half:])
    corner = jnp.concatenate([corner_low, corner_high], axis=0)
    mine = jnp.where(place.x == 0, jnp.stack([block, by_x]), jnp.stack([by_x, block]))
    away = jnp.where(place.x == 0, jnp.stack([by_y, corner]), jnp.stack([corner, by_y]))
    rows = jnp.where(place.p == 0, jnp.stack([mine, away]), jnp.stack([away, mine]))
    other = place.swap_core(rows)
    first = jnp.where(place.c == 0, rows, other)
    second = jnp.where(place.c == 0, other, rows)
    return jnp.stack([first, second], axis=2).reshape((2, place.n_seq) + block.shape)


def scatter_plane(place, whole):
    view = whole.reshape((2, place.n_x, 2) + whole.shape[2:])
    mine = lax.dynamic_index_in_dim(view, place.c, 2, False)
    theirs = lax.dynamic_index_in_dim(view, 1 - place.c, 2, False)
    chip = add_low(mine, place.swap_core(theirs)).astype(BF16)
    if place.n_x != 2:
        near = lax.dynamic_index_in_dim(chip, place.p, 0, False)
        far = lax.dynamic_index_in_dim(chip, 1 - place.p, 0, False)
        pair = add_low(near, place.swap_pair(far)).astype(BF16)
        return line_sum(
            lambda i: lax.dynamic_index_in_dim(pair, i, 0, False), place.n_x, place.x, x_step(place)
        )
    half = whole.shape[2] // 2
    step = x_step(place)

    def part(p, x):
        return lax.dynamic_index_in_dim(lax.dynamic_index_in_dim(chip, p, 0, False), x, 0, False)

    corner = part(1 - place.p, 1 - place.x)
    low = step(corner[:half], [0, 1], None)
    high = place.swap_pair(corner[half:])
    to_y = part(1 - place.p, place.x)
    to_x = part(place.p, 1 - place.x)
    to_y = jnp.concatenate([add_low(to_y[:half], low).astype(BF16), to_y[half:]], axis=0)
    to_x = jnp.concatenate([to_x[:half], add_low(to_x[half:], high).astype(BF16)], axis=0)
    got_y = place.swap_pair(to_y)
    got_x = step(to_x, [0, 1], None)
    return add_low(part(place.p, place.x), got_x, got_y)


def sum_dp(place, whole):
    view = whole.reshape((place.n_q, 2) + whole.shape[1:])
    mine = lax.dynamic_index_in_dim(view, place.p, 1, False)
    theirs = lax.dynamic_index_in_dim(view, 1 - place.p, 1, False)
    pair = add_low(mine, place.swap_pair(theirs)).astype(BF16)
    return line_sum(
        lambda i: lax.dynamic_index_in_dim(pair, i, 0, False), place.n_q, place.q, q_step(place)
    )


def split_pair(place, total, axis):
    half = total.shape[axis] // 2
    mine = lax.dynamic_slice_in_dim(total, place.p * half, half, axis)
    theirs = lax.dynamic_slice_in_dim(total, (1 - place.p) * half, half, axis).astype(BF16)
    got = place.swap_pair(theirs).astype(F32)
    pair = [jnp.concatenate(two, axis=1 - axis) for two in ([mine, got], [got, mine])]
    return jnp.where(place.p == 0, *pair)


def turned(place, a, back):
    route = [(s * place.n_dp + j, j * place.n_seq + s) for s in range(place.n_seq) for j in range(place.n_dp)]
    if back:
        route = [(there, here) for here, there in route]
    return lax.ppermute(a, BOTH, route)


def window(place, a, axis, own, spread):
    start = own * place.seq % BLOCK
    if own % BLOCK == 0:
        return a
    if 2 * own % BLOCK == 0 and spread == own + BLOCK // 2:
        edge = BLOCK // 2
        last = lax.slice_in_dim(a, own - edge, own, axis=axis)
        first = lax.slice_in_dim(a, 0, edge, axis=axis)
        got = place.swap_core(jnp.where(place.c == 0, last, first))
        return jnp.where(
            place.c == 0,
            jnp.concatenate([a, got], axis=axis),
            jnp.concatenate([got, a], axis=axis),
        )
    whole = lax.all_gather(a, "seq", axis=axis, tiled=True)
    begin = jnp.minimum(own * place.seq - start, whole.shape[axis] - spread)
    return lax.dynamic_slice_in_dim(whole, begin, spread, axis=axis)


def row_offsets(lengths, places):
    row_ends = jnp.cumsum(lengths)
    starts = row_ends - lengths
    row_begin = jnp.max(jnp.where(starts[None, :] <= places[:, None], starts[None, :], 0), axis=1)
    return places - row_begin


def shift_rows(a, distance, fill):
    count = a.shape[0]
    if distance > 0:
        return jnp.concatenate([jnp.full((distance, a.shape[1]), fill, a.dtype), a[: count - distance]], 0)
    return jnp.concatenate([a[-distance:], jnp.full((-distance, a.shape[1]), fill, a.dtype)], 0)


def scan_rows(decay, source, way):
    distance = 1
    while distance < decay.shape[0]:
        source = source + decay * shift_rows(source, way * distance, 0.0)
        decay = decay * shift_rows(decay, way * distance, 1.0)
        distance *= 2
    return decay, source


def gelu_parts(v):
    root = 0.7978845608028654
    cubic = 0.044715
    inner = root * (v + cubic * v * v * v)
    tanh = jnp.tanh(inner)
    value = 0.5 * v * (1.0 + tanh)
    slope = 0.5 * (1.0 + tanh) + 0.5 * v * (1.0 - tanh * tanh) * root * (1.0 + 3.0 * cubic * v * v)
    return value, slope


def softplus_row(recur):
    return jnp.maximum(-recur, 0.0) + jnp.log1p(jnp.exp(-jnp.abs(recur)))


def lru_parts(pre_rate, pre_entry, soft):
    rate = jax.nn.sigmoid(pre_rate)
    entry = jax.nn.sigmoid(pre_entry)
    power = 8.0 * soft * rate
    decay = jnp.exp(-power)
    twice = 2.0 * power
    series = twice * (
        1.0 - twice * (0.5 - twice * (1.0 / 6.0 - twice * (1.0 / 24.0 - twice * (1.0 / 120.0))))
    )
    square = jnp.where(twice < 0.25, series, 1.0 - decay * decay)
    return rate, entry, decay, square


STEP_ROWS = 64
TILE = 8


def row_steps(count):
    return count // STEP_ROWS


def step_rows(i):
    return pl.ds(pl.multiple_of(i * STEP_ROWS, STEP_ROWS), STEP_ROWS)


def tile_before(i):
    return pl.ds(pl.multiple_of(jnp.maximum(i * STEP_ROWS - TILE, 0), TILE), TILE)


def tile_after(i, count):
    return pl.ds(pl.multiple_of(jnp.minimum((i + 1) * STEP_ROWS, count - TILE), TILE), TILE)


def tile_sum(a):
    return jnp.sum(a.reshape(-1, TILE, a.shape[1]), axis=0)


def conv_kernel(inner_ref, taps_ref, offset_ref, conv_ref):
    taps = taps_ref[...]

    def step(i, carry):
        r = step_rows(i)
        near = jnp.concatenate([inner_ref[tile_before(i), :], inner_ref[r, :]], axis=0).astype(F32)
        offset = offset_ref[r, :]
        total = taps[WIDTH : WIDTH + 1, :] + taps[0:1, :] * near[TILE:]
        for k in range(1, WIDTH):
            total = total + taps[k : k + 1, :] * jnp.where(offset >= k, near[TILE - k : TILE - k + STEP_ROWS], 0.0)
        conv_ref[r, :] = total.astype(BF16)
        return carry

    lax.fori_loop(0, row_steps(inner_ref.shape[0]), step, 0, unroll=4)


def forward_kernel(rate_ref, entry_ref, conv_ref, branch_ref, vec_ref, offset_ref, states_ref, mixed_ref):
    vec = vec_ref[...]
    soft = softplus_row(vec[2:3, :])

    def step(i, carry):
        r = step_rows(i)
        _, entry, decay, square = lru_parts(rate_ref[r, :] + vec[0:1, :], entry_ref[r, :] + vec[1:2, :], soft)
        source = jnp.sqrt(square) * entry * conv_ref[r, :].astype(F32)
        decay = jnp.where(offset_ref[r, :] > 0, decay, 0.0)
        product, local = scan_rows(decay, source, 1)
        states = local + product * carry
        states_ref[r, :] = states
        mixed_ref[r, :] = (gelu_parts(branch_ref[r, :])[0] * states).astype(BF16)
        return states[STEP_ROWS - 1 :, :]

    lax.fori_loop(0, row_steps(states_ref.shape[0]), step, jnp.zeros_like(soft), unroll=4)


def backward_kernel(
    rate_ref, entry_ref, conv_ref, branch_ref, vec_ref, offset_ref, states_ref, back_ref,
    back_branch_ref, back_gates_ref, direct_ref, sums_ref,
):
    vec = vec_ref[...]
    recur = vec[2:3, :]
    soft = softplus_row(recur)
    steps = row_steps(states_ref.shape[0])

    def step(n, carry):
        later, later_decay, rate_sum, entry_sum, recur_sum = carry
        i = steps - 1 - n
        r = step_rows(i)
        rate, entry, decay, square = lru_parts(rate_ref[r, :] + vec[0:1, :], entry_ref[r, :] + vec[1:2, :], soft)
        conv = conv_ref[r, :].astype(F32)
        states = states_ref[r, :]
        back_mixed = back_ref[r, :]
        value, slope = gelu_parts(branch_ref[r, :])
        back_branch_ref[r, :] = (back_mixed * states * slope).astype(BF16)
        keep = offset_ref[r, :] > 0
        kept_decay = jnp.where(keep, decay, 0.0)
        following = jnp.concatenate([kept_decay[1:], later_decay], axis=0)
        product, local = scan_rows(following, back_mixed * value, -1)
        adjoint = local + product * later
        inverse = lax.rsqrt(square)
        root = square * inverse
        pulled = adjoint * entry * conv
        previous = jnp.concatenate([states_ref[tile_before(i), :][TILE - 1 :], states[: STEP_ROWS - 1]], axis=0)
        back_decay = adjoint * jnp.where(keep, previous, 0.0) - pulled * decay * inverse
        back_power = back_decay * decay * rate
        back_rate = back_power * (-8.0 * soft) * (1.0 - rate)
        back_entry = pulled * root * (1.0 - entry)
        back_gates_ref[0, r, :] = back_rate.astype(BF16)
        back_gates_ref[1, r, :] = back_entry.astype(BF16)
        direct_ref[r, :] = adjoint * root * entry
        return (
            adjoint[:1], kept_decay[:1], rate_sum + tile_sum(back_rate), entry_sum + tile_sum(back_entry),
            recur_sum + tile_sum(back_power),
        )

    row, tile = jnp.zeros_like(recur), jnp.zeros((TILE, recur.shape[1]), F32)
    _, _, rate_sum, entry_sum, recur_sum = lax.fori_loop(0, steps, step, (row, row, tile, tile, tile), unroll=4)
    total = lambda a: jnp.sum(a, axis=0, keepdims=True)
    sums_ref[...] = jnp.concatenate(
        [
            total(rate_sum),
            total(entry_sum),
            total(recur_sum) * (8.0 * jax.nn.sigmoid(-recur)),
            jnp.zeros((TILE - 3,) + recur.shape[1:], F32),
        ],
        axis=0,
    )


def conv_back_kernel(direct_ref, gates_ref, inner_ref, taps_ref, offset_ref, back_ref, sums_ref):
    count = direct_ref.shape[0]
    taps = taps_ref[...]
    steps = row_steps(count)

    def step(i, sums):
        r, before, after = step_rows(i), tile_before(i), tile_after(i, count)
        last = jnp.where(i + 1 < steps, 1.0, 0.0)
        here = direct_ref[r, :] + gates_ref[r, :]
        wide = jnp.concatenate([here, (direct_ref[after, :] + gates_ref[after, :]) * last], axis=0)
        offset = jnp.concatenate([offset_ref[r, :], offset_ref[after, :]], axis=0)
        inner = jnp.concatenate([inner_ref[before, :], inner_ref[r, :]], axis=0).astype(F32)
        total = taps[0:1, :] * here
        new = [sums[0] + tile_sum(here * inner[TILE:])]
        for k in range(1, WIDTH):
            masked = jnp.where(offset >= k, wide, 0.0)
            total = total + taps[k : k + 1, :] * masked[k : k + STEP_ROWS]
            new.append(sums[k] + tile_sum(masked[:STEP_ROWS] * inner[TILE - k : TILE - k + STEP_ROWS]))
        new.append(sums[WIDTH] + tile_sum(here))
        back_ref[r, :] = total.astype(BF16)
        return tuple(new)

    tile = jnp.zeros((TILE, taps.shape[1]), F32)
    sums = lax.fori_loop(0, steps, step, (tile,) * (WIDTH + 1), unroll=4)
    rows = [jnp.sum(a, axis=0, keepdims=True) for a in sums]
    sums_ref[...] = jnp.concatenate(rows + [jnp.zeros((TILE - len(rows), taps.shape[1]), F32)], axis=0)


def forward_gates_kernel(
    first_ref, block_ref, w_rate_ref, w_entry_ref, conv_ref, branch_ref, vec_ref, offset_ref, states_ref, mixed_ref,
    rate_ref, entry_ref,
):
    rate_ref[...] = dot(block_ref[...], w_rate_ref[...])
    entry_ref[...] = dot(block_ref[...], w_entry_ref[...])
    forward_kernel(rate_ref, entry_ref, conv_ref, branch_ref, vec_ref, offset_ref, states_ref, mixed_ref)


def backward_gates_kernel(
    first_ref, block_ref, w_rate_ref, w_entry_ref, conv_ref, branch_ref, vec_ref, offset_ref, states_ref, back_ref,
    back_branch_ref, back_gates_ref, direct_ref, sums_ref, rate_ref, entry_ref,
):
    rate_ref[...] = dot(block_ref[...], w_rate_ref[...])
    entry_ref[...] = dot(block_ref[...], w_entry_ref[...])
    backward_kernel(
        rate_ref, entry_ref, conv_ref, branch_ref, vec_ref, offset_ref, states_ref, back_ref,
        back_branch_ref, back_gates_ref, direct_ref, sums_ref,
    )


def conv_wide_kernel(first_ref, inner_ref, taps_ref, offset_ref, conv_ref):
    conv_kernel(inner_ref, taps_ref, offset_ref, conv_ref)


def conv_back_gates_kernel(
    first_ref, gates_ref, w_rate_ref, w_entry_ref, direct_ref, inner_ref, taps_ref, offset_ref, back_ref, sums_ref,
    total_ref,
):
    total_ref[...] = contract_cols(gates_ref[0], w_rate_ref[...]) + contract_cols(gates_ref[1], w_entry_ref[...])
    conv_back_kernel(direct_ref, total_ref, inner_ref, taps_ref, offset_ref, back_ref, sums_ref)


def by_block(kernel, first, ins, outs, scratch, own):
    def spec(how, shape):
        rows = shape[-2]
        half = BLOCK // LANES
        return {
            "own": pl.BlockSpec((rows, LANES), lambda j, f: (0, j)),
            "wide": pl.BlockSpec((rows, LANES), lambda j, f: (0, f[0] + j)),
            "block": pl.BlockSpec((rows, BLOCK), lambda j, f: (0, (f[0] + j) // half)),
            "wide2": pl.BlockSpec((2, rows, LANES), lambda j, f: (0, 0, f[0] + j)),
            "block2": pl.BlockSpec((2, rows, BLOCK), lambda j, f: (0, 0, (f[0] + j) // half)),
            "columns": pl.BlockSpec((BLOCK, LANES), lambda j, f: ((f[0] + j) // half, (f[0] + j) % half)),
            "rows": pl.BlockSpec((LANES, BLOCK), lambda j, f: (f[0] + j, 0)),
            "one": pl.BlockSpec((rows, 1), lambda j, f: (0, 0)),
        }[how]

    count = ins[0][1].shape[-2]
    return pl.pallas_call(
        kernel,
        grid_spec=pltpu.PrefetchScalarGridSpec(
            num_scalar_prefetch=1,
            grid=(own // LANES,),
            in_specs=[spec(how, a.shape) for how, a in ins],
            out_specs=[spec(how, shape) for how, shape, _ in outs],
            scratch_shapes=[pltpu.VMEM((count, LANES), F32)] * scratch,
        ),
        out_shape=[jax.ShapeDtypeStruct(shape, kind) for _, shape, kind in outs],
        compiler_params=pltpu.CompilerParams(vmem_limit_bytes=VMEM_BYTES),
        cost_estimate=pl.CostEstimate(
            flops=60 * count * own,
            bytes_accessed=sum(a.size * a.dtype.itemsize for _, a in ins) * 2,
            transcendentals=4 * count * own,
        ),
    )(first, *(a for _, a in ins))


def fill_edge(place, wide, own):
    edge = wide.shape[-1] - own
    from_lane = jnp.where(place.c == 0, own - edge, edge)
    to_lane = jnp.where(place.c == 0, own, 0)
    got = place.swap_core(lax.dynamic_slice_in_dim(wide, from_lane, edge, axis=wide.ndim - 1))
    return lax.dynamic_update_slice_in_dim(wide, got, to_lane, axis=wide.ndim - 1)


def by_channel(kernel, ins, outs, width, cost=40):
    padded = -(-width // LANES) * LANES

    def widened(a):
        return a if a.shape[1] in (1, padded) else jnp.pad(a, ((0, 0), (0, padded - width)))

    ins = [widened(a) for a in ins]
    specs = [
        pl.BlockSpec((a.shape[0], 1), lambda i: (0, 0))
        if a.shape[1] == 1
        else pl.BlockSpec((a.shape[0], LANES), lambda i: (0, i))
        for a in ins
    ]
    results = pl.pallas_call(
        kernel,
        grid=(padded // LANES,),
        in_specs=specs,
        out_specs=[
            pl.BlockSpec(rows + (LANES,), lambda i, rows=rows: (0,) * len(rows) + (i,)) for rows, _ in outs
        ],
        out_shape=[jax.ShapeDtypeStruct(rows + (padded,), kind) for rows, kind in outs],
        compiler_params=pltpu.CompilerParams(vmem_limit_bytes=VMEM_BYTES),
        cost_estimate=pl.CostEstimate(
            flops=cost * outs[0][0][0] * padded,
            bytes_accessed=sum(a.size * a.dtype.itemsize for a in ins) * 2,
            transcendentals=4 * outs[0][0][0] * padded,
        ),
    )(*ins)
    return [a[..., :width] for a in results]


def rms_norm(values, gain):
    return values * lax.rsqrt(jnp.mean(values * values, axis=-1, keepdims=True) + EPSILON) * gain


def rms_back(values, gain, back):
    scale = lax.rsqrt(jnp.mean(values * values, axis=-1, keepdims=True) + EPSILON)
    unit = values * scale
    grad_gain = jnp.sum(back * unit, axis=0)
    lifted = back * gain
    return scale * (lifted - unit * jnp.mean(lifted * unit, axis=-1, keepdims=True)), grad_gain


class Near:
    def __init__(self):
        self.n_dp, self.n_seq = lax.axis_size("dp"), lax.axis_size("seq")
        self.n_q = self.n_dp // 2
        self.dp, self.seq = lax.axis_index("dp"), lax.axis_index("seq")
        self.p, self.q = self.dp % 2, self.dp // 2
        self.c, self.x = self.seq % 2, self.seq // 2
        self.core = {"dp": self.dp, "seq": self.seq + 1 - 2 * self.c}
        self.over_x = {"dp": self.dp, "seq": self.seq + 2 - 4 * self.x}
        self.over_y = {"dp": self.dp + 1 - 2 * self.p, "seq": self.seq}

    def z(self, way):
        return {"dp": self.dp + 2 * way, "seq": self.seq}


def signal(device):
    pl.semaphore_signal(
        pltpu.get_barrier_semaphore(), inc=1, device_id=device, device_id_type=pl.DeviceIdType.MESH
    )


def remote(source, target, sems, index, device):
    return pltpu.make_async_remote_copy(
        src_ref=source,
        dst_ref=target,
        send_sem=sems[0].at[index],
        recv_sem=sems[1].at[index],
        device_id=device,
        device_id_type=pl.DeviceIdType.MESH,
    )


def gather_kernel(in_pack, out_pack, tok, cot, in_all, out_all, group_x, cot_c, cot_o, send, recv, local):
    near = Near()
    n_q, n_seq, n_dp = near.n_q, near.n_seq, near.n_dp
    dp, seq, p, q = near.dp, near.seq, near.p, near.q
    sems = (send, recv)
    place = dp * n_seq + seq
    to_dp, to_seq = place % n_dp, place // n_dp
    origin = seq * n_dp + dp
    turned_to = {"dp": to_dp, "seq": to_seq}
    turned_from = {"dp": origin // n_seq, "seq": origin % n_seq}
    moves = jnp.logical_or(to_dp != dp, to_seq != seq)
    above, below = q + 1 < n_q, q >= 1

    A2A, TURN, TOK, COT, TOKC, COTC, YB, YIN = 0, 3, 4, 5, 6, 8, 10, 11
    YOUT = YIN + n_q
    ZIN, ZOUT, ZB = YOUT + n_q, YOUT + n_q + n_q, YOUT + 3 * n_q
    SEND_DOWN = ZB + 2 * n_q

    for d in range(1, n_seq):
        signal({"dp": dp, "seq": (seq + d) % n_seq})
    signal(near.over_y)
    pl.when(above)(lambda: signal(near.z(1)))
    pl.when(below)(lambda: signal(near.z(-1)))
    pl.when(moves)(lambda: signal(turned_from))
    pl.semaphore_wait(
        pltpu.get_barrier_semaphore(),
        n_seq + above.astype(jnp.int32) + below.astype(jnp.int32) + moves.astype(jnp.int32),
    )

    sent = []

    def go(copy):
        copy.start()
        sent.append(copy)
        return copy

    for d in range(1, n_seq):
        peer = (seq + d) % n_seq
        go(remote(in_pack.at[peer], in_all.at[dp, seq], sems, A2A + d - 1, {"dp": dp, "seq": peer}))
    turn = remote(out_pack, out_all.at[to_dp], sems, TURN, turned_to)
    keep = [
        pltpu.make_async_copy(in_pack.at[seq], in_all.at[dp, seq], local.at[0]),
        pltpu.make_async_copy(tok, group_x.at[seq], local.at[1]),
        pltpu.make_async_copy(cot, cot_c.at[0], local.at[2]),
    ]
    stay = pltpu.make_async_copy(out_pack, out_all.at[dp], local.at[3])
    pl.when(moves)(turn.start)
    pl.when(jnp.logical_not(moves))(stay.start)
    for copy in keep:
        copy.start()
    go(remote(tok, group_x.at[seq], sems, TOK, near.over_x))
    go(remote(cot, cot_c.at[1], sems, COT, near.over_x))
    go(remote(tok, group_x.at[seq], sems, TOKC, near.core))
    go(remote(cot, cot_o.at[0], sems, COTC, near.core))

    def lines(block):
        d = 2 * block + p
        return [(ZIN + block, in_all.at[d, pl.ds(0, n_seq - 1)]), (ZOUT + block, out_all.at[d])]

    def corners(block):
        return [(ZB + 2 * block + i, in_all.at[2 * block + i, n_seq - 1]) for i in range(2)]

    def z_copy(number, ref, way):
        index = number if way > 0 else number + (SEND_DOWN - ZIN)
        return pltpu.make_async_remote_copy(
            src_ref=ref, dst_ref=ref, send_sem=send.at[index], recv_sem=recv.at[number],
            device_id=near.z(way), device_id_type=pl.DeviceIdType.MESH,
        )

    def y_copies(block):
        d = 2 * block + p
        return [
            remote(in_all.at[d, pl.ds(0, n_seq - 1)], in_all.at[d, pl.ds(0, n_seq - 1)], sems, YIN + block, near.over_y),
            remote(out_all.at[d], out_all.at[d], sems, YOUT + block, near.over_y),
        ]

    def y_arrivals(block):
        d = 2 * block + 1 - p
        return [
            remote(in_all.at[d, pl.ds(0, n_seq - 1)], in_all.at[d, pl.ds(0, n_seq - 1)], sems, YIN + block, near.over_y),
            remote(out_all.at[d], out_all.at[d], sems, YOUT + block, near.over_y),
        ]

    for d in range(1, n_seq):
        source = (seq + n_seq - d) % n_seq
        remote(in_pack.at[0], in_all.at[dp, source], sems, A2A + d - 1, {"dp": dp, "seq": source}).wait_recv()
    keep[0].wait()
    y_first = remote(in_all.at[dp, n_seq - 1], in_all.at[dp, n_seq - 1], sems, YB, near.over_y)
    go(y_first)

    def both_ways(pairs):
        for number, ref in pairs:
            pl.when(above)(lambda number=number, ref=ref: z_copy(number, ref, 1).start())
            pl.when(below)(lambda number=number, ref=ref: z_copy(number, ref, -1).start())

    own, own_y = lines(q), y_copies(q)
    both_ways(own[:1])
    go(own_y[0])
    pl.when(moves)(lambda: remote(out_pack, out_all.at[dp], sems, TURN, turned_to).wait_recv())
    pl.when(jnp.logical_not(moves))(stay.wait)
    both_ways(own[1:])
    go(own_y[1])
    other = 2 * q + 1 - p
    remote(in_all.at[other, n_seq - 1], in_all.at[other, n_seq - 1], sems, YB, near.over_y).wait_recv()
    both_ways(corners(q))

    for k in range(1, n_q):
        for way in (1, -1):
            block = q - way * k
            there = block >= 0 if way > 0 else block < n_q
            on = above if way > 0 else below

            def arrived(block=block, way=way, on=on):
                for (number, ref), y_copy in zip(lines(block), y_copies(block)):
                    z_copy(number, ref, way).wait_recv()
                    pl.when(on)(lambda number=number, ref=ref: z_copy(number, ref, way).start())
                    y_copy.start()
                for number, ref in corners(block):
                    z_copy(number, ref, way).wait_recv()
                    pl.when(on)(lambda number=number, ref=ref: z_copy(number, ref, way).start())

            pl.when(there)(arrived)
        if k == 1:
            other_x = seq + 2 - 4 * near.x
            remote(tok, group_x.at[other_x], sems, TOK, near.over_x).wait_recv()
            go(remote(group_x.at[other_x], group_x.at[other_x], sems, TOKC + 1, near.core))
            remote(cot, cot_c.at[1], sems, COT, near.over_x).wait_recv()
            go(remote(cot_c.at[1], cot_o.at[1], sems, COTC + 1, near.core))

    for block in range(n_q):
        for copy in y_arrivals(block):
            copy.wait_recv()
    for number, place_at in ((0, seq + 1 - 2 * near.c), (1, seq + 1 - 2 * near.c + 2 - 4 * near.x)):
        remote(tok, group_x.at[place_at], sems, TOKC + number, near.core).wait_recv()
        remote(cot, cot_o.at[number], sems, COTC + number, near.core).wait_recv()

    for copy in sent:
        copy.wait_send()
    pl.when(moves)(turn.wait_send)
    keep[1].wait()
    keep[2].wait()
    for k in range(n_q):
        for way in (1, -1):
            block = q - way * k
            there = block >= 0 if way > 0 else block < n_q
            on = above if way > 0 else below

            def gone(block=block, way=way, on=on, k=k):
                for number, ref in lines(block) + corners(block):
                    pl.when(on)(lambda number=number, ref=ref: z_copy(number, ref, way).wait_send())
                if k > 0:
                    for copy in y_copies(block):
                        copy.wait_send()

            pl.when(there)(gone)


def gather_all(place, in_pack, out_pack, tok, cot):
    n_dp, n_seq, n_q = place.n_dp, place.n_seq, place.n_q
    kept = [pl.BlockSpec(memory_space=pl.ANY)] * 5
    total = 11 + 6 * n_q + 4 * n_q
    return pl.pallas_call(
        gather_kernel,
        in_specs=[pl.BlockSpec(memory_space=pltpu.VMEM)] * 4,
        out_specs=kept,
        out_shape=[
            jax.ShapeDtypeStruct((n_dp,) + in_pack.shape, BF16),
            jax.ShapeDtypeStruct((n_dp,) + out_pack.shape, BF16),
            jax.ShapeDtypeStruct((n_seq,) + tok.shape, BF16),
            jax.ShapeDtypeStruct((2,) + cot.shape, BF16),
            jax.ShapeDtypeStruct((2,) + cot.shape, BF16),
        ],
        scratch_shapes=[
            pltpu.SemaphoreType.DMA((total,)),
            pltpu.SemaphoreType.DMA((total,)),
            pltpu.SemaphoreType.DMA((4,)),
        ],
        compiler_params=pltpu.CompilerParams(
            collective_id=0, has_side_effects=True, vmem_limit_bytes=VMEM_BYTES
        ),
        name="gather_all",
    )(in_pack, out_pack, tok, cot)


CHUNKS = 4


class Chunks:
    def __init__(self, sems, rows):
        self.sems, self.size, self.sent = sems, rows // CHUNKS, []

    def rows(self, i):
        return pl.ds(i * self.size, self.size)

    def copy(self, group, i, source, target, device):
        return remote(source, target, self.sems, CHUNKS * group + i, device)

    def go(self, group, i, source, target, device):
        copy = self.copy(group, i, source, target, device)
        copy.start()
        self.sent.append(copy)

    def arrived(self, group, i, target, device):
        self.copy(group, i, target, target, device).wait_recv()

    def finish(self):
        for copy in self.sent:
            copy.wait_send()


def greet(devices):
    for device in devices:
        signal(device)
    pl.semaphore_wait(pltpu.get_barrier_semaphore(), len(devices))


def middle_kernel(
    mixed, w_out, tok, gain, cot_c, cot_o, away, middle, rows, pair_cot,
    part, from_core, to_x, from_x, normed, send, recv, local,
    cots_here, cot_send, cot_recv, cot_local,
):
    near = Near()
    x, c, seq = near.x, near.c, near.seq
    ch = Chunks((send, recv), tok.shape[0])
    all_chunks = range(CHUNKS)
    seq_x, seq_c = seq + 2 - 4 * x, seq + 1 - 2 * c
    seq_cx = seq_c + 2 - 4 * x
    loads = [
        pltpu.make_async_copy(source, cots_here.at[n], cot_local.at[n]) for n, source in enumerate((cot_c, cot_o, away))
    ]
    for load in loads:
        load.start()
    greet([near.core, near.over_x, near.over_y])
    far_cot = remote(cots_here.at[2], pair_cot.at[1, 1], (cot_send, cot_recv), 0, near.core)
    cots = [
        pltpu.make_async_copy(cots_here.at[n], pair_cot.at[i], cot_local.at[n])
        for n, i in enumerate(((0, 0), (0, 1), (1, 0)))
    ]
    CORE_FAR, CORE_NEAR, SUM_X, OWN_X, OWN_Y, OWN_C, FWD_X, FWD_Y, FWD_C = 0, 1, 2, 3, 4, 5, 6, 7, 8
    FWD_C2, FWD_C3 = 9, 10

    for group, slot, at in ((CORE_FAR, 0, seq_cx), (CORE_NEAR, 1, seq_c)):
        part[at, :, :] = dot(mixed[at], w_out[...]).astype(BF16)
        for i in all_chunks:
            r = ch.rows(i)
            ch.go(group, i, part.at[at, r], from_core.at[slot, r], near.core)
        own = seq_x if slot == 0 else seq
        part[own, :, :] = dot(mixed[own], w_out[...]).astype(BF16)
    for i in all_chunks:
        r = ch.rows(i)
        ch.arrived(CORE_FAR, i, from_core.at[0, r], near.core)
        to_x[r, :] = (part[seq_x, r, :].astype(F32) + from_core[0, r, :].astype(F32)).astype(BF16)
        ch.go(SUM_X, i, to_x.at[r], from_x.at[r], near.over_x)
    for load in loads:
        load.wait()
    far_cot.start()
    for copy in cots:
        copy.start()
    kept = []
    for i in all_chunks:
        r = ch.rows(i)
        ch.arrived(CORE_NEAR, i, from_core.at[1, r], near.core)
        ch.arrived(SUM_X, i, from_x.at[r], near.over_x)
        total = tok[r, :].astype(F32) + (
            part[seq, r, :].astype(F32) + from_core[1, r, :].astype(F32) + from_x[r, :].astype(F32)
        )
        middle[r, :] = total
        scale = lax.rsqrt(jnp.mean(total * total, axis=-1, keepdims=True) + EPSILON)
        normed[r, :] = (total * scale * gain[...]).astype(BF16)
        ch.go(OWN_X, i, normed.at[r], rows.at[0, 0, 1, r], near.over_x)
        ch.go(OWN_Y, i, normed.at[r], rows.at[1, 0, 0, r], near.over_y)
        ch.go(OWN_C, i, normed.at[r], rows.at[0, 1, 0, r], near.core)
        keep = pltpu.make_async_copy(normed.at[r], rows.at[0, 0, 0, r], local.at[i])
        keep.start()
        kept.append(keep)
    for i in all_chunks:
        r = ch.rows(i)
        here = rows.at[0, 0, 1, r]
        ch.arrived(OWN_X, i, here, near.over_x)
        if i >= CHUNKS // 2:
            ch.go(FWD_Y, i, here, rows.at[1, 0, 1, r], near.over_y)
        ch.go(FWD_C, i, here, rows.at[0, 1, 1, r], near.core)
        here = rows.at[1, 0, 0, r]
        ch.arrived(OWN_Y, i, here, near.over_y)
        if i < CHUNKS // 2:
            ch.go(FWD_X, i, here, rows.at[1, 0, 1, r], near.over_x)
        ch.go(FWD_C2, i, here, rows.at[1, 1, 0, r], near.core)
    for i in all_chunks:
        r = ch.rows(i)
        here = rows.at[1, 0, 1, r]
        if i < CHUNKS // 2:
            ch.arrived(FWD_X, i, here, near.over_x)
        else:
            ch.arrived(FWD_Y, i, here, near.over_y)
        ch.go(FWD_C3, i, here, rows.at[1, 1, 1, r], near.core)
    for group, at in ((OWN_C, (0, 0)), (FWD_C, (0, 1)), (FWD_C2, (1, 0)), (FWD_C3, (1, 1))):
        for i in all_chunks:
            ch.arrived(group, i, rows.at[at[0], 1, at[1], ch.rows(i)], near.core)
    for keep in kept + cots:
        keep.wait()
    far_cot.wait()
    ch.finish()


def sum_middle(place, mixed, w_out, tok, gain, cot_c, cot_o, away):
    count, width = tok.shape
    vmem, kept = pl.BlockSpec(memory_space=pltpu.VMEM), pl.BlockSpec(memory_space=pl.ANY)
    return pl.pallas_call(
        middle_kernel,
        in_specs=[vmem, vmem, vmem, vmem, kept, kept, kept],
        out_specs=[vmem, kept, kept],
        out_shape=[
            jax.ShapeDtypeStruct((count, width), F32),
            jax.ShapeDtypeStruct((2, 2, 2, count, width), BF16),
            jax.ShapeDtypeStruct((2, 2, 2, count, width), BF16),
        ],
        scratch_shapes=[
            pltpu.VMEM((place.n_seq, count, width), BF16),
            pltpu.VMEM((2, count, width), BF16),
            pltpu.VMEM((count, width), BF16),
            pltpu.VMEM((count, width), BF16),
            pltpu.VMEM((count, width), BF16),
            pltpu.SemaphoreType.DMA((11 * CHUNKS,)),
            pltpu.SemaphoreType.DMA((11 * CHUNKS,)),
            pltpu.SemaphoreType.DMA((CHUNKS,)),
            pltpu.VMEM((3,) + cot_c.shape, BF16),
            pltpu.SemaphoreType.DMA((1,)),
            pltpu.SemaphoreType.DMA((1,)),
            pltpu.SemaphoreType.DMA((3,)),
        ],
        compiler_params=pltpu.CompilerParams(
            collective_id=1, has_side_effects=True, vmem_limit_bytes=VMEM_BYTES
        ),
        name="sum_middle",
    )(mixed.reshape(place.n_seq, count, -1), w_out, tok, gain, cot_c, cot_o, away)


class Piece:
    def __init__(self, kind, refs, start, rows):
        self.kind = kind
        self.part, self.total, self.up, self.down, self.low = refs[:5]
        self.over, self.pair = refs[5:] if len(refs) > 5 else (None, self.part)
        self.start, self.count = start, rows
        self.rows = pl.ds(start, rows)
        self.width = self.low.shape[1]

    def at(self, ref, block):
        return ref.at[block, self.rows]

    def read(self, ref, block):
        return ref[block, self.rows, :].astype(F32)

    def columns(self, block, width):
        return pl.ds(block * width if isinstance(block, int) else pl.multiple_of(block * width, width), width)

    def pair_at(self, block):
        if self.kind == "columns":
            return self.pair.at[self.rows, self.columns(block, self.width)]
        return self.pair.at[block, self.rows]

    def pair_value(self, block):
        if self.kind == "columns":
            return self.pair[self.rows, self.columns(block, self.width)]
        return self.pair[block, self.rows, :]

    def side(self, way):
        return self.up if way > 0 else self.down


class LineSums:
    def __init__(self, near, pieces, sems, local):
        self.near, self.pieces, self.sems, self.local = near, pieces, sems, local
        n_q, n_seq, n_dp = near.n_q, near.n_seq, near.n_dp
        self.ends = n_q + 2 * (n_q - 1)
        self.per = self.ends + n_seq
        owner = near.seq * n_dp + near.dp
        self.to_dp, self.to_seq = owner // n_seq, owner % n_seq
        self.moves = jnp.logical_or(self.to_dp != near.dp, self.to_seq != near.seq)
        self.above, self.below = near.q + 1 < n_q, near.q >= 1

    def y_copy(self, n, block):
        piece, near = self.pieces[n], self.near
        source = piece.at(piece.part, 2 * block + 1 - near.p)
        return remote(source, piece.at(piece.over, block), self.sems, n * self.per + block, near.over_y)

    def z_copy(self, n, k, way, arrival=False):
        piece, n_q = self.pieces[n], self.near.n_q
        side = piece.side(way)
        target = piece.at(side, k - 1)
        if arrival:
            source = target
        elif k == 1:
            source = piece.pair_at(n_q - 1 if way > 0 else 0)
        else:
            source = piece.at(side, k - 2)
        number = n * self.per + n_q + (k - 1) * 2 + (way < 0)
        return remote(source, target, self.sems, number, self.near.z(way))

    def sends(self, k, way):
        q, n_q = self.near.q, self.near.n_q
        if way > 0:
            return jnp.logical_and(q <= k - 1, self.above)
        return jnp.logical_and(q >= n_q - k, self.below)

    def gets(self, k, way):
        q, n_q = self.near.q, self.near.n_q
        if way > 0:
            return jnp.logical_and(q <= k, self.below)
        return jnp.logical_and(q + 1 >= n_q - k, self.above)

    def y_start(self, *numbers):
        for n in numbers:
            for block in range(self.near.n_q):
                self.y_copy(n, block).start()

    def pair_up(self, n):
        piece = self.pieces[n]
        for block in range(self.near.n_q):
            self.y_copy(n, block).wait_recv()
            total = piece.read(piece.part, 2 * block + self.near.p) + piece.read(piece.over, block)
            piece.pair[block, piece.rows, :] = total.astype(BF16)

    def z_step(self, n, k):
        piece, q, n_q = self.pieces[n], self.near.q, self.near.n_q
        for way in (1, -1):

            def stage(way=way):
                side = piece.side(way)
                if k > 1:
                    block = n_q - k + q if way > 0 else k + q - n_q
                    came = self.gets(k - 1, way)

                    def add():
                        self.z_copy(n, k - 1, way, True).wait_recv()
                        total = piece.read(side, k - 2) + piece.pair_value(block).astype(F32)
                        side[k - 2, piece.rows, :] = total.astype(BF16)

                    def begin():
                        side[k - 2, piece.rows, :] = piece.pair_value(block)

                    pl.when(came)(add)
                    pl.when(jnp.logical_not(came))(begin)
                self.z_copy(n, k, way).start()

            pl.when(self.sends(k, way))(stage)

    def owners(self, n):
        piece, near = self.pieces[n], self.near
        if piece.kind == "turn":
            return [(None, self.moves)]
        if piece.kind == "rows":
            other = piece.start // (piece.low.shape[0] // 2)
            return [(other, near.p != other)]
        if piece.kind == "columns":
            return [(near.p, None), (1 - near.p, True)]
        each = piece.low.shape[0] // near.n_seq
        first = piece.start // each
        return [(j, near.seq != j) for j in range(first, first + piece.count // each)]

    def end_refs(self, n, j, source=None):
        piece, near = self.pieces[n], self.near
        if piece.kind == "turn":
            return piece.low.at[piece.rows], piece.total.at[piece.rows]
        if piece.kind == "rows":
            to = pl.ds(piece.start % (piece.low.shape[0] // 2), piece.count)
            p = near.p if source is None else source
            return piece.low.at[piece.rows], piece.total.at[to, piece.columns(p, piece.width)]
        if piece.kind == "columns":
            p = near.p if source is None else source
            return piece.low.at[piece.rows, piece.columns(j, piece.width // 2)], piece.total.at[p, piece.rows]
        each = piece.low.shape[0] // near.n_seq
        seq = near.seq if source is None else source
        return piece.low.at[pl.ds(j * each, each)], piece.total.at[:, piece.columns(seq, piece.width)]

    def end_copy(self, n, j, source=None):
        piece, near = self.pieces[n], self.near
        here, target = self.end_refs(n, j, source)
        first = n * self.per + self.ends
        if piece.kind == "turn":
            return remote(here, target, self.sems, first, {"dp": self.to_dp, "seq": self.to_seq})
        if piece.kind in ("rows", "columns"):
            return remote(target if source is not None else here, target, self.sems, first, near.over_y)
        if source is not None:
            return remote(target, target, self.sems, first + source, {"dp": near.dp, "seq": j})
        return pltpu.make_async_remote_copy(
            src_ref=here, dst_ref=target, send_sem=self.sems[0].at[first + j],
            recv_sem=self.sems[1].at[first + near.seq],
            device_id={"dp": near.dp, "seq": j}, device_id_type=pl.DeviceIdType.MESH,
        )

    def stay_copy(self, n, j):
        here, target = self.end_refs(n, j)
        return pltpu.make_async_copy(here, target, self.local.at[n])

    def finish(self, n):
        piece, k = self.pieces[n], self.near.n_q - 1
        piece.low[piece.rows, :] = piece.pair_value(self.near.q)

        def add(way):
            self.z_copy(n, k, way, True).wait_recv()
            total = piece.low[piece.rows, :].astype(F32) + piece.read(piece.side(way), k - 1)
            piece.low[piece.rows, :] = total.astype(BF16)

        pl.when(self.below)(lambda: add(1))
        pl.when(self.above)(lambda: add(-1))
        for j, away in self.owners(n):
            if piece.kind == "columns":
                (self.end_copy if away else self.stay_copy)(n, j).start()
                continue
            pl.when(away)(lambda j=j: self.end_copy(n, j).start())
            pl.when(jnp.logical_not(away))(lambda j=j: self.stay_copy(n, j).start())

    def z_steps(self, numbers, k):
        for n in numbers:
            self.z_step(n, k)

    def finish_all(self, numbers):
        for n in numbers:
            self.finish(n)

    def arrive(self, n, j):
        piece, near = self.pieces[n], self.near
        self.stay_copy(n, j).wait()
        if piece.kind in ("rows", "columns"):
            self.end_copy(n, j, 1 - near.p).wait_recv()
            return
        for source in range(near.n_seq):
            if source != j:
                self.end_copy(n, j, source).wait_recv()

    def close(self):
        for n, piece in enumerate(self.pieces):
            for j, away in self.owners(n):
                if piece.kind == "turn":
                    pl.when(away)(lambda n=n, j=j: self.end_copy(n, j).wait())
                    pl.when(jnp.logical_not(away))(lambda n=n, j=j: self.stay_copy(n, j).wait())
                elif piece.kind == "columns":
                    self.end_copy(n, j).wait_send() if away else self.arrive(n, j)
                else:
                    pl.when(away)(lambda n=n, j=j: self.end_copy(n, j).wait_send())
                    pl.when(jnp.logical_not(away))(lambda n=n, j=j: self.arrive(n, j))
            if piece.over is not None:
                for block in range(self.near.n_q):
                    self.y_copy(n, block).wait_send()
            for k in range(1, self.near.n_q):
                for way in (1, -1):
                    pl.when(self.sends(k, way))(lambda n=n, k=k, way=way: self.z_copy(n, k, way).wait_send())


def line_scratch(place, parts, cuts):
    n_q, n_seq = place.n_q, place.n_seq
    outs, scratch, pieces = [], [], 0
    for part, (kind, cut) in zip(parts, cuts):
        rows, cols = part.shape[-2:]
        if kind == "columns":
            cols = cols // n_q
        shape = {
            "seq": (rows // n_seq, n_seq * cols),
            "turn": (rows, cols),
            "rows": (rows // 2, 2 * cols),
            "columns": (2, rows, cols // 2),
        }[kind]
        outs.append(jax.ShapeDtypeStruct(shape, BF16))
        sizes = [(n_q - 1, rows, cols)] * 2 + [(rows, cols)]
        if kind in ("seq", "turn"):
            sizes += [(n_q, rows, cols)] * 2
        scratch += [pltpu.VMEM(size, BF16) for size in sizes]
        pieces += cut
    total = pieces * (n_q + 2 * (n_q - 1) + n_seq)
    sems = [
        pltpu.SemaphoreType.DMA((total,)),
        pltpu.SemaphoreType.DMA((total,)),
        pltpu.SemaphoreType.DMA((pieces,)),
    ]
    return outs, scratch + sems


def line_pieces(cuts, parts, totals, scratch):
    pieces, scratch = [], list(scratch)
    for (kind, cut), part, total in zip(cuts, parts, totals):
        take = 5 if kind in ("seq", "turn") else 3
        refs = [part, total] + scratch[:take]
        scratch = scratch[take:]
        rows = part.shape[-2] // cut
        pieces += [Piece(kind, refs, i * rows, rows) for i in range(cut)]
    return pieces


def greet_lines(near, others=()):
    above, below = near.q + 1 < near.n_q, near.q >= 1
    for device in others:
        signal(device)
    pl.when(above)(lambda: signal(near.z(1)))
    pl.when(below)(lambda: signal(near.z(-1)))
    return len(others) + above.astype(jnp.int32) + below.astype(jnp.int32)


def weight_sums_kernel(cuts, *refs):
    count = len(cuts)
    near = Near()
    x, c, seq, p, q, n_q = near.x, near.c, near.seq, near.p, near.q, near.n_q
    part, tok, back, gain, mid_grad = refs[:5]
    parts = refs[5 : 5 + count]
    grad_tok, gains = refs[5 + count : 7 + count]
    totals = refs[7 + count : 7 + 2 * count]
    own, from_core, from_x, gain_near, gain_line, send, recv, local, load, gain_send, gain_recv = refs[
        7 + 2 * count : 18 + 2 * count
    ]
    line_refs = refs[18 + 2 * count :]
    lines = LineSums(near, line_pieces(cuts, parts, totals, line_refs[:-3]), line_refs[-3:-1], line_refs[-1])
    ch = Chunks((send, recv), tok.shape[0])
    seq_x, seq_c = seq + 2 - 4 * x, seq + 1 - 2 * c
    seq_cx = seq_c + 2 - 4 * x
    loads = [
        pltpu.make_async_copy(part.at[at], own.at[i], load.at[i]) for i, at in enumerate((seq_x, seq))
    ]
    for copy in loads:
        copy.start()
    origin = near.dp * near.n_seq + seq
    others = [{"dp": near.dp, "seq": (seq + d) % near.n_seq} for d in range(1, near.n_seq)]
    others += [near.over_y]
    along = [{"dp": 2 * ((q + d) % n_q) + p, "seq": seq} for d in range(1, n_q)]
    for device in others + along:
        signal(device)
    pl.when(lines.moves)(lambda: signal({"dp": origin % near.n_dp, "seq": origin // near.n_dp}))
    pl.semaphore_wait(
        pltpu.get_barrier_semaphore(), len(others + along) + lines.moves.astype(jnp.int32)
    )
    CORE_FAR, CORE_NEAR, SUM_X = range(3)
    for group, at, slot in ((CORE_FAR, seq_cx, 0), (CORE_NEAR, seq_c, 1)):
        for i in range(CHUNKS):
            r = ch.rows(i)
            ch.go(group, i, part.at[at, r], from_core.at[slot, r], near.core)
    ready = [n for n, piece in enumerate(lines.pieces) if piece.over is None]
    waiting = [n for n, piece in enumerate(lines.pieces) if piece.over is not None]
    ahead = 2
    lines.y_start(*waiting[:ahead])
    lines.z_steps(ready, 1)
    for copy in loads:
        copy.wait()
    for i in range(CHUNKS):
        r = ch.rows(i)
        ch.arrived(CORE_FAR, i, from_core.at[0, r], near.core)
        from_core[0, r, :] = (own[0, r, :].astype(F32) + from_core[0, r, :].astype(F32)).astype(BF16)
        ch.go(SUM_X, i, from_core.at[0, r], from_x.at[r], near.over_x)
    lines.z_steps(ready, 2)
    gain_sum = jnp.zeros_like(gain)
    for i in range(CHUNKS):
        r = ch.rows(i)
        ch.arrived(CORE_NEAR, i, from_core.at[1, r], near.core)
        ch.arrived(SUM_X, i, from_x.at[r], near.over_x)
        total = own[1, r, :].astype(F32) + from_core[1, r, :].astype(F32) + from_x[r, :].astype(F32)
        value = tok[r, :].astype(F32)
        scale = lax.rsqrt(jnp.mean(value * value, axis=-1, keepdims=True) + EPSILON)
        unit = value * scale
        gain_sum = gain_sum + jnp.sum(total * unit, axis=0, keepdims=True)
        lifted = total * gain[...]
        grad_tok[r, :] = back[r, :] + scale * (
            lifted - unit * jnp.mean(lifted * unit, axis=-1, keepdims=True)
        )

    gain_near[0, :, :] = jnp.concatenate(
        [gain_sum, mid_grad[...], jnp.zeros((TILE - 2, gain.shape[1]), F32)], axis=0
    )
    pairs = [
        remote(gain_near.at[2 * i], gain_near.at[2 * i + 1], (gain_send, gain_recv), i, device)
        for i, device in enumerate((near.core, near.over_x, near.over_y))
    ]
    copies = [
        remote(gain_near.at[6], gain_line.at[i], (gain_send, gain_recv), 3 + i, device) for i, device in enumerate(along)
    ]

    def gain_step(i):
        if 0 < i <= 3:
            pairs[i - 1].wait()
            gain_near[2 * i, :, :] = gain_near[2 * i - 2, :, :] + gain_near[2 * i - 1, :, :]
        for copy in pairs[i : i + 1] if i < 3 else copies if i == 3 else []:
            copy.start()

    gain_step(0)
    for k in range(3, n_q):
        lines.z_steps(ready, k)
    gain_step(1)
    for t in range(len(waiting) + n_q):
        if t < len(waiting):
            lines.pair_up(waiting[t])
            lines.y_start(*waiting[t + ahead : t + ahead + 1])
        for k in range(1, n_q):
            if 0 <= t - (k - 1) < len(waiting):
                lines.z_step(waiting[t - (k - 1)], k)
        if 0 <= t - (n_q - 1) < len(waiting):
            lines.finish(waiting[t - (n_q - 1)])
        if t == 0:
            gain_step(2)
            lines.finish_all(ready)
        if t == 2:
            gain_step(3)
    total = gain_near[6, :, :]
    for i, copy in enumerate(copies):
        copy.wait()
        total = total + gain_line[i, :, :]
    gains[...] = total
    ch.finish()
    lines.close()


def weight_sums(place, part, tok, back, gain, mid_grad, parts, cuts):
    rows, width = tok.shape
    vmem, kept = pl.BlockSpec(memory_space=pltpu.VMEM), pl.BlockSpec(memory_space=pl.ANY)
    outs, scratch = line_scratch(place, parts, cuts)
    n_q = place.n_q
    return pl.pallas_call(
        partial(weight_sums_kernel, cuts),
        in_specs=[kept] + [vmem] * (4 + len(parts)),
        out_specs=[vmem, vmem] + [kept] * len(parts),
        out_shape=[jax.ShapeDtypeStruct((rows, width), F32), jax.ShapeDtypeStruct((TILE, width), F32)] + outs,
        scratch_shapes=[
            pltpu.VMEM((2, rows, width), BF16),
            pltpu.VMEM((2, rows, width), BF16),
            pltpu.VMEM((rows, width), BF16),
            pltpu.VMEM((7, TILE, width), F32),
            pltpu.VMEM((n_q - 1, TILE, width), F32),
            pltpu.SemaphoreType.DMA((3 * CHUNKS,)),
            pltpu.SemaphoreType.DMA((3 * CHUNKS,)),
            pltpu.SemaphoreType.DMA((1,)),
            pltpu.SemaphoreType.DMA((2,)),
            pltpu.SemaphoreType.DMA((2 + n_q,)),
            pltpu.SemaphoreType.DMA((2 + n_q,)),
        ]
        + scratch,
        compiler_params=pltpu.CompilerParams(
            collective_id=3, has_side_effects=True, vmem_limit_bytes=VMEM_BYTES
        ),
        name="weight_sums",
    )(part, tok, back, gain, mid_grad, *parts)


class PlaneSum:
    FAR, TO_X, TO_Y, NEAR = range(4)
    AT = {0: (1, 1), 1: (0, 1), 2: (1, 0), 3: (0, 0)}

    def __init__(self, near, ch, groups, part, local, own, from_core, corner_x, corner_y, got_x, got_y):
        self.near, self.ch, self.part, self.own, self.from_core = near, ch, part, own, from_core
        self.corner_x, self.corner_y, self.got_x, self.got_y = corner_x, corner_y, got_x, got_y
        self.core_group = groups
        self.cx, self.cy, self.gx, self.gy = range(groups + 4, groups + 8)
        half = CHUNKS // 2
        self.half, self.first, self.last = half, range(half), range(half, CHUNKS)
        self.loads = [pltpu.make_async_copy(part.at[i, 0], own.at[i], local.at[i]) for i in range(2)]
        for load in self.loads:
            load.start()

    def to_core(self, group, chunks):
        other_p, other_x = self.AT[group]
        for i in chunks:
            r = self.ch.rows(i)
            self.ch.go(
                self.core_group + group, i, self.part.at[other_p, 1, other_x, r], self.from_core.at[group, r], self.near.core
            )

    def on_chip(self, group, i):
        r = self.ch.rows(i)
        other_p, other_x = self.AT[group]
        self.ch.arrived(self.core_group + group, i, self.from_core.at[group, r], self.near.core)
        return self.own[other_p, other_x, r, :].astype(F32) + self.from_core[group, r, :].astype(F32)

    def start(self):
        for load in self.loads:
            load.wait()
        self.to_core(self.FAR, (0, self.half, 1, self.half + 1))
        self.to_core(self.TO_X, self.first)
        self.to_core(self.TO_Y, self.last)
        self.to_core(self.TO_X, self.last)
        self.to_core(self.TO_Y, self.first)
        self.to_core(self.NEAR, range(CHUNKS))

    def corners(self):
        near, ch = self.near, self.ch
        for i in (0, self.half, 1, self.half + 1):
            r = ch.rows(i)
            self.from_core[self.FAR, r, :] = self.on_chip(self.FAR, i).astype(BF16)
            if i < self.half:
                ch.go(self.cx, i, self.from_core.at[self.FAR, r], self.corner_x.at[r], near.over_x)
            else:
                b = ch.rows(i - self.half)
                ch.go(self.cy, i - self.half, self.from_core.at[self.FAR, r], self.corner_y.at[b], near.over_y)

    def straight(self):
        for i, j in zip(self.first, self.last):
            self.along(self.TO_X, i, self.on_chip(self.TO_X, i))
            self.along(self.TO_Y, j, self.on_chip(self.TO_Y, j))

    def along(self, group, i, total):
        r = self.ch.rows(i)
        self.from_core[group, r, :] = total.astype(BF16)
        if group == self.TO_X:
            self.ch.go(self.gx, i, self.from_core.at[group, r], self.got_x.at[r], self.near.over_x)
        else:
            self.ch.go(self.gy, i, self.from_core.at[group, r], self.got_y.at[r], self.near.over_y)

    def turned(self):
        ch = self.ch
        for i, j in zip(self.first, self.last):
            b = ch.rows(j - self.half)
            ch.arrived(self.cy, j - self.half, self.corner_y.at[b], self.near.over_y)
            self.along(self.TO_X, j, self.on_chip(self.TO_X, j) + self.corner_y[b, :].astype(F32))
            r = ch.rows(i)
            ch.arrived(self.cx, i, self.corner_x.at[r], self.near.over_x)
            self.along(self.TO_Y, i, self.on_chip(self.TO_Y, i) + self.corner_x[r, :].astype(F32))

    def total(self, i):
        r = self.ch.rows(i)
        total = self.on_chip(self.NEAR, i)
        self.ch.arrived(self.gx, i, self.got_x.at[r], self.near.over_x)
        self.ch.arrived(self.gy, i, self.got_y.at[r], self.near.over_y)
        return total + self.got_x[r, :].astype(F32) + self.got_y[r, :].astype(F32)

    @staticmethod
    def scratch(count, width):
        block = pltpu.VMEM((count, width), BF16)
        half = pltpu.VMEM((count // 2, width), BF16)
        return [
            pltpu.VMEM((2, 2, count, width), BF16), pltpu.VMEM((4, count, width), BF16), half, half, block, block
        ]


def back_middle_kernel(cuts, *refs):
    count = len(cuts)
    part, down_part, middle, cot, gain = refs[:5]
    grads = refs[5 : 5 + count]
    back, rows, gain_grad, result = refs[5 + count : 9 + count]
    totals = refs[9 + count : 9 + 2 * count]
    rest = refs[9 + 2 * count :]
    plane_a, plane_b, low = rest[:6], rest[6:12], rest[12]
    send, recv, local, loads_a, loads_b = rest[13:18]
    line_refs = rest[18:]
    near = Near()
    x, c, seq = near.x, near.c, near.seq
    ch = Chunks((send, recv), cot.shape[0])
    seq_x, seq_c = seq + 2 - 4 * x, seq + 1 - 2 * c
    seq_cx = seq_c + 2 - 4 * x
    lines = LineSums(near, line_pieces(cuts, grads, totals, line_refs[:-3]), line_refs[-3:-1], line_refs[-1])
    main = PlaneSum(near, ch, 0, part, loads_a, *plane_a)
    side = PlaneSum(near, ch, 8, down_part, loads_b, *plane_b)
    expected = greet_lines(near, [near.core, near.over_x, near.over_y])
    pl.semaphore_wait(pltpu.get_barrier_semaphore(), expected)
    OWN_X, OWN_C, FWD_C = 16, 17, 18
    half = len(lines.pieces) // 2
    early, late = range(half), range(half, 2 * half)
    steps = range(1, near.n_q)
    schedule = [partial(lines.z_steps, group, k) for k in steps for group in (early, late)]
    schedule += [partial(lines.finish_all, early), partial(lines.finish_all, late)]
    schedule = iter(schedule)

    def along_z():
        work = next(schedule, None)
        if work is not None:
            work()

    main.start()
    along_z()
    along_z()
    main.corners()
    along_z()
    main.straight()
    main.turned()
    side.start()
    along_z()
    gain_sum = jnp.zeros_like(gain)
    kept = []
    for i in range(CHUNKS):
        r = ch.rows(i)
        total = main.total(i)
        value = middle[r, :]
        scale = lax.rsqrt(jnp.mean(value * value, axis=-1, keepdims=True) + EPSILON)
        unit = value * scale
        gain_sum = gain_sum + jnp.sum(total * unit, axis=0, keepdims=True)
        lifted = total * gain[...]
        whole = cot[r, :].astype(F32) + scale * (lifted - unit * jnp.mean(lifted * unit, axis=-1, keepdims=True))
        back[r, :] = whole
        low[r, :] = whole.astype(BF16)
        ch.go(OWN_X, i, low.at[r], rows.at[seq, r], near.over_x)
        ch.go(OWN_C, i, low.at[r], rows.at[seq, r], near.core)
        keep = pltpu.make_async_copy(low.at[r], rows.at[seq, r], local.at[i])
        keep.start()
        kept.append(keep)
    gain_grad[...] = gain_sum
    side.corners()
    along_z()
    side.straight()
    along_z()
    for i in range(CHUNKS):
        here = rows.at[seq_x, ch.rows(i)]
        ch.arrived(OWN_X, i, here, near.over_x)
        ch.go(FWD_C, i, here, here, near.core)
    side.turned()
    along_z()
    for i in range(CHUNKS):
        r = ch.rows(i)
        result[r, :] = (middle[r, :] + side.total(i)).astype(BF16)
    for _ in range(2 * near.n_q):
        along_z()
    for i in range(CHUNKS):
        ch.arrived(OWN_C, i, rows.at[seq_c, ch.rows(i)], near.core)
        ch.arrived(FWD_C, i, rows.at[seq_cx, ch.rows(i)], near.core)
    for keep in kept:
        keep.wait()
    ch.finish()
    lines.close()


def sum_back_middle(place, part, down_part, middle, cot, gain, grads):
    count, width = cot.shape
    cuts = (("columns", 4), ("rows", 4))
    vmem, kept = pl.BlockSpec(memory_space=pltpu.VMEM), pl.BlockSpec(memory_space=pl.ANY)
    outs, scratch = line_scratch(place, grads, cuts)
    return pl.pallas_call(
        partial(back_middle_kernel, cuts),
        in_specs=[kept, kept] + [vmem] * (3 + len(grads)),
        out_specs=[vmem, kept, vmem, vmem] + [kept] * len(grads),
        out_shape=[
            jax.ShapeDtypeStruct((count, width), F32),
            jax.ShapeDtypeStruct((place.n_seq, count, width), BF16),
            jax.ShapeDtypeStruct((1, width), F32),
            jax.ShapeDtypeStruct((count, width), BF16),
        ]
        + outs,
        scratch_shapes=PlaneSum.scratch(count, width)
        + PlaneSum.scratch(count, width)
        + [
            pltpu.VMEM((count, width), BF16),
            pltpu.SemaphoreType.DMA((19 * CHUNKS,)),
            pltpu.SemaphoreType.DMA((19 * CHUNKS,)),
            pltpu.SemaphoreType.DMA((CHUNKS,)),
            pltpu.SemaphoreType.DMA((2,)),
            pltpu.SemaphoreType.DMA((2,)),
        ]
        + scratch,
        compiler_params=pltpu.CompilerParams(
            collective_id=2, has_side_effects=True, vmem_limit_bytes=VMEM_BYTES
        ),
        name="sum_back_middle",
    )(part, down_part, middle, cot, gain, *grads)


def entry_kernel(x_ref, w_ref, normed_ref, branch_ref, inner_ref, gains_ref):
    own = branch_ref.shape[1]

    @pl.when(pl.program_id(0) == 0)
    def _():
        gains_ref[...] = w_ref[:, 2 * own :].astype(F32).T[:TILE, :]

    value = x_ref[...].astype(F32)
    scale = lax.rsqrt(jnp.mean(value * value, axis=-1, keepdims=True) + EPSILON)
    normed = (value * scale * gains_ref[0:1, :]).astype(BF16)
    normed_ref[...] = normed
    inner_ref[...] = dot(normed, w_ref[:, own : 2 * own]).astype(BF16)
    branch_ref[...] = dot(normed, w_ref[:, :own])


def entry_products(x, weights, own, tile):
    rows, width = x.shape
    whole = lambda shape: pl.BlockSpec(shape, lambda i: (0, 0), pipeline_mode=pl.Buffered(1))
    by_tile = lambda cols: pl.BlockSpec((tile, cols), lambda i: (i, 0))
    return pl.pallas_call(
        entry_kernel,
        grid=(rows // tile,),
        in_specs=[by_tile(width), whole(weights.shape)],
        out_specs=[by_tile(width), by_tile(own), by_tile(own), pl.BlockSpec((TILE, width), lambda i: (0, 0))],
        out_shape=[
            jax.ShapeDtypeStruct((rows, width), BF16),
            jax.ShapeDtypeStruct((rows, own), F32),
            jax.ShapeDtypeStruct((rows, own), BF16),
            jax.ShapeDtypeStruct((TILE, width), F32),
        ],
        compiler_params=pltpu.CompilerParams(vmem_limit_bytes=VMEM_BYTES),
        cost_estimate=pl.CostEstimate(
            flops=4 * rows * width * own, bytes_accessed=weights.size * 2 + rows * (width * 4 + own * 6), transcendentals=rows
        ),
        name="entry_products",
    )(x, weights)


def mlp_kernel(
    p_ref, x_ref, cot_ref, gate_ref, up_ref, down_ref, hidden_ref, back_gate_ref, back_up_ref, down_part_ref, back_ref
):
    x = x_ref[...]
    gate_pre = dot(x, gate_ref[...])
    up_pre = dot(x, up_ref[...])
    back_hidden = contract_cols(cot_ref[...], down_ref[...])
    value, slope = gelu_parts(gate_pre)
    hidden = (value * up_pre).astype(BF16)
    back_gate = (back_hidden * up_pre * slope).astype(BF16)
    back_up = (back_hidden * value).astype(BF16)
    hidden_ref[...] = hidden
    back_gate_ref[...] = back_gate
    back_up_ref[...] = back_up
    down_part_ref[...] = dot(hidden, down_ref[...]).astype(BF16)
    back_ref[...] = (contract_cols(back_gate, gate_ref[...]) + contract_cols(back_up, up_ref[...])).astype(BF16)


def mlp_products(p, x, cot, gate_weight, up_weight, down_weight, tile):
    rows, width = x.shape
    units = gate_weight.shape[1] // 2
    by_tile = lambda cols: pl.BlockSpec((tile, cols), lambda i, p: (i, 0))
    half = lambda shape, at: pl.BlockSpec(shape, at, pipeline_mode=pl.Buffered(1))
    columns = half((width, units), lambda i, p: (0, p[0]))
    return pl.pallas_call(
        mlp_kernel,
        grid_spec=pltpu.PrefetchScalarGridSpec(
            num_scalar_prefetch=1,
            grid=(rows // tile,),
            in_specs=[
                by_tile(width), by_tile(width), columns, columns, half((units, width), lambda i, p: (p[0], 0))
            ],
            out_specs=[by_tile(units)] * 3 + [by_tile(width)] * 2,
        ),
        out_shape=[jax.ShapeDtypeStruct((rows, units), BF16)] * 3 + [jax.ShapeDtypeStruct((rows, width), BF16)] * 2,
        compiler_params=pltpu.CompilerParams(vmem_limit_bytes=VMEM_BYTES),
        cost_estimate=pl.CostEstimate(
            flops=12 * rows * width * units, bytes_accessed=rows * width * 8 + units * width * 6, transcendentals=rows * units
        ),
        name="mlp_products",
    )(p, x, cot, gate_weight, up_weight, down_weight)


def mlp_grads_kernel(x_ref, cot_ref, hidden_ref, back_gate_ref, back_up_ref, down_ref, gate_ref, up_ref):
    x = x_ref[...]
    down_ref[...] = contract_rows(hidden_ref[...], cot_ref[...]).astype(BF16)
    gate_ref[...] = contract_rows(x, back_gate_ref[...]).astype(BF16)
    up_ref[...] = contract_rows(x, back_up_ref[...]).astype(BF16)


def mlp_grads(x, cot, hidden, back_gate, back_up, tile):
    rows, width = x.shape
    units = hidden.shape[1]
    columns = pl.BlockSpec((rows, tile), lambda i: (0, i))
    whole = pl.BlockSpec((rows, units), lambda i: (0, 0), pipeline_mode=pl.Buffered(1))
    by_tile = pl.BlockSpec((tile, units), lambda i: (i, 0))
    return pl.pallas_call(
        mlp_grads_kernel,
        grid=(width // tile,),
        in_specs=[columns, columns, whole, whole, whole],
        out_specs=[pl.BlockSpec((units, tile), lambda i: (0, i)), by_tile, by_tile],
        out_shape=[jax.ShapeDtypeStruct((units, width), BF16)] + [jax.ShapeDtypeStruct((width, units), BF16)] * 2,
        compiler_params=pltpu.CompilerParams(vmem_limit_bytes=VMEM_BYTES),
        cost_estimate=pl.CostEstimate(
            flops=6 * rows * width * units, bytes_accessed=rows * width * 4 + units * (rows + width) * 6, transcendentals=0
        ),
        name="mlp_grads",
    )(x, cot, hidden, back_gate, back_up)


def exit_kernel(
    normed_ref, back_out_ref, w_ref, branch_ref, inner_ref, mixed_ref,
    grad_branch_ref, grad_inner_ref, grad_output_ref, part_ref,
):
    own = branch_ref.shape[1]
    normed = normed_ref[...]
    grad_branch_ref[...] = contract_rows(normed, branch_ref[...]).astype(BF16)
    grad_inner_ref[...] = contract_rows(normed, inner_ref[...]).astype(BF16)
    grad_output_ref[...] = contract_rows(mixed_ref[...], back_out_ref[...]).astype(BF16)
    part_ref[...] = (
        contract_cols(branch_ref[...], w_ref[:, :own]) + contract_cols(inner_ref[...], w_ref[:, own : 2 * own])
    ).astype(BF16)


def exit_products(normed, back_out, weights, back_branch, back_inner, mixed, tile):
    rows, width = normed.shape
    own = mixed.shape[1]
    columns = pl.BlockSpec((rows, tile), lambda i: (0, i))
    whole = pl.BlockSpec((rows, own), lambda i: (0, 0), pipeline_mode=pl.Buffered(1))
    by_tile = lambda cols: pl.BlockSpec((tile, cols), lambda i: (i, 0))
    return pl.pallas_call(
        exit_kernel,
        grid=(width // tile,),
        in_specs=[columns, columns, by_tile(weights.shape[1]), whole, whole, whole],
        out_specs=[by_tile(own), by_tile(own), pl.BlockSpec((own, tile), lambda i: (0, i)), columns],
        out_shape=[
            jax.ShapeDtypeStruct((width, own), BF16),
            jax.ShapeDtypeStruct((width, own), BF16),
            jax.ShapeDtypeStruct((own, width), BF16),
            jax.ShapeDtypeStruct((rows, width), BF16),
        ],
        compiler_params=pltpu.CompilerParams(vmem_limit_bytes=VMEM_BYTES),
        cost_estimate=pl.CostEstimate(
            flops=10 * rows * width * own, bytes_accessed=rows * width * 6 + own * (rows + width) * 10, transcendentals=0
        ),
        name="exit_products",
    )(normed, back_out, weights, back_branch, back_inner, mixed)


def shards(
    tokens, row_lengths, branch_weight, inner_weight, output_weight, rate_weight, entry_weight,
    rate_bias, entry_bias, conv_weight, conv_bias, recur_param, norm_gain, mlp_gain,
    gate_weight, up_weight, down_weight, cotangent,
):
    place = Place()
    n_dp, n_seq = place.n_dp, place.n_seq
    tok, width = tokens.shape
    count = tok * n_seq
    rec = branch_weight.shape[1]
    own = rec // n_seq
    blocks = max(-(-(own * (s + 1)) // BLOCK) - own * s // BLOCK for s in range(n_seq))
    spread = blocks * BLOCK
    d_rows = branch_weight.shape[0]
    r_rows = output_weight.shape[0]

    gains = jnp.stack([norm_gain, mlp_gain], axis=1)
    gains = jnp.pad(gains, ((0, 0), (0, LANES - 2)))
    cut = lambda w: w.reshape(d_rows, n_seq, own).swapaxes(0, 1)
    in_pack = jnp.concatenate(
        [cut(branch_weight), cut(inner_weight), jnp.broadcast_to(gains[None], (n_seq,) + gains.shape)], axis=2
    )
    vectors = jnp.concatenate(
        [conv_weight, jnp.stack([conv_bias, rate_bias, entry_bias, recur_param])], axis=0
    )
    vectors = jnp.pad(vectors.T, ((0, 0), (0, LANES - 2 * WIDTH)))
    out_pack = jnp.concatenate([output_weight, rate_weight, entry_weight, vectors], axis=1)
    fast = place.n_x == 2
    if fast:
        in_all, out_all, group_x, cot_c, cot_o = gather_all(place, in_pack, out_pack, tokens, cotangent)
        in_all = in_all.reshape(n_dp * n_seq * d_rows, -1)
        out_all = out_all.reshape(n_dp * r_rows, -1)
    else:
        in_pack = lax.all_to_all(in_pack, "seq", 0, 0, tiled=True).reshape(n_seq * d_rows, -1)
        out_pack = turned(place, out_pack, False)
        in_all = lax.all_gather(in_pack, "dp", axis=0, tiled=True)
        out_all = lax.all_gather(out_pack, "dp", axis=0, tiled=True)
        group_x = gather_seq(place, tokens)
        group_c = gather_seq(place, cotangent)
    w_out = out_all[:, :width]
    gate_rows = window(place, out_all[:, width : width + 2 * BLOCK], 0, own, spread)
    w_rate, w_entry = gate_rows[:, :BLOCK], gate_rows[:, BLOCK:]
    vec = out_all[:, width + 2 * BLOCK : width + 2 * BLOCK + 2 * WIDTH].astype(F32).T
    taps = jnp.pad(vec[: WIDTH + 1], ((0, 7 - WIDTH), (0, 0)))
    gate_vec = jnp.pad(vec[WIDTH + 1 :], ((0, 9 - 2 * WIDTH + WIDTH), (0, 0)))
    first = own * place.seq - jnp.minimum(own * place.seq // BLOCK * BLOCK, rec - spread)
    owned = lambda a, axis: lax.dynamic_slice_in_dim(a, first, own, axis=axis) if spread != own else a

    group_x = group_x.reshape(count, width)
    away = place.swap_pair(cot_c if fast else group_c)
    offsets = row_offsets(row_lengths[0], jnp.arange(count, dtype=jnp.int32))[:, None]

    normed, branch_pre, inner, gain_rows = entry_products(group_x, in_all, own, ENTRY_TILE)
    gain_in, gain_mid = gain_rows[0:1], gain_rows[1:2]
    heads = partial(jnp.einsum, preferred_element_type=F32)
    if fast:
        gate_first = (own * place.seq % BLOCK // LANES).astype(jnp.int32)[None]
        (conv_wide,) = by_block(
            conv_wide_kernel, gate_first, [("own", inner), ("own", taps), ("one", offsets)],
            [("wide", (count, spread), BF16)], 0, own,
        )
        conv_wide = fill_edge(place, conv_wide, own)
        gate_ins = [("block", conv_wide), ("columns", w_rate), ("columns", w_entry), ("wide", conv_wide)]
        gate_ins += [("own", branch_pre), ("own", gate_vec), ("one", offsets)]
        states, mixed = by_block(
            forward_gates_kernel, gate_first, gate_ins,
            [("own", (count, own), F32), ("own", (count, own), BF16)], 2, own,
        )
    else:
        (conv,) = by_channel(conv_kernel, [inner, taps, offsets], [((count,), BF16)], own)
        conv_wide = window(place, conv, 1, own, spread)
        conv_heads = conv_wide.reshape(count, blocks, BLOCK)
        pre_rate, pre_entry = (
            owned(heads("tbc,bcd->tbd", conv_heads, w.reshape(blocks, BLOCK, BLOCK)).reshape(count, spread), 1)
            for w in (w_rate, w_entry)
        )
        states, mixed = by_channel(
            forward_kernel,
            [pre_rate, pre_entry, conv, branch_pre, gate_vec, offsets],
            [((count,), F32), ((count,), BF16)],
            own,
        )
    mixed, away = lax.optimization_barrier((mixed, away))
    whole_x = tokens.astype(F32)
    if fast:
        middle, rows, pair_cot = sum_middle(place, mixed, w_out, tokens, gain_mid, cot_c, cot_o, away)
    else:
        out_part = dot(mixed, w_out).astype(BF16).reshape(n_seq, tok, width)
        middle = whole_x + scatter_seq(place, out_part)
        rows = gather_plane(place, rms_norm(middle, gain_mid).astype(BF16))
        pair_cot = jnp.stack([jnp.where(place.p == 0, group_c, away), jnp.where(place.p == 0, away, group_c)])
    rows, pair_cot = rows.reshape(2 * count, width), pair_cot.reshape(2 * count, width)

    units = gate_weight.shape[1] // 2
    hidden, back_gate, back_up, down_part, back_part = mlp_products(
        place.p.astype(jnp.int32)[None], rows, pair_cot, gate_weight, up_weight, down_weight, MLP_TILE
    )

    n_q = place.n_q
    grad_down_part, grad_gate_part, grad_up_part = mlp_grads(rows, pair_cot, hidden, back_gate, back_up, GRAD_TILE)
    grad_gate_part, grad_up_part = (a.reshape(n_q, -1, units) for a in (grad_gate_part, grad_up_part))
    if fast:
        plane = (2, 2, 2, tok, width)
        back_middle, back_out, grad_mlp_gain, result, down_sum, gate_sum = sum_back_middle(
            place, back_part.reshape(plane), down_part.reshape(plane), middle, cotangent, gain_mid,
            [grad_down_part, grad_gate_part],
        )
        grad_mlp_gain = grad_mlp_gain[0]
    else:
        plane = (2, n_seq, tok, width)
        result = (middle + scatter_plane(place, down_part.reshape(plane))).astype(BF16)
        back_norm, grad_mlp_gain = rms_back(middle, gain_mid, scatter_plane(place, back_part.reshape(plane)))
        back_middle = cotangent.astype(F32) + back_norm
        back_out = gather_seq(place, back_middle.astype(BF16))
        step = q_step(place)
        strip = width // n_q
        down_sum = line_sum(
            lambda i: lax.dynamic_slice_in_dim(grad_down_part, i * strip, strip, 1), n_q, place.q, step
        )
        gate_sum, up_sum = (
            line_sum(partial(lax.dynamic_index_in_dim, a, axis=0, keepdims=False), n_q, place.q, step)
            for a in (grad_gate_part, grad_up_part)
        )
        down_sum, gate_sum, up_sum = (
            split_pair(place, a, axis) for a, axis in ((down_sum, 1), (gate_sum, 0), (up_sum, 0))
        )
    back_out = back_out.reshape(count, width)

    back_mixed = contract_cols(back_out, w_out)
    if fast:
        back_branch, back_gates, direct, gate_sums = by_block(
            backward_gates_kernel, gate_first, gate_ins + [("own", states), ("own", back_mixed)],
            [("own", (count, own), BF16), ("wide2", (2, count, spread), BF16), ("own", (count, own), F32),
             ("own", (TILE, own), F32)], 2, own,
        )
        back_gates = fill_edge(place, back_gates, own)
        back_inner, conv_sums = by_block(
            conv_back_gates_kernel, gate_first,
            [("block2", back_gates), ("rows", w_rate), ("rows", w_entry), ("own", direct), ("own", inner),
             ("own", taps), ("one", offsets)],
            [("own", (count, own), BF16), ("own", (TILE, own), F32)], 1, own,
        )
    else:
        back_branch, back_gates, direct, gate_sums = by_channel(
            backward_kernel,
            [pre_rate, pre_entry, conv, branch_pre, gate_vec, offsets, states, back_mixed],
            [((count,), BF16), ((2, count), BF16), ((count,), F32), ((TILE,), F32)],
            own,
        )
        back_gates = jnp.stack([window(place, a, 1, own, spread) for a in (back_gates[0], back_gates[1])])
        gates_back = sum(
            heads("tbd,bcd->tbc", a.reshape(count, blocks, BLOCK), w.reshape(blocks, BLOCK, BLOCK)).reshape(count, spread)
            for a, w in ((back_gates[0], w_rate), (back_gates[1], w_entry))
        )
        back_inner, conv_sums = by_channel(
            conv_back_kernel,
            [direct, owned(gates_back, 1), inner, taps, offsets],
            [((count,), BF16), ((TILE,), F32)],
            own,
        )
    grad_rate_part, grad_entry_part = (
        owned(
            jnp.concatenate(
                [contract_rows(conv_wide[:, b : b + BLOCK], a[:, b : b + BLOCK]) for b in range(0, spread, BLOCK)], axis=0
            ),
            0,
        )
        for a in (back_gates[0], back_gates[1])
    )
    grad_branch_part, grad_inner_part, grad_output_part, normed_part = exit_products(
        normed, back_out, in_all, back_branch, back_inner, mixed, EXIT_TILE
    )
    normed_part = normed_part.reshape(n_seq, tok, width)

    sums = jnp.concatenate([conv_sums[: WIDTH + 1], gate_sums[:3]], axis=0).T
    sums = jnp.pad(sums, ((0, 0), (0, LANES - 2 * WIDTH))).astype(BF16)
    gate_grads = jnp.concatenate([grad_rate_part.astype(BF16), grad_entry_part.astype(BF16), sums], axis=1)
    parts = [
        a.reshape(n_dp, -1, a.shape[1]) for a in (grad_output_part, grad_branch_part, gate_grads, grad_inner_part)
    ]
    if fast:
        grad_tokens, gains, up_sum, output_sum, branch_sum, gates_sum, inner_sum = weight_sums(
            place, normed_part, tokens, back_middle, gain_in, grad_mlp_gain[None], [grad_up_part] + parts,
            (("rows", 4), ("turn", 1), ("seq", 2), ("turn", 1), ("seq", 2)),
        )
        gains = lax.dynamic_slice_in_dim(gains[:2], (place.dp * n_seq + place.seq) * d_rows, d_rows, axis=1)
    else:
        back_x, grad_norm_gain = rms_back(whole_x, gain_in, scatter_seq(place, normed_part))
        grad_tokens = back_middle + back_x
        gains = lax.psum_scatter(
            jnp.stack([grad_norm_gain, grad_mlp_gain]), BOTH, scatter_dimension=1, tiled=True
        )
        totals = [sum_dp(place, a) for a in parts]
        output_sum, gates_sum = (turned(place, totals[i], True) for i in (0, 2))
        branch_sum, inner_sum = (
            jnp.swapaxes(
                lax.all_to_all(totals[i].reshape(n_seq, d_rows, -1), "seq", 0, 0, tiled=True), 0, 1
            ).reshape(d_rows, rec)
            for i in (1, 3)
        )
    down_sum = down_sum.reshape(-1, width // n_dp)
    grad_output, grad_branch, gates_sum, grad_inner, grad_down, grad_gate, grad_up = (
        a.astype(F32) for a in (output_sum, branch_sum, gates_sum, inner_sum, down_sum, gate_sum, up_sum)
    )
    grad_rate = gates_sum[:, :BLOCK]
    grad_entry = gates_sum[:, BLOCK : 2 * BLOCK]
    vec_sum = gates_sum[:, 2 * BLOCK :]

    return (
        result,
        grad_tokens,
        grad_branch,
        grad_inner,
        grad_output,
        grad_rate,
        grad_entry,
        vec_sum[:, WIDTH + 1],
        vec_sum[:, WIDTH + 2],
        vec_sum[:, :WIDTH].T,
        vec_sum[:, WIDTH],
        vec_sum[:, WIDTH + 3],
        gains[0],
        gains[1],
        grad_gate,
        grad_up,
        grad_down,
    )


def solution(mesh):
    rows, flat = P(BOTH, None), P(BOTH)
    in_specs = (
        rows, P("dp", None), rows, rows, rows, rows, rows, flat, flat, P(None, BOTH), flat, flat, flat, flat,
        P(None, "seq"), P(None, "seq"), P("seq", None), rows,
    )
    out_specs = (
        rows, rows, rows, rows, rows, rows, rows, flat, flat, P(None, BOTH), flat, flat, flat, flat,
        P("dp", "seq"), P("dp", "seq"), P("seq", "dp"),
    )
    return jax.shard_map(shards, mesh=mesh, in_specs=in_specs, out_specs=out_specs, check_vma=False)
```

time: 2470 us -> 690 us (0.28)
  waiting for transfers between devices: 1490 us -> 1.15 us
  Pallas kernels: 0 us -> 615 us
  local copies, waits for them, and re-layouts: 458 us -> 25.7 us
  matrix products: 207 us -> 9.2 us
  blocking collectives: 131 us -> 0 us
  other arithmetic: 144 us -> 18.8 us
    reduce_scatter x10 -> x0, waiting for transfers between devices: 1340 us -> none  [the longest x1 257 us: shards(): lax.psum_scatter(grad_output_part, ('dp', 'seq'), scatter_dimension=0, ti...]
    pallas_call x0 -> x12, Pallas kernels: none -> 615 us  [the longest x1 152 us: weight_sums(): pl.pallas_call(partial(weight_sums_kernel, cuts), in_specs=[kept] + [vmem...]
    slice x114 -> x11, local copies, waits for them, and re-layouts: 263 us -> 10.7 us  [the longest x1 1.85 us: shards(): w_out = out_all[:, :width]]
    dot_general x24 -> x7, matrix products: 207 us -> 9.2 us  [the longest x1 7.12 us: contract_cols(): lax.dot_general(left, right, (((1,), (1,)), ((), ())), preferred_element_...]
    all_gather x7 -> x0, waiting for transfers between devices: 145 us -> none  [the longest x1 50.6 us: shards(): lax.all_gather(sharded[4], ('dp', 'seq'), axis=0, tiled=True)]
    pad x56 -> x2, local copies, waits for them, and re-layouts: 112 us -> 0.62 us  [the longest x1 0.61 us: shards(): gate_vec = jnp.pad(vec[WIDTH + 1:], ((0, 9 - 2 * WIDTH + WIDTH), (0, 0)))]
    unnamed x2 -> x0, blocking collectives: 83.3 us -> none
    add x50 -> x0, other arithmetic: 57.9 us -> none  [the longest x16 23.6 us: shards(): lax.associative_scan(combine, (following, back_states), reverse=True)]
  transfers between devices with their start and end apart: 20 -> 4, of which waited for: 16 -> 1; matrix products, arithmetic and copies ran while one was open for 17% -> 2% of each run, Pallas kernels for 0% -> 5%
where the time goes in v1:
time: 690 us; the launch traced here: 679 us
  Pallas kernels  615 us (89%)
  local copies, waits for them, and re-layouts  25.7 us (4%)
  other arithmetic  18.8 us (3%)
  matrix products  9.2 us (1%)
  starting transfers between devices  7.91 us (1%)
    pallas_call x1, Pallas kernels, weight_sums(): pl.pallas_call(partial(weight_sums_kernel, cuts), in_specs=[kept] + [vmem...  152 us
    pallas_call x1, Pallas kernels, sum_back_middle(): pl.pallas_call(partial(back_middle_kernel, cuts), in_specs=[kept, kept] +...  127 us
    pallas_call x1, Pallas kernels, gather_all(): pl.pallas_call(gather_kernel, in_specs=[pl.BlockSpec(memory_space=pltpu.V...  115 us
    pallas_call x1, Pallas kernels, sum_middle(): pl.pallas_call(middle_kernel, in_specs=[vmem, vmem, vmem, vmem, kept, kep...  70 us
    pallas_call x1, Pallas kernels, mlp_products(): pl.pallas_call(mlp_kernel, grid_spec=pltpu.PrefetchScalarGridSpec(num_sca...  46.9 us
    pallas_call x4, Pallas kernels, by_block(): pl.pallas_call(kernel, grid_spec=pltpu.PrefetchScalarGridSpec(num_scalar_...  44.5 us
    pallas_call x1, Pallas kernels, mlp_grads(): pl.pallas_call(mlp_grads_kernel, grid=(width // tile,), in_specs=[columns...  26.6 us
    pallas_call x1, Pallas kernels, exit_products(): pl.pallas_call(exit_kernel, grid=(width // tile,), in_specs=[columns, col...  21.3 us
  transfers between devices with their start and end apart: 4, of which 1 were waited for; matrix products, arithmetic and copies ran while one was open for 2% of the time, Pallas kernels for 5%

profile of v1, /device:TPU:19, one launch (start us, length us, event | category | flops | bytes accessed | tf_op | source)
XLA Modules:
  0.0 679.2 jit_solution(325792530676284404)
XLA Ops:
  5.3 114.8 %gather_all.1 = (bf16[8,4,64,1408]{3,2,1,0:T(8,128)(2,1)}, bf16[8,80,2688]{2,1,0:T(8,128)(2,1)}, bf16[4,256,2048]{2,1,0:T(8,128)(2,1)}, bf16[2,256,2048]{2,1,0:T(8,128)(2,1)}, bf16[2,256,2048]{2,1,0:T(8,128)(2,1)}) custom-call(bf16[4,64,1408]{2,1,0:T(8,128)(2,1)} %pad_maximum_fusion.in_pack, bf16[80,2688]{1,0:T(8,128)(2,1)} %fusion.27.out_pack, ...), custom_call_target="tpu_custom_call" | custom-call | tf_op jit(solution)/shard_map/gather_all/pallas_call | solution.py:749
  120.1 1.6 slice_select_fusion
  121.7 5.5 collective-permute-start.2
  130.3 12.4 %entry_products.1 = (bf16[1024,2048]{1,0:T(8,128)(2,1)}, f32[1024,640]{1,0:T(8,128)}, bf16[1024,640]{1,0:T(8,128)(2,1)}, f32[8,2048]{1,0:T(8,128)}) custom-call(bf16[1024,2048]{1,0:T(8,128)(2,1)} %bitcast.87, bf16[2048,1408]{1,0:T(8,128)(2,1)} %bitcast.85), custom_call_target="tpu_custom_call" | custom-call | flops 5368709120 | bytes 18087936 | tf_op jit(solution)/shard_map/entry_products/pallas_call | solution.py:1552
  142.7 6.2 shard_map.305
  149.0 1.7 constant_dynamic-slice_fusion.2
  151.8 1.8 slice.154.w_out
  153.6 1.5 fusion.32
  155.8 1.6 maximum_select_fusion
  158.4 1.7 constant_dynamic-update-slice_fusion.1.block_ref.conv_ref
  160.0 12.3 %shard_map.306 = (f32[1024,640]{1,0:T(8,128)}, bf16[1024,640]{1,0:T(8,128)(2,1)}) custom-call(s32[1]{0:T(128)} %bitcast.1.first_ref, bf16[1024,768]{1,0:T(8,128)(2,1)} %constant_dynamic-update-slice_fusion.1.block_ref.conv_ref, bf16[768,256]{1,0:T(8,128)(2,1)} %get-tuple-element.186.w_rate_ref, bf16[768,256]{1,0:T(8,128)(2,1)} %get-tuple-element.185.w_entry_ref, ...), custom_call_target="tpu_custom_call" | custom-call | flops 39321600 | bytes 13156352 | tf_op jit(solution)/shard_map/pallas_call | solution.py:486
  173.5 70.0 %sum_middle.1 = (f32[256,2048]{1,0:T(8,128)}, bf16[2,2,2,256,2048]{4,3,2,1,0:T(8,128)(2,1)}, bf16[2,2,2,256,2048]{4,3,2,1,0:T(8,128)(2,1)}) custom-call(bf16[4,256,640]{2,1,0:T(8,128)(2,1)} %bitcast.72, bf16[640,2048]{1,0:T(8,128)(2,1)} %slice.154.w_out, bf16[256,2048]{1,0:T(8,128)(2,1)} %refs_1_.1, f32[1,2048]{1,0:T(1,128)} %get-tuple-element.190.gain.refs_4_, ...), custom_call_target="tpu_custom_call" | custom-call | tf_op jit(solution)/shard_map/sum_middle/pallas_call | solution.py:895
  243.6 46.9 %mlp_products.1 = (bf16[2048,768]{1,0:T(8,128)(2,1)}, bf16[2048,768]{1,0:T(8,128)(2,1)}, bf16[2048,768]{1,0:T(8,128)(2,1)}, bf16[2048,2048]{1,0:T(8,128)(2,1)}, bf16[2048,2048]{1,0:T(8,128)(2,1)}) custom-call(s32[1]{0:T(128)} %bitcast.p_ref, bf16[2048,2048]{1,0:T(8,128)(2,1)} %bitcast.81, bf16[2048,2048]{1,0:T(8,128)(2,1)} %bitcast.83, ...), custom_call_target="tpu_custom_call" | custom-call | flops 38654705664 | bytes 42991616 | tf_op jit(solution)/shard_map/mlp_products/pallas_call | solution.py:1595
  290.5 26.6 %mlp_grads.1 = (bf16[768,2048]{1,0:T(8,128)(2,1)}, bf16[2048,768]{1,0:T(8,128)(2,1)}, bf16[2048,768]{1,0:T(8,128)(2,1)}) custom-call(bf16[2048,2048]{1,0:T(8,128)(2,1)} %bitcast.82, bf16[2048,2048]{1,0:T(8,128)(2,1)} %bitcast.84, bf16[2048,768]{1,0:T(8,128)(2,1)} %get-tuple-element.80.hidden_ref, bf16[2048,768]{1,0:T(8,128)(2,1)} %get-tuple-element.81.back_gate_ref, ...), custom_call_target="tpu_custom_call" | custom-call | flops 19327352832 | bytes 35651584 | tf_op jit(solution)/shard_map/mlp_grads/pallas_call | solution.py:1627
  317.1 127.0 %sum_back_middle.1 = (f32[256,2048]{1,0:T(8,128)}, bf16[4,256,2048]{2,1,0:T(8,128)(2,1)}, f32[1,2048]{1,0:T(1,128)}, bf16[256,2048]{1,0:T(8,128)(2,1)}, bf16[2,7...) custom-call(bf16[2,2,2,256,2048]{4,3,2,1,0:T(8,128)(2,1)} %bitcast.59, bf16[2,2,2,256,2048]{4,3,2,1,0:T(8,128)(2,1)} %bitcast.58, ...), custom_call_target="tpu_custom_call" | custom-call | tf_op jit(solution)/shard_map/sum_back_middle/pallas_call | solution.py:1504
  444.1 7.1 %fusion.28.back_ref = f32[1024,640]{1,0:T(8,128)} fusion(bf16[1024,2048]{1,0:T(8,128)(2,1)} %bitcast.88, bf16[640,2688]{1,0:T(8,128)(2,1)S(1)} %bitcast.65), kind=kOutput, calls=%fused_computation.66 | convolution fusion | flops 2684354560 | bytes 9437184 | tf_op jit(solution)/shard_map/dot_general | solution.py:33
  451.2 16.4 %shard_map.307 = (bf16[1024,640]{1,0:T(8,128)(2,1)}, bf16[2,1024,768]{2,1,0:T(8,128)(2,1)}, f32[1024,640]{1,0:T(8,128)}, f32[8,640]{1,0:T(8,128)}) custom-call(s32[1]{0:T(128)} %bitcast.1.first_ref, bf16[1024,768]{1,0:T(8,128)(2,1)} %constant_dynamic-update-slice_fusion.1.block_ref.conv_ref, bf16[768,256]{1,0:T(8,128)(2,1)} %get-tuple-element.186.w_rate_ref, ...), custom_call_target="tpu_custom_call" | custom-call | flops 39321600 | bytes 23642112 | tf_op jit(solution)/shard_map/pallas_call | solution.py:486
  469.6 2.2 collective-permute-start.3
  474.7 1.4 copy-done.2
  479.2 9.5 %shard_map.308 = (bf16[1024,640]{1,0:T(8,128)(2,1)}, f32[8,640]{1,0:T(8,128)}) custom-call(s32[1]{0:T(128)} %bitcast.1.first_ref, bf16[2,1024,768]{2,1,0:T(8,128)(2,1)} %copy-done.2, bf16[768,256]{1,0:T(8,128)(2,1)} %get-tuple-element.186.w_rate_ref, bf16[768,256]{1,0:T(8,128)(2,1)} %get-tuple-element.185.w_entry_ref, ...), custom_call_target="tpu_custom_call" | custom-call | flops 39321600 | bytes 15777792 | tf_op jit(solution)/shard_map/pallas_call | solution.py:486
  489.6 21.3 %exit_products.1 = (bf16[2048,640]{1,0:T(8,128)(2,1)}, bf16[2048,640]{1,0:T(8,128)(2,1)}, bf16[640,2048]{1,0:T(8,128)(2,1)}, bf16[1024,2048]{1,0:T(8,128)(2,1)}) custom-call(bf16[1024,2048]{1,0:T(8,128)(2,1)} %get-tuple-element.86.normed_ref, bf16[1024,2048]{1,0:T(8,128)(2,1)} %bitcast.89, bf16[2048,1408]{1,0:T(8,128)(2,1)} %bitcast.86, ...), custom_call_target="tpu_custom_call" | custom-call | flops 13421772800 | bytes 32243712 | tf_op jit(solution)/shard_map/exit_products/pallas_call | solution.py:1661
  513.8 151.6 %weight_sums.1 = (f32[256,2048]{1,0:T(8,128)}, f32[8,2048]{1,0:T(8,128)}, bf16[256,1536]{1,0:T(8,128)(2,1)}, bf16[80,2048]{1,0:T(8,128)(2,1)}, bf16[64,2560]{1,0...) custom-call(bf16[4,256,2048]{2,1,0:T(8,128)(2,1)} %bitcast.60, bf16[256,2048]{1,0:T(8,128)(2,1)} %refs_1_.1, ...), custom_call_target="tpu_custom_call" | custom-call | tf_op jit(solution)/shard_map/weight_sums/pallas_call | solution.py:1299
  665.4 1.5 fusion.31
  670.7 1.9 convert_element_type.44
  (89 shorter events, 33.2 us)
Async XLA Ops:
  0.7 3.8 copy-start.12
  0.7 3.8 copy-start.13
  0.7 3.8 copy-start.9
  5.3 122.8 %copy-start.15 = (s32[1,4]{1,0:T(1,128)S(1)}, s32[1,4]{1,0:T(1,128)}, u32[]{:S(2)}) copy-start(s32[1,4]{1,0:T(1,128)} %param.19) | copy-start | bytes 52
  5.3 123.1 %copy-start.14 = (pred[8]{0:T(512)(128)(4,1)S(1)}, pred[8]{0:T(512)(128)(4,1)}, u32[]{:S(2)}) copy-start(pred[8]{0:T(512)(128)(4,1)} %constant.78.clone.1) | copy-start | bytes 28
  121.7 34.1 %collective-permute-start.1 = (bf16[128,512]{1,0:T(8,128)(2,1)}, bf16[128,512]{1,0:T(8,128)(2,1)}, u32[]{:S(2)}, u32[]{:S(2)}) collective-permute-start(bf16[128,512]{1,0:T(8,128)(2,1)} %slice_select_fusion), channel_id=1, source_target_pairs={{0,1},{1,0},{2,3},{3,2},{4,5},{5,4},{6,7},{7,6},{8,9},{9,8},{10,11... | collective-permute-start | bytes 393224 | tf_op jit(solution)/shard_map/ppermute | solution.py:50
  121.7 51.8 %collective-permute-start.2 = (bf16[2,256,2048]{2,1,0:T(8,128)(2,1)}, bf16[2,256,2048]{2,1,0:T(8,128)(2,1)}, u32[]{:S(2)}, u32[]{:S(2)}) collective-permute-start(bf16[2,256,2048]{2,1,0:T(8,128)(2,1)} %get-tuple-element.70.cot_c), channel_id=1, source_target_pairs={{0,4},{4,0},{8,12},{12,8},{16,20},{20,16},{24,28},{28,24},{1,5},{5... | collective-permute-start | bytes 6291464 | tf_op jit(solution)/shard_map/ppermute | solution.py:53
  142.7 8.2 %copy-start.3 = (bf16[8,80,2688]{2,1,0:T(8,128)(2,1)S(1)}, bf16[8,80,2688]{2,1,0:T(8,128)(2,1)}, u32[]{:S(2)}) copy-start(bf16[8,80,2688]{2,1,0:T(8,128)(2,1)} %get-tuple-element.67) | copy-start | bytes 10321924
  150.6 7.8 %collective-permute-start = (bf16[1024,128]{1,0:T(8,128)(2,1)}, bf16[1024,128]{1,0:T(8,128)(2,1)}, u32[]{:S(2)}, u32[]{:S(2)}) collective-permute-start(bf16[1024,128]{1,0:T(8,128)(2,1)} %constant_dynamic-slice_fusion.2), channel_id=1, source_target_pairs={{0,1},{1,0},{2,3},{3,2},{4,5},{5,4},{6,7},{7,6},{8,9},{9,8},{10,11... | collective-permute-start | bytes 786440 | tf_op jit(solution)/shard_map/ppermute | solution.py:50
  451.2 20.5 %copy-start.8 = (bf16[256,1536]{1,0:T(8,128)(2,1)S(1)}, bf16[256,1536]{1,0:T(8,128)(2,1)}, u32[]{:S(2)}) copy-start(bf16[256,1536]{1,0:T(8,128)(2,1)} %get-tuple-element.108) | copy-start | bytes 2359300
  468.4 4.7 copy-start.7
  469.6 4.8 collective-permute-start.3
  471.7 2.6 copy-start.1
  474.5 1.7 copy-start.2
  474.5 2.5 copy-start
  665.4 7.2 %copy-start.11 = (bf16[64,2560]{1,0:T(8,128)(2,1)S(1)}, bf16[64,2560]{1,0:T(8,128)(2,1)}, u32[]{:S(2)}) copy-start(bf16[64,2560]{1,0:T(8,128)(2,1)} %get-tuple-element.104) | copy-start | bytes 983044
  665.4 8.1 %copy-start.10 = (bf16[80,2048]{1,0:T(8,128)(2,1)S(1)}, bf16[80,2048]{1,0:T(8,128)(2,1)}, u32[]{:S(2)}) copy-start(bf16[80,2048]{1,0:T(8,128)(2,1)} %get-tuple-element.105) | copy-start | bytes 983044
  667.9 6.5 copy-start.6
  673.5 2.2 copy-start.5
  675.7 2.0 copy-start.4

commit v2 on v1

--- a/solution.py
+++ b/solution.py
@@ -316,6 +316,19 @@
 
 def tile_sum(a):
     return jnp.sum(a.reshape(-1, TILE, a.shape[1]), axis=0)
+
+
+def mlp_tile(x, cot, gate_weight, up_weight, down_weight):
+    gate_pre = dot(x, gate_weight)
+    up_pre = dot(x, up_weight)
+    back_hidden = contract_cols(cot, down_weight)
+    value, slope = gelu_parts(gate_pre)
+    hidden = (value * up_pre).astype(BF16)
+    back_gate = (back_hidden * up_pre * slope).astype(BF16)
+    back_up = (back_hidden * value).astype(BF16)
+    down = dot(hidden, down_weight).astype(BF16)
+    back = (contract_cols(back_gate, gate_weight) + contract_cols(back_up, up_weight)).astype(BF16)
+    return hidden, back_gate, back_up, down, back
 
 
 def conv_kernel(inner_ref, taps_ref, offset_ref, conv_ref):
@@ -802,29 +815,38 @@
 
 
 def middle_kernel(
-    mixed, w_out, tok, gain, cot_c, cot_o, away, middle, rows, pair_cot,
-    part, from_core, to_x, from_x, normed, send, recv, local,
-    cots_here, cot_send, cot_recv, cot_local,
+    mixed, w_out, tok, gain, cot_c, cot_o, away, gate_weight, up_weight, down_weight,
+    middle, rows, pair_cot, hidden, back_gate, back_up, down_part, back_part,
+    part, from_core, to_x, from_x, rows_here, cots_here, w_gate, w_up, w_down, units, wides,
+    send, recv, cot_send, cot_recv, load_sem, keep_sem, out_sem,
 ):
     near = Near()
-    x, c, seq = near.x, near.c, near.seq
+    p, x, c, seq = near.p, near.x, near.c, near.seq
     ch = Chunks((send, recv), tok.shape[0])
     all_chunks = range(CHUNKS)
     seq_x, seq_c = seq + 2 - 4 * x, seq + 1 - 2 * c
     seq_cx = seq_c + 2 - 4 * x
+    count = units.shape[-1]
+    half = pl.ds(pl.multiple_of(p * count, count), count)
     loads = [
-        pltpu.make_async_copy(source, cots_here.at[n], cot_local.at[n]) for n, source in enumerate((cot_c, cot_o, away))
+        pltpu.make_async_copy(source, target, load_sem.at[n])
+        for n, (source, target) in enumerate(
+            (
+                (cot_c, cots_here.at[pl.ds(0, 2)]),
+                (cot_o, cots_here.at[pl.ds(2, 2)]),
+                (away, cots_here.at[pl.ds(4, 2)]),
+                (gate_weight.at[:, half], w_gate),
+                (up_weight.at[:, half], w_up),
+                (down_weight.at[half], w_down),
+            )
+        )
     ]
     for load in loads:
         load.start()
     greet([near.core, near.over_x, near.over_y])
-    far_cot = remote(cots_here.at[2], pair_cot.at[1, 1], (cot_send, cot_recv), 0, near.core)
-    cots = [
-        pltpu.make_async_copy(cots_here.at[n], pair_cot.at[i], cot_local.at[n])
-        for n, i in enumerate(((0, 0), (0, 1), (1, 0)))
-    ]
     CORE_FAR, CORE_NEAR, SUM_X, OWN_X, OWN_Y, OWN_C, FWD_X, FWD_Y, FWD_C = 0, 1, 2, 3, 4, 5, 6, 7, 8
     FWD_C2, FWD_C3 = 9, 10
+    OWN, X, C, CX, Y, XY, CY, CXY = range(8)
 
     for group, slot, at in ((CORE_FAR, 0, seq_cx), (CORE_NEAR, 1, seq_c)):
         part[at, :, :] = dot(mixed[at], w_out[...]).astype(BF16)
@@ -840,10 +862,8 @@
         ch.go(SUM_X, i, to_x.at[r], from_x.at[r], near.over_x)
     for load in loads:
         load.wait()
+    far_cot = remote(cots_here.at[pl.ds(Y, 2)], cots_here.at[pl.ds(CY, 2)], (cot_send, cot_recv), 0, near.core)
     far_cot.start()
-    for copy in cots:
-        copy.start()
-    kept = []
     for i in all_chunks:
         r = ch.rows(i)
         ch.arrived(CORE_NEAR, i, from_core.at[1, r], near.core)
@@ -853,73 +873,123 @@
         )
         middle[r, :] = total
         scale = lax.rsqrt(jnp.mean(total * total, axis=-1, keepdims=True) + EPSILON)
-        normed[r, :] = (total * scale * gain[...]).astype(BF16)
-        ch.go(OWN_X, i, normed.at[r], rows.at[0, 0, 1, r], near.over_x)
-        ch.go(OWN_Y, i, normed.at[r], rows.at[1, 0, 0, r], near.over_y)
-        ch.go(OWN_C, i, normed.at[r], rows.at[0, 1, 0, r], near.core)
-        keep = pltpu.make_async_copy(normed.at[r], rows.at[0, 0, 0, r], local.at[i])
-        keep.start()
-        kept.append(keep)
+        rows_here[OWN, r, :] = (total * scale * gain[...]).astype(BF16)
+        own = rows_here.at[OWN, r]
+        ch.go(OWN_X, i, own, rows_here.at[X, r], near.over_x)
+        ch.go(OWN_Y, i, own, rows_here.at[Y, r], near.over_y)
+        ch.go(OWN_C, i, own, rows_here.at[C, r], near.core)
+    keeps = []
+
+    def keep(*slots):
+        for slot in slots:
+            copy = pltpu.make_async_copy(rows_here.at[slot], rows.at[slot], keep_sem.at[slot])
+            copy.start()
+            keeps.append(copy)
+
+    def stored(n, slot):
+        whole = [(units.at[n, i], ref.at[slot]) for i, ref in enumerate((hidden, back_gate, back_up))]
+        whole += [(wides.at[n, i], ref.at[slot]) for i, ref in enumerate((down_part, back_part))]
+        return [pltpu.make_async_copy(here, there, out_sem.at[n, i]) for i, (here, there) in enumerate(whole)]
+
+    def products(first, second, before):
+        def one(n, carry):
+            slot = first + (second - first) * n
+            if before is not None:
+                for copy in stored(n, before[0] + (before[1] - before[0]) * n):
+                    copy.wait()
+            results = mlp_tile(rows_here[slot], cots_here[slot], w_gate[...], w_up[...], w_down[...])
+            for i in range(3):
+                units[n, i, :, :] = results[i]
+            for i in range(2):
+                wides[n, i, :, :] = results[3 + i]
+            for copy in stored(n, slot):
+                copy.start()
+            return carry
+
+        lax.fori_loop(0, 2, one, 0)
+
+    def core_arrived(group, slot):
+        for i in all_chunks:
+            ch.arrived(group, i, rows_here.at[slot, ch.rows(i)], near.core)
+
+    core_arrived(OWN_C, C)
+    keep(OWN, C)
+    products(OWN, C, None)
     for i in all_chunks:
         r = ch.rows(i)
-        here = rows.at[0, 0, 1, r]
+        here = rows_here.at[X, r]
         ch.arrived(OWN_X, i, here, near.over_x)
         if i >= CHUNKS // 2:
-            ch.go(FWD_Y, i, here, rows.at[1, 0, 1, r], near.over_y)
-        ch.go(FWD_C, i, here, rows.at[0, 1, 1, r], near.core)
-        here = rows.at[1, 0, 0, r]
+            ch.go(FWD_Y, i, here, rows_here.at[XY, r], near.over_y)
+        ch.go(FWD_C, i, here, rows_here.at[CX, r], near.core)
+        here = rows_here.at[Y, r]
         ch.arrived(OWN_Y, i, here, near.over_y)
         if i < CHUNKS // 2:
-            ch.go(FWD_X, i, here, rows.at[1, 0, 1, r], near.over_x)
-        ch.go(FWD_C2, i, here, rows.at[1, 1, 0, r], near.core)
+            ch.go(FWD_X, i, here, rows_here.at[XY, r], near.over_x)
+        ch.go(FWD_C2, i, here, rows_here.at[CY, r], near.core)
+    keep(X, Y)
+    products(X, Y, (OWN, C))
     for i in all_chunks:
         r = ch.rows(i)
-        here = rows.at[1, 0, 1, r]
+        here = rows_here.at[XY, r]
         if i < CHUNKS // 2:
             ch.arrived(FWD_X, i, here, near.over_x)
         else:
             ch.arrived(FWD_Y, i, here, near.over_y)
-        ch.go(FWD_C3, i, here, rows.at[1, 1, 1, r], near.core)
-    for group, at in ((OWN_C, (0, 0)), (FWD_C, (0, 1)), (FWD_C2, (1, 0)), (FWD_C3, (1, 1))):
-        for i in all_chunks:
-            ch.arrived(group, i, rows.at[at[0], 1, at[1], ch.rows(i)], near.core)
-    for keep in kept + cots:
-        keep.wait()
+        ch.go(FWD_C3, i, here, rows_here.at[CXY, r], near.core)
+    core_arrived(FWD_C, CX)
+    core_arrived(FWD_C2, CY)
     far_cot.wait()
+    cots = pltpu.make_async_copy(cots_here, pair_cot, load_sem.at[0])
+    cots.start()
+    keep(CX, CY, XY)
+    products(CX, CY, (X, Y))
+    core_arrived(FWD_C3, CXY)
+    keep(CXY)
+    products(XY, CXY, (CX, CY))
+    for n, slot in enumerate((XY, CXY)):
+        for copy in stored(n, slot):
+            copy.wait()
+    for copy in keeps + [cots]:
+        copy.wait()
     ch.finish()
 
 
-def sum_middle(place, mixed, w_out, tok, gain, cot_c, cot_o, away):
+def sum_middle(place, mixed, w_out, tok, gain, cot_c, cot_o, away, gate_weight, up_weight, down_weight):
     count, width = tok.shape
+    units = gate_weight.shape[1] // 2
     vmem, kept = pl.BlockSpec(memory_space=pltpu.VMEM), pl.BlockSpec(memory_space=pl.ANY)
+    wide, narrow = (jax.ShapeDtypeStruct((8, count, cols), BF16) for cols in (width, units))
     return pl.pallas_call(
         middle_kernel,
-        in_specs=[vmem, vmem, vmem, vmem, kept, kept, kept],
-        out_specs=[vmem, kept, kept],
-        out_shape=[
-            jax.ShapeDtypeStruct((count, width), F32),
-            jax.ShapeDtypeStruct((2, 2, 2, count, width), BF16),
-            jax.ShapeDtypeStruct((2, 2, 2, count, width), BF16),
-        ],
+        in_specs=[vmem] * 4 + [kept] * 6,
+        out_specs=[vmem] + [kept] * 7,
+        out_shape=[jax.ShapeDtypeStruct((count, width), F32), wide, wide, narrow, narrow, narrow, wide, wide],
         scratch_shapes=[
             pltpu.VMEM((place.n_seq, count, width), BF16),
             pltpu.VMEM((2, count, width), BF16),
             pltpu.VMEM((count, width), BF16),
             pltpu.VMEM((count, width), BF16),
-            pltpu.VMEM((count, width), BF16),
+            pltpu.VMEM((8, count, width), BF16),
+            pltpu.VMEM((8, count, width), BF16),
+            pltpu.VMEM((width, units), BF16),
+            pltpu.VMEM((width, units), BF16),
+            pltpu.VMEM((units, width), BF16),
+            pltpu.VMEM((2, 3, count, units), BF16),
+            pltpu.VMEM((2, 2, count, width), BF16),
             pltpu.SemaphoreType.DMA((11 * CHUNKS,)),
             pltpu.SemaphoreType.DMA((11 * CHUNKS,)),
-            pltpu.SemaphoreType.DMA((CHUNKS,)),
-            pltpu.VMEM((3,) + cot_c.shape, BF16),
             pltpu.SemaphoreType.DMA((1,)),
             pltpu.SemaphoreType.DMA((1,)),
-            pltpu.SemaphoreType.DMA((3,)),
+            pltpu.SemaphoreType.DMA((6,)),
+            pltpu.SemaphoreType.DMA((8,)),
+            pltpu.SemaphoreType.DMA((2, 5)),
         ],
         compiler_params=pltpu.CompilerParams(
             collective_id=1, has_side_effects=True, vmem_limit_bytes=VMEM_BYTES
         ),
         name="sum_middle",
-    )(mixed.reshape(place.n_seq, count, -1), w_out, tok, gain, cot_c, cot_o, away)
+    )(mixed.reshape(place.n_seq, count, -1), w_out, tok, gain, cot_c, cot_o, away, gate_weight, up_weight, down_weight)
 
 
 class Piece:
@@ -935,7 +1005,7 @@
         return ref.at[block, self.rows]
 
     def read(self, ref, block):
-        return ref[block, self.rows, :].astype(F32)
+        return ref[block, self.rows, :]
 
     def columns(self, block, width):
         return pl.ds(block * width if isinstance(block, int) else pl.multiple_of(block * width, width), width)
@@ -1005,7 +1075,7 @@
         for block in range(self.near.n_q):
             self.y_copy(n, block).wait_recv()
             total = piece.read(piece.part, 2 * block + self.near.p) + piece.read(piece.over, block)
-            piece.pair[block, piece.rows, :] = total.astype(BF16)
+            piece.pair[block, piece.rows, :] = total
 
     def z_step(self, n, k):
         piece, q, n_q = self.pieces[n], self.near.q, self.near.n_q
@@ -1019,8 +1089,8 @@
 
                     def add():
                         self.z_copy(n, k - 1, way, True).wait_recv()
-                        total = piece.read(side, k - 2) + piece.pair_value(block).astype(F32)
-                        side[k - 2, piece.rows, :] = total.astype(BF16)
+                        total = piece.read(side, k - 2) + piece.pair_value(block)
+                        side[k - 2, piece.rows, :] = total
 
                     def begin():
                         side[k - 2, piece.rows, :] = piece.pair_value(block)
@@ -1085,8 +1155,7 @@
 
         def add(way):
             self.z_copy(n, k, way, True).wait_recv()
-            total = piece.low[piece.rows, :].astype(F32) + piece.read(piece.side(way), k - 1)
-            piece.low[piece.rows, :] = total.astype(BF16)
+            piece.low[piece.rows, :] = piece.low[piece.rows, :] + piece.read(piece.side(way), k - 1)
 
         pl.when(self.below)(lambda: add(1))
         pl.when(self.above)(lambda: add(-1))
@@ -1568,22 +1637,10 @@
     )(x, weights)
 
 
-def mlp_kernel(
-    p_ref, x_ref, cot_ref, gate_ref, up_ref, down_ref, hidden_ref, back_gate_ref, back_up_ref, down_part_ref, back_ref
-):
-    x = x_ref[...]
-    gate_pre = dot(x, gate_ref[...])
-    up_pre = dot(x, up_ref[...])
-    back_hidden = contract_cols(cot_ref[...], down_ref[...])
-    value, slope = gelu_parts(gate_pre)
-    hidden = (value * up_pre).astype(BF16)
-    back_gate = (back_hidden * up_pre * slope).astype(BF16)
-    back_up = (back_hidden * value).astype(BF16)
-    hidden_ref[...] = hidden
-    back_gate_ref[...] = back_gate
-    back_up_ref[...] = back_up
-    down_part_ref[...] = dot(hidden, down_ref[...]).astype(BF16)
-    back_ref[...] = (contract_cols(back_gate, gate_ref[...]) + contract_cols(back_up, up_ref[...])).astype(BF16)
+def mlp_kernel(p_ref, x_ref, cot_ref, gate_ref, up_ref, down_ref, *result_refs):
+    results = mlp_tile(x_ref[...], cot_ref[...], gate_ref[...], up_ref[...], down_ref[...])
+    for ref, value in zip(result_refs, results):
+        ref[...] = value
 
 
 def mlp_products(p, x, cot, gate_weight, up_weight, down_weight, tile):
@@ -1762,18 +1819,21 @@
     mixed, away = lax.optimization_barrier((mixed, away))
     whole_x = tokens.astype(F32)
     if fast:
-        middle, rows, pair_cot = sum_middle(place, mixed, w_out, tokens, gain_mid, cot_c, cot_o, away)
+        middle, rows, pair_cot, hidden, back_gate, back_up, down_part, back_part = sum_middle(
+            place, mixed, w_out, tokens, gain_mid, cot_c, cot_o, away, gate_weight, up_weight, down_weight
+        )
     else:
         out_part = dot(mixed, w_out).astype(BF16).reshape(n_seq, tok, width)
         middle = whole_x + scatter_seq(place, out_part)
         rows = gather_plane(place, rms_norm(middle, gain_mid).astype(BF16))
         pair_cot = jnp.stack([jnp.where(place.p == 0, group_c, away), jnp.where(place.p == 0, away, group_c)])
-    rows, pair_cot = rows.reshape(2 * count, width), pair_cot.reshape(2 * count, width)
-
+        hidden, back_gate, back_up, down_part, back_part = mlp_products(
+            place.p.astype(jnp.int32)[None], rows.reshape(2 * count, width), pair_cot.reshape(2 * count, width),
+            gate_weight, up_weight, down_weight, MLP_TILE,
+        )
+    flat = lambda a: a.reshape(2 * count, -1)
+    rows, pair_cot, hidden, back_gate, back_up = (flat(a) for a in (rows, pair_cot, hidden, back_gate, back_up))
     units = gate_weight.shape[1] // 2
-    hidden, back_gate, back_up, down_part, back_part = mlp_products(
-        place.p.astype(jnp.int32)[None], rows, pair_cot, gate_weight, up_weight, down_weight, MLP_TILE
-    )
 
     n_q = place.n_q
     grad_down_part, grad_gate_part, grad_up_part = mlp_grads(rows, pair_cot, hidden, back_gate, back_up, GRAD_TILE)

time: 690 us -> 671 us (0.972)
  Pallas kernels: 615 us -> 596 us
    pallas_call x2 -> x1, Pallas kernels: 117 us -> 99.2 us  [sum_middle(): pl.pallas_call(middle_kernel, in_specs=[vmem] * 4 + [kept] * 6, out_specs...]
where the time goes in v2:
time: 671 us; the launch traced here: 661 us
  Pallas kernels  596 us (89%)
  local copies, waits for them, and re-layouts  25.6 us (4%)
  other arithmetic  18.9 us (3%)
  matrix products  9.21 us (1%)
  starting transfers between devices  9 us (1%)
    pallas_call x1, Pallas kernels, weight_sums(): pl.pallas_call(partial(weight_sums_kernel, cuts), in_specs=[kept] + [vmem...  153 us
    pallas_call x1, Pallas kernels, sum_back_middle(): pl.pallas_call(partial(back_middle_kernel, cuts), in_specs=[kept, kept] +...  124 us
    pallas_call x1, Pallas kernels, gather_all(): pl.pallas_call(gather_kernel, in_specs=[pl.BlockSpec(memory_space=pltpu.V...  115 us
    pallas_call x1, Pallas kernels, sum_middle(): pl.pallas_call(middle_kernel, in_specs=[vmem] * 4 + [kept] * 6, out_specs...  99.2 us
    pallas_call x4, Pallas kernels, by_block(): pl.pallas_call(kernel, grid_spec=pltpu.PrefetchScalarGridSpec(num_scalar_...  44.5 us
    pallas_call x1, Pallas kernels, mlp_grads(): pl.pallas_call(mlp_grads_kernel, grid=(width // tile,), in_specs=[columns...  26.3 us
    pallas_call x1, Pallas kernels, exit_products(): pl.pallas_call(exit_kernel, grid=(width // tile,), in_specs=[columns, col...  21.3 us
  transfers between devices with their start and end apart: 4, of which 1 were waited for; matrix products, arithmetic and copies ran while one was open for 2% of the time, Pallas kernels for 5%

profile of v2, /device:TPU:19, one launch (start us, length us, event | category | flops | bytes accessed | tf_op | source)
XLA Modules:
  0.0 661.0 jit_solution(18414785955708253202)
XLA Ops:
  5.3 114.8 %gather_all.1 = (bf16[8,4,64,1408]{3,2,1,0:T(8,128)(2,1)}, bf16[8,80,2688]{2,1,0:T(8,128)(2,1)}, bf16[4,256,2048]{2,1,0:T(8,128)(2,1)}, bf16[2,256,2048]{2,1,0:T(8,128)(2,1)}, bf16[2,256,2048]{2,1,0:T(8,128)(2,1)}) custom-call(bf16[4,64,1408]{2,1,0:T(8,128)(2,1)} %pad_maximum_fusion.in_pack, bf16[80,2688]{1,0:T(8,128)(2,1)} %fusion.27.out_pack, ...), custom_call_target="tpu_custom_call" | custom-call | tf_op jit(solution)/shard_map/gather_all/pallas_call | solution.py:762
  120.1 1.6 slice_select_fusion
  121.7 5.5 collective-permute-start.2
  130.3 12.4 %entry_products.1 = (bf16[1024,2048]{1,0:T(8,128)(2,1)}, f32[1024,640]{1,0:T(8,128)}, bf16[1024,640]{1,0:T(8,128)(2,1)}, f32[8,2048]{1,0:T(8,128)}) custom-call(bf16[1024,2048]{1,0:T(8,128)(2,1)} %bitcast.87, bf16[2048,1408]{1,0:T(8,128)(2,1)} %bitcast.85), custom_call_target="tpu_custom_call" | custom-call | flops 5368709120 | bytes 18087936 | tf_op jit(solution)/shard_map/entry_products/pallas_call | solution.py:1621
  142.7 6.2 shard_map.305
  149.0 1.7 constant_dynamic-slice_fusion.2
  151.8 1.8 slice.154.w_out
  153.6 1.5 fusion.32
  155.8 1.7 maximum_select_fusion
  158.4 1.7 constant_dynamic-update-slice_fusion.1.block_ref.conv_ref
  160.0 12.4 %shard_map.306 = (f32[1024,640]{1,0:T(8,128)}, bf16[1024,640]{1,0:T(8,128)(2,1)}) custom-call(s32[1]{0:T(128)} %bitcast.first_ref, bf16[1024,768]{1,0:T(8,128)(2,1)} %constant_dynamic-update-slice_fusion.1.block_ref.conv_ref, bf16[768,256]{1,0:T(8,128)(2,1)} %get-tuple-element.186.w_rate_ref, bf16[768,256]{1,0:T(8,128)(2,1)} %get-tuple-element.185.w_entry_ref, ...), custom_call_target="tpu_custom_call" | custom-call | flops 39321600 | bytes 13156352 | tf_op jit(solution)/shard_map/pallas_call | solution.py:499
  173.5 99.2 %sum_middle.1 = (f32[256,2048]{1,0:T(8,128)}, bf16[8,256,2048]{2,1,0:T(8,128)(2,1)}, bf16[8,256,2048]{2,1,0:T(8,128)(2,1)}, bf16[8,256,768]{2,1,0:T(8,128)(2,1)}...) custom-call(bf16[4,256,640]{2,1,0:T(8,128)(2,1)} %bitcast.74, ...), custom_call_target="tpu_custom_call" | custom-call | tf_op jit(solution)/shard_map/sum_middle/pallas_call | solution.py:963
  272.7 26.3 %mlp_grads.1 = (bf16[768,2048]{1,0:T(8,128)(2,1)}, bf16[2048,768]{1,0:T(8,128)(2,1)}, bf16[2048,768]{1,0:T(8,128)(2,1)}) custom-call(bf16[2048,2048]{1,0:T(8,128)(2,1)} %bitcast.83, bf16[2048,2048]{1,0:T(8,128)(2,1)} %bitcast.84, bf16[2048,768]{1,0:T(8,128)(2,1)} %bitcast.90, bf16[2048,768]{1,0:T(8,128)(2,1)} %bitcast.91, bf16[2048,768]{1,0:T(8,128)(2,1)} %bitcast.92), custom_call_target="tpu_custom_call" | custom-call | flops 19327352832 | bytes 35651584 | tf_op jit(solution)/shard_map/mlp_grads/pallas_call | solution.py:1684
  299.0 124.4 %sum_back_middle.1 = (f32[256,2048]{1,0:T(8,128)}, bf16[4,256,2048]{2,1,0:T(8,128)(2,1)}, f32[1,2048]{1,0:T(1,128)}, bf16[256,2048]{1,0:T(8,128)(2,1)}, bf16[2,7...) custom-call(bf16[2,2,2,256,2048]{4,3,2,1,0:T(8,128)(2,1)} %bitcast.61, bf16[2,2,2,256,2048]{4,3,2,1,0:T(8,128)(2,1)} %bitcast.60, ...), custom_call_target="tpu_custom_call" | custom-call | tf_op jit(solution)/shard_map/sum_back_middle/pallas_call | solution.py:1573
  423.4 7.1 %fusion.28.back_ref = f32[1024,640]{1,0:T(8,128)} fusion(bf16[1024,2048]{1,0:T(8,128)(2,1)} %bitcast.88, bf16[640,2688]{1,0:T(8,128)(2,1)S(1)} %bitcast.67), kind=kOutput, calls=%fused_computation.66 | convolution fusion | flops 2684354560 | bytes 9437184 | tf_op jit(solution)/shard_map/dot_general | solution.py:33
  430.6 16.4 %shard_map.307 = (bf16[1024,640]{1,0:T(8,128)(2,1)}, bf16[2,1024,768]{2,1,0:T(8,128)(2,1)}, f32[1024,640]{1,0:T(8,128)}, f32[8,640]{1,0:T(8,128)}) custom-call(s32[1]{0:T(128)} %bitcast.first_ref, bf16[1024,768]{1,0:T(8,128)(2,1)} %constant_dynamic-update-slice_fusion.1.block_ref.conv_ref, bf16[768,256]{1,0:T(8,128)(2,1)} %get-tuple-element.186.w_rate_ref, ...), custom_call_target="tpu_custom_call" | custom-call | flops 39321600 | bytes 23642112 | tf_op jit(solution)/shard_map/pallas_call | solution.py:499
  448.9 3.3 collective-permute-start.3
  452.2 1.3 convert_element_type.48
  455.2 1.4 copy-done.2
  459.6 9.5 %shard_map.308 = (bf16[1024,640]{1,0:T(8,128)(2,1)}, f32[8,640]{1,0:T(8,128)}) custom-call(s32[1]{0:T(128)} %bitcast.first_ref, bf16[2,1024,768]{2,1,0:T(8,128)(2,1)} %copy-done.2, bf16[768,256]{1,0:T(8,128)(2,1)} %get-tuple-element.186.w_rate_ref, bf16[768,256]{1,0:T(8,128)(2,1)} %get-tuple-element.185.w_entry_ref, ...), custom_call_target="tpu_custom_call" | custom-call | flops 39321600 | bytes 15777792 | tf_op jit(solution)/shard_map/pallas_call | solution.py:499
  470.0 21.3 %exit_products.1 = (bf16[2048,640]{1,0:T(8,128)(2,1)}, bf16[2048,640]{1,0:T(8,128)(2,1)}, bf16[640,2048]{1,0:T(8,128)(2,1)}, bf16[1024,2048]{1,0:T(8,128)(2,1)}) custom-call(bf16[1024,2048]{1,0:T(8,128)(2,1)} %get-tuple-element.86.normed_ref, bf16[1024,2048]{1,0:T(8,128)(2,1)} %bitcast.89, bf16[2048,1408]{1,0:T(8,128)(2,1)} %bitcast.86, ...), custom_call_target="tpu_custom_call" | custom-call | flops 13421772800 | bytes 32243712 | tf_op jit(solution)/shard_map/exit_products/pallas_call | solution.py:1718
  494.2 152.8 %weight_sums.1 = (f32[256,2048]{1,0:T(8,128)}, f32[8,2048]{1,0:T(8,128)}, bf16[256,1536]{1,0:T(8,128)(2,1)}, bf16[80,2048]{1,0:T(8,128)(2,1)}, bf16[64,2560]{1,0...) custom-call(bf16[4,256,2048]{2,1,0:T(8,128)(2,1)} %bitcast.62, bf16[256,2048]{1,0:T(8,128)(2,1)} %refs_1_.1, ...), custom_call_target="tpu_custom_call" | custom-call | tf_op jit(solution)/shard_map/weight_sums/pallas_call | solution.py:1368
  647.0 1.5 fusion.31
  652.3 1.9 convert_element_type.44
  (88 shorter events, 31.8 us)
Async XLA Ops:
  0.7 3.8 copy-start.12
  0.7 3.8 copy-start.13
  0.7 3.8 copy-start.9
  5.3 122.8 %copy-start.15 = (s32[1,4]{1,0:T(1,128)S(1)}, s32[1,4]{1,0:T(1,128)}, u32[]{:S(2)}) copy-start(s32[1,4]{1,0:T(1,128)} %param.19) | copy-start | bytes 52
  5.3 123.1 %copy-start.14 = (pred[8]{0:T(512)(128)(4,1)S(1)}, pred[8]{0:T(512)(128)(4,1)}, u32[]{:S(2)}) copy-start(pred[8]{0:T(512)(128)(4,1)} %constant.71.clone.1) | copy-start | bytes 28
  121.7 34.0 %collective-permute-start.1 = (bf16[128,512]{1,0:T(8,128)(2,1)}, bf16[128,512]{1,0:T(8,128)(2,1)}, u32[]{:S(2)}, u32[]{:S(2)}) collective-permute-start(bf16[128,512]{1,0:T(8,128)(2,1)} %slice_select_fusion), channel_id=1, source_target_pairs={{0,1},{1,0},{2,3},{3,2},{4,5},{5,4},{6,7},{7,6},{8,9},{9,8},{10,11... | collective-permute-start | bytes 393224 | tf_op jit(solution)/shard_map/ppermute | solution.py:50
  121.7 51.8 %collective-permute-start.2 = (bf16[2,256,2048]{2,1,0:T(8,128)(2,1)}, bf16[2,256,2048]{2,1,0:T(8,128)(2,1)}, u32[]{:S(2)}, u32[]{:S(2)}) collective-permute-start(bf16[2,256,2048]{2,1,0:T(8,128)(2,1)} %get-tuple-element.70.cot_c), channel_id=1, source_target_pairs={{0,4},{4,0},{8,12},{12,8},{16,20},{20,16},{24,28},{28,24},{1,5},{5... | collective-permute-start | bytes 6291464 | tf_op jit(solution)/shard_map/ppermute | solution.py:53
  142.7 8.2 %copy-start.3 = (bf16[8,80,2688]{2,1,0:T(8,128)(2,1)S(1)}, bf16[8,80,2688]{2,1,0:T(8,128)(2,1)}, u32[]{:S(2)}) copy-start(bf16[8,80,2688]{2,1,0:T(8,128)(2,1)} %get-tuple-element.67) | copy-start | bytes 10321924
  150.6 7.7 %collective-permute-start = (bf16[1024,128]{1,0:T(8,128)(2,1)}, bf16[1024,128]{1,0:T(8,128)(2,1)}, u32[]{:S(2)}, u32[]{:S(2)}) collective-permute-start(bf16[1024,128]{1,0:T(8,128)(2,1)} %constant_dynamic-slice_fusion.2), channel_id=1, source_target_pairs={{0,1},{1,0},{2,3},{3,2},{4,5},{5,4},{6,7},{7,6},{8,9},{9,8},{10,11... | collective-permute-start | bytes 786440 | tf_op jit(solution)/shard_map/ppermute | solution.py:50
  430.6 21.6 %copy-start.8 = (bf16[256,1536]{1,0:T(8,128)(2,1)S(1)}, bf16[256,1536]{1,0:T(8,128)(2,1)}, u32[]{:S(2)}) copy-start(bf16[256,1536]{1,0:T(8,128)(2,1)} %get-tuple-element.108) | copy-start | bytes 2359300
  447.7 5.8 copy-start.7
  448.9 5.9 collective-permute-start.3
  452.2 2.6 copy-start.1
  454.9 1.7 copy-start.2
  454.9 2.5 copy-start
  647.0 7.2 %copy-start.11 = (bf16[64,2560]{1,0:T(8,128)(2,1)S(1)}, bf16[64,2560]{1,0:T(8,128)(2,1)}, u32[]{:S(2)}) copy-start(bf16[64,2560]{1,0:T(8,128)(2,1)} %get-tuple-element.104) | copy-start | bytes 983044
  647.0 8.1 %copy-start.10 = (bf16[80,2048]{1,0:T(8,128)(2,1)S(1)}, bf16[80,2048]{1,0:T(8,128)(2,1)}, u32[]{:S(2)}) copy-start(bf16[80,2048]{1,0:T(8,128)(2,1)} %get-tuple-element.105) | copy-start | bytes 983044
  649.5 6.5 copy-start.6
  655.0 2.2 copy-start.5
  657.3 2.0 copy-start.4

commit v3 on v2

--- a/solution.py
+++ b/solution.py
@@ -11,7 +11,8 @@
 WIDTH = 4
 EPSILON = 1e-06
 LANES = 128
-VMEM_BYTES = 56 * 1024 * 1024
+VMEM_BYTES = 60 * 1024 * 1024
+MOST_VMEM_BYTES = 63 * 1024 * 1024
 ENTRY_TILE = 256
 MLP_TILE = 256
 GRAD_TILE = 512
@@ -996,7 +997,8 @@
     def __init__(self, kind, refs, start, rows):
         self.kind = kind
         self.part, self.total, self.up, self.down, self.low = refs[:5]
-        self.over, self.pair = refs[5:] if len(refs) > 5 else (None, self.part)
+        self.over = refs[5] if len(refs) > 5 else None
+        self.pair = self.part if self.over is None else self.over
         self.start, self.count = start, rows
         self.rows = pl.ds(start, rows)
         self.width = self.low.shape[1]
@@ -1219,7 +1221,7 @@
         outs.append(jax.ShapeDtypeStruct(shape, BF16))
         sizes = [(n_q - 1, rows, cols)] * 2 + [(rows, cols)]
         if kind in ("seq", "turn"):
-            sizes += [(n_q, rows, cols)] * 2
+            sizes += [(n_q, rows, cols)]
         scratch += [pltpu.VMEM(size, BF16) for size in sizes]
         pieces += cut
     total = pieces * (n_q + 2 * (n_q - 1) + n_seq)
@@ -1234,7 +1236,7 @@
 def line_pieces(cuts, parts, totals, scratch):
     pieces, scratch = [], list(scratch)
     for (kind, cut), part, total in zip(cuts, parts, totals):
-        take = 5 if kind in ("seq", "turn") else 3
+        take = 4 if kind in ("seq", "turn") else 3
         refs = [part, total] + scratch[:take]
         scratch = scratch[take:]
         rows = part.shape[-2] // cut
@@ -1252,26 +1254,20 @@
 
 
 def weight_sums_kernel(cuts, *refs):
-    count = len(cuts)
     near = Near()
     x, c, seq, p, q, n_q = near.x, near.c, near.seq, near.p, near.q, near.n_q
-    part, tok, back, gain, mid_grad = refs[:5]
-    parts = refs[5 : 5 + count]
-    grad_tok, gains = refs[5 + count : 7 + count]
-    totals = refs[7 + count : 7 + 2 * count]
-    own, from_core, from_x, gain_near, gain_line, send, recv, local, load, gain_send, gain_recv = refs[
-        7 + 2 * count : 18 + 2 * count
-    ]
-    line_refs = refs[18 + 2 * count :]
+    normed, weights, branch, inner, tok, back, gain, mid_grad, up_part, out_part, gate_part = refs[:11]
+    grad_tok, gains = refs[11:13]
+    totals = refs[13:18]
+    branch_part, inner_part, part, from_core, from_x, gain_near, gain_line = refs[18:25]
+    send, recv, gain_send, gain_recv = refs[25:29]
+    line_refs = refs[29:]
+    own = branch.shape[-1]
+    parts = [up_part, out_part, branch_part, gate_part, inner_part]
     lines = LineSums(near, line_pieces(cuts, parts, totals, line_refs[:-3]), line_refs[-3:-1], line_refs[-1])
     ch = Chunks((send, recv), tok.shape[0])
     seq_x, seq_c = seq + 2 - 4 * x, seq + 1 - 2 * c
     seq_cx = seq_c + 2 - 4 * x
-    loads = [
-        pltpu.make_async_copy(part.at[at], own.at[i], load.at[i]) for i, at in enumerate((seq_x, seq))
-    ]
-    for copy in loads:
-        copy.start()
     origin = near.dp * near.n_seq + seq
     others = [{"dp": near.dp, "seq": (seq + d) % near.n_seq} for d in range(1, near.n_seq)]
     others += [near.over_y]
@@ -1282,30 +1278,56 @@
     pl.semaphore_wait(
         pltpu.get_barrier_semaphore(), len(others + along) + lines.moves.astype(jnp.int32)
     )
+
+    def enter_norm(at):
+        rows = branch[at], inner[at]
+        part[at, :, :] = (
+            contract_cols(rows[0], weights[:, :own]) + contract_cols(rows[1], weights[:, own : 2 * own])
+        ).astype(BF16)
+
+    def weight_blocks(target, grads, places):
+        height = target.shape[1]
+
+        def one(block, carry):
+            at = 2 * block + places
+            columns = normed[:, pl.ds(pl.multiple_of(at * height, height), height)]
+            target[at, :, :] = contract_rows(columns, grads[...].reshape(-1, own)).astype(BF16)
+            return carry
+
+        lax.fori_loop(0, n_q, one, 0)
+
+    numbers = [[n for n, piece in enumerate(lines.pieces) if piece.part is ref] for ref in parts]
+    ready, out_n, branch_n, gate_n, inner_n = numbers
+    waiting = out_n + branch_n + gate_n + inner_n
     CORE_FAR, CORE_NEAR, SUM_X = range(3)
-    for group, at, slot in ((CORE_FAR, seq_cx, 0), (CORE_NEAR, seq_c, 1)):
+    lines.z_steps(ready, 1)
+    lines.y_start(*out_n)
+    for group, slot, at, mine in ((CORE_FAR, 0, seq_cx, seq_x), (CORE_NEAR, 1, seq_c, seq)):
+        enter_norm(at)
         for i in range(CHUNKS):
             r = ch.rows(i)
             ch.go(group, i, part.at[at, r], from_core.at[slot, r], near.core)
-    ready = [n for n, piece in enumerate(lines.pieces) if piece.over is None]
-    waiting = [n for n, piece in enumerate(lines.pieces) if piece.over is not None]
-    ahead = 2
-    lines.y_start(*waiting[:ahead])
-    lines.z_steps(ready, 1)
-    for copy in loads:
-        copy.wait()
+        enter_norm(mine)
+    weight_blocks(branch_part, branch, 1 - p)
+    lines.y_start(*branch_n)
     for i in range(CHUNKS):
         r = ch.rows(i)
         ch.arrived(CORE_FAR, i, from_core.at[0, r], near.core)
-        from_core[0, r, :] = (own[0, r, :].astype(F32) + from_core[0, r, :].astype(F32)).astype(BF16)
+        from_core[0, r, :] = from_core[0, r, :] + part[seq_x, r, :]
         ch.go(SUM_X, i, from_core.at[0, r], from_x.at[r], near.over_x)
     lines.z_steps(ready, 2)
+    weight_blocks(branch_part, branch, p)
+    weight_blocks(inner_part, inner, 1 - p)
+    lines.y_start(*gate_n, *inner_n)
+    for k in range(3, n_q):
+        lines.z_steps(ready, k)
+    weight_blocks(inner_part, inner, p)
     gain_sum = jnp.zeros_like(gain)
     for i in range(CHUNKS):
         r = ch.rows(i)
         ch.arrived(CORE_NEAR, i, from_core.at[1, r], near.core)
         ch.arrived(SUM_X, i, from_x.at[r], near.over_x)
-        total = own[1, r, :].astype(F32) + from_core[1, r, :].astype(F32) + from_x[r, :].astype(F32)
+        total = part[seq, r, :].astype(F32) + from_core[1, r, :].astype(F32) + from_x[r, :].astype(F32)
         value = tok[r, :].astype(F32)
         scale = lax.rsqrt(jnp.mean(value * value, axis=-1, keepdims=True) + EPSILON)
         unit = value * scale
@@ -1334,22 +1356,20 @@
             copy.start()
 
     gain_step(0)
-    for k in range(3, n_q):
-        lines.z_steps(ready, k)
-    gain_step(1)
-    for t in range(len(waiting) + n_q):
+    for t in range(len(waiting) + n_q - 1):
         if t < len(waiting):
             lines.pair_up(waiting[t])
-            lines.y_start(*waiting[t + ahead : t + ahead + 1])
         for k in range(1, n_q):
             if 0 <= t - (k - 1) < len(waiting):
                 lines.z_step(waiting[t - (k - 1)], k)
         if 0 <= t - (n_q - 1) < len(waiting):
             lines.finish(waiting[t - (n_q - 1)])
         if t == 0:
+            gain_step(1)
+            lines.finish_all(ready)
+        if t == 1:
             gain_step(2)
-            lines.finish_all(ready)
-        if t == 2:
+        if t == len(waiting) - 1:
             gain_step(3)
     total = gain_near[6, :, :]
     for i, copy in enumerate(copies):
@@ -1360,26 +1380,30 @@
     lines.close()
 
 
-def weight_sums(place, part, tok, back, gain, mid_grad, parts, cuts):
+def weight_sums(place, normed, weights, back_branch, back_inner, tok, back, gain, mid_grad, up_part, out_part, gate_part):
     rows, width = tok.shape
+    n_q, n_seq, n_dp = place.n_q, place.n_seq, place.n_dp
+    own = back_branch.shape[1]
     vmem, kept = pl.BlockSpec(memory_space=pltpu.VMEM), pl.BlockSpec(memory_space=pl.ANY)
-    outs, scratch = line_scratch(place, parts, cuts)
-    n_q = place.n_q
+    made = jax.ShapeDtypeStruct((n_dp, width // n_dp, own), BF16)
+    cuts = (("rows", 4), ("turn", 1), ("seq", 2), ("turn", 1), ("seq", 2))
+    outs, scratch = line_scratch(place, [up_part, out_part, made, gate_part, made], cuts)
+    by_seq = lambda a: a.reshape(n_seq, rows, own)
     return pl.pallas_call(
         partial(weight_sums_kernel, cuts),
-        in_specs=[kept] + [vmem] * (4 + len(parts)),
-        out_specs=[vmem, vmem] + [kept] * len(parts),
+        in_specs=[vmem] * 11,
+        out_specs=[vmem, vmem] + [kept] * len(cuts),
         out_shape=[jax.ShapeDtypeStruct((rows, width), F32), jax.ShapeDtypeStruct((TILE, width), F32)] + outs,
         scratch_shapes=[
-            pltpu.VMEM((2, rows, width), BF16),
+            pltpu.VMEM(made.shape, BF16),
+            pltpu.VMEM(made.shape, BF16),
+            pltpu.VMEM((n_seq, rows, width), BF16),
             pltpu.VMEM((2, rows, width), BF16),
             pltpu.VMEM((rows, width), BF16),
             pltpu.VMEM((7, TILE, width), F32),
             pltpu.VMEM((n_q - 1, TILE, width), F32),
             pltpu.SemaphoreType.DMA((3 * CHUNKS,)),
             pltpu.SemaphoreType.DMA((3 * CHUNKS,)),
-            pltpu.SemaphoreType.DMA((1,)),
-            pltpu.SemaphoreType.DMA((2,)),
             pltpu.SemaphoreType.DMA((2 + n_q,)),
             pltpu.SemaphoreType.DMA((2 + n_q,)),
         ]
@@ -1388,7 +1412,7 @@
             collective_id=3, has_side_effects=True, vmem_limit_bytes=VMEM_BYTES
         ),
         name="weight_sums",
-    )(part, tok, back, gain, mid_grad, *parts)
+    )(normed, weights, by_seq(back_branch), by_seq(back_inner), tok, back, gain, mid_grad, up_part, out_part, gate_part)
 
 
 class PlaneSum:
@@ -1403,6 +1427,8 @@
         half = CHUNKS // 2
         self.half, self.first, self.last = half, range(half), range(half, CHUNKS)
         self.loads = [pltpu.make_async_copy(part.at[i, 0], own.at[i], local.at[i]) for i in range(2)]
+
+    def load(self):
         for load in self.loads:
             load.start()
 
@@ -1421,8 +1447,6 @@
         return self.own[other_p, other_x, r, :].astype(F32) + self.from_core[group, r, :].astype(F32)
 
     def start(self):
-        for load in self.loads:
-            load.wait()
         self.to_core(self.FAR, (0, self.half, 1, self.half + 1))
         self.to_core(self.TO_X, self.first)
         self.to_core(self.TO_Y, self.last)
@@ -1432,6 +1456,8 @@
 
     def corners(self):
         near, ch = self.near, self.ch
+        for load in self.loads:
+            load.wait()
         for i in (0, self.half, 1, self.half + 1):
             r = ch.rows(i)
             self.from_core[self.FAR, r, :] = self.on_chip(self.FAR, i).astype(BF16)
@@ -1475,53 +1501,76 @@
     def scratch(count, width):
         block = pltpu.VMEM((count, width), BF16)
         half = pltpu.VMEM((count // 2, width), BF16)
-        return [
-            pltpu.VMEM((2, 2, count, width), BF16), pltpu.VMEM((4, count, width), BF16), half, half, block, block
-        ]
+        return [pltpu.VMEM((4, count, width), BF16), half, half, block, block]
 
 
 def back_middle_kernel(cuts, *refs):
-    count = len(cuts)
-    part, down_part, middle, cot, gain = refs[:5]
-    grads = refs[5 : 5 + count]
-    back, rows, gain_grad, result = refs[5 + count : 9 + count]
-    totals = refs[9 + count : 9 + 2 * count]
-    rest = refs[9 + 2 * count :]
-    plane_a, plane_b, low = rest[:6], rest[6:12], rest[12]
-    send, recv, local, loads_a, loads_b = rest[13:18]
-    line_refs = rest[18:]
+    part, down_part, rows_in, cots_in, middle, cot, gain, hidden, back_gate, back_up = refs[:10]
+    back, rows, gain_grad, result, up_out = refs[10:15]
+    totals = refs[15:17]
+    own, plane_a, plane_b, low = refs[17], refs[18:23], refs[23:28], refs[28]
+    grad_down, grad_gate, grad_up, tiles = refs[29:33]
+    send, recv, local, loads_a, loads_b, tile_sem, up_sem = refs[33:40]
+    line_refs = refs[40:]
     near = Near()
     x, c, seq = near.x, near.c, near.seq
     ch = Chunks((send, recv), cot.shape[0])
     seq_x, seq_c = seq + 2 - 4 * x, seq + 1 - 2 * c
     seq_cx = seq_c + 2 - 4 * x
-    lines = LineSums(near, line_pieces(cuts, grads, totals, line_refs[:-3]), line_refs[-3:-1], line_refs[-1])
-    main = PlaneSum(near, ch, 0, part, loads_a, *plane_a)
-    side = PlaneSum(near, ch, 8, down_part, loads_b, *plane_b)
+    lines = LineSums(
+        near, line_pieces(cuts, (grad_down, grad_gate), totals, line_refs[:-3]), line_refs[-3:-1], line_refs[-1]
+    )
+    main = PlaneSum(near, ch, 0, part, loads_a, own, *plane_a)
+    side = PlaneSum(near, ch, 8, down_part, loads_b, own, *plane_b)
+    main.load()
+
+    cols = tiles.shape[2]
+    order = [(source, t) for group in ((3, 0), (2, 1)) for source in (cots_in, rows_in) for t in group]
+    fetches = [
+        pltpu.make_async_copy(source.at[:, pl.ds(t * cols, cols)], tiles.at[n % 2], tile_sem.at[n % 2])
+        for n, (source, t) in enumerate(order)
+    ]
+    tile_number = iter(range(len(order)))
+    for fetch in fetches[:2]:
+        fetch.start()
+    ups = []
+
+    def gradients(times):
+        for _ in range(times):
+            n = next(tile_number)
+            source, t = order[n]
+            fetches[n].wait()
+            if source is cots_in:
+                grad_down[:, t * cols : (t + 1) * cols] = contract_rows(hidden[...], tiles[n % 2]).astype(BF16)
+            else:
+                grad_gate[t, :, :] = contract_rows(tiles[n % 2], back_gate[...]).astype(BF16)
+                if ups:
+                    ups[-1].wait()
+                grad_up[...] = contract_rows(tiles[n % 2], back_up[...]).astype(BF16)
+                ups.append(pltpu.make_async_copy(grad_up, up_out.at[t], up_sem.at[0]))
+                ups[-1].start()
+            if n + 2 < len(order):
+                fetches[n + 2].start()
+
     expected = greet_lines(near, [near.core, near.over_x, near.over_y])
     pl.semaphore_wait(pltpu.get_barrier_semaphore(), expected)
     OWN_X, OWN_C, FWD_C = 16, 17, 18
     half = len(lines.pieces) // 2
     early, late = range(half), range(half, 2 * half)
-    steps = range(1, near.n_q)
-    schedule = [partial(lines.z_steps, group, k) for k in steps for group in (early, late)]
-    schedule += [partial(lines.finish_all, early), partial(lines.finish_all, late)]
-    schedule = iter(schedule)
-
-    def along_z():
-        work = next(schedule, None)
-        if work is not None:
-            work()
-
     main.start()
-    along_z()
-    along_z()
+    gradients(2)
+    lines.z_steps(early, 1)
     main.corners()
-    along_z()
+    gradients(1)
     main.straight()
+    gradients(1)
+    lines.z_steps(late, 1)
+    gradients(2)
     main.turned()
     side.start()
-    along_z()
+    lines.z_steps(early, 2)
+    gradients(2)
+    lines.z_steps(late, 2)
     gain_sum = jnp.zeros_like(gain)
     kept = []
     for i in range(CHUNKS):
@@ -1541,21 +1590,22 @@
         keep.start()
         kept.append(keep)
     gain_grad[...] = gain_sum
+    side.load()
+    lines.z_steps(early, 3)
     side.corners()
-    along_z()
     side.straight()
-    along_z()
+    lines.z_steps(late, 3)
     for i in range(CHUNKS):
         here = rows.at[seq_x, ch.rows(i)]
         ch.arrived(OWN_X, i, here, near.over_x)
         ch.go(FWD_C, i, here, here, near.core)
     side.turned()
-    along_z()
+    lines.finish_all(early)
     for i in range(CHUNKS):
         r = ch.rows(i)
         result[r, :] = (middle[r, :] + side.total(i)).astype(BF16)
-    for _ in range(2 * near.n_q):
-        along_z()
+    lines.finish_all(late)
+    ups[-1].wait()
     for i in range(CHUNKS):
         ch.arrived(OWN_C, i, rows.at[seq_c, ch.rows(i)], near.core)
         ch.arrived(FWD_C, i, rows.at[seq_cx, ch.rows(i)], near.core)
@@ -1565,38 +1615,49 @@
     lines.close()
 
 
-def sum_back_middle(place, part, down_part, middle, cot, gain, grads):
+def sum_back_middle(place, part, down_part, rows, cots, middle, cot, gain, hidden, back_gate, back_up):
     count, width = cot.shape
+    tokens, units = hidden.shape
+    n_q = place.n_q
     cuts = (("columns", 4), ("rows", 4))
     vmem, kept = pl.BlockSpec(memory_space=pltpu.VMEM), pl.BlockSpec(memory_space=pl.ANY)
-    outs, scratch = line_scratch(place, grads, cuts)
+    made = jax.ShapeDtypeStruct((units, width), BF16), jax.ShapeDtypeStruct((n_q, width // n_q, units), BF16)
+    outs, scratch = line_scratch(place, made, cuts)
     return pl.pallas_call(
         partial(back_middle_kernel, cuts),
-        in_specs=[kept, kept] + [vmem] * (3 + len(grads)),
-        out_specs=[vmem, kept, vmem, vmem] + [kept] * len(grads),
+        in_specs=[kept] * 4 + [vmem] * 6,
+        out_specs=[vmem, kept, vmem, vmem, kept, kept, kept],
         out_shape=[
             jax.ShapeDtypeStruct((count, width), F32),
             jax.ShapeDtypeStruct((place.n_seq, count, width), BF16),
             jax.ShapeDtypeStruct((1, width), F32),
             jax.ShapeDtypeStruct((count, width), BF16),
+            made[1],
         ]
         + outs,
-        scratch_shapes=PlaneSum.scratch(count, width)
+        scratch_shapes=[pltpu.VMEM((2, 2, count, width), BF16)]
+        + PlaneSum.scratch(count, width)
         + PlaneSum.scratch(count, width)
         + [
             pltpu.VMEM((count, width), BF16),
+            pltpu.VMEM(made[0].shape, BF16),
+            pltpu.VMEM(made[1].shape, BF16),
+            pltpu.VMEM(made[1].shape[1:], BF16),
+            pltpu.VMEM((2, tokens, width // n_q), BF16),
             pltpu.SemaphoreType.DMA((19 * CHUNKS,)),
             pltpu.SemaphoreType.DMA((19 * CHUNKS,)),
             pltpu.SemaphoreType.DMA((CHUNKS,)),
             pltpu.SemaphoreType.DMA((2,)),
             pltpu.SemaphoreType.DMA((2,)),
+            pltpu.SemaphoreType.DMA((2,)),
+            pltpu.SemaphoreType.DMA((1,)),
         ]
         + scratch,
         compiler_params=pltpu.CompilerParams(
-            collective_id=2, has_side_effects=True, vmem_limit_bytes=VMEM_BYTES
+            collective_id=2, has_side_effects=True, vmem_limit_bytes=MOST_VMEM_BYTES
         ),
         name="sum_back_middle",
-    )(part, down_part, middle, cot, gain, *grads)
+    )(part, down_part, rows, cots, middle, cot, gain, hidden, back_gate, back_up)
 
 
 def entry_kernel(x_ref, w_ref, normed_ref, branch_ref, inner_ref, gains_ref):
@@ -1696,42 +1757,39 @@
 
 
 def exit_kernel(
-    normed_ref, back_out_ref, w_ref, branch_ref, inner_ref, mixed_ref,
-    grad_branch_ref, grad_inner_ref, grad_output_ref, part_ref,
+    normed_ref, w_ref, branch_ref, inner_ref, grad_branch_ref, grad_inner_ref, part_ref
 ):
     own = branch_ref.shape[1]
     normed = normed_ref[...]
     grad_branch_ref[...] = contract_rows(normed, branch_ref[...]).astype(BF16)
     grad_inner_ref[...] = contract_rows(normed, inner_ref[...]).astype(BF16)
-    grad_output_ref[...] = contract_rows(mixed_ref[...], back_out_ref[...]).astype(BF16)
     part_ref[...] = (
         contract_cols(branch_ref[...], w_ref[:, :own]) + contract_cols(inner_ref[...], w_ref[:, own : 2 * own])
     ).astype(BF16)
 
 
-def exit_products(normed, back_out, weights, back_branch, back_inner, mixed, tile):
+def exit_products(normed, weights, back_branch, back_inner, tile):
     rows, width = normed.shape
-    own = mixed.shape[1]
+    own = back_inner.shape[1]
     columns = pl.BlockSpec((rows, tile), lambda i: (0, i))
     whole = pl.BlockSpec((rows, own), lambda i: (0, 0), pipeline_mode=pl.Buffered(1))
     by_tile = lambda cols: pl.BlockSpec((tile, cols), lambda i: (i, 0))
     return pl.pallas_call(
         exit_kernel,
         grid=(width // tile,),
-        in_specs=[columns, columns, by_tile(weights.shape[1]), whole, whole, whole],
-        out_specs=[by_tile(own), by_tile(own), pl.BlockSpec((own, tile), lambda i: (0, i)), columns],
+        in_specs=[columns, by_tile(weights.shape[1]), whole, whole],
+        out_specs=[by_tile(own), by_tile(own), columns],
         out_shape=[
             jax.ShapeDtypeStruct((width, own), BF16),
             jax.ShapeDtypeStruct((width, own), BF16),
-            jax.ShapeDtypeStruct((own, width), BF16),
             jax.ShapeDtypeStruct((rows, width), BF16),
         ],
         compiler_params=pltpu.CompilerParams(vmem_limit_bytes=VMEM_BYTES),
         cost_estimate=pl.CostEstimate(
-            flops=10 * rows * width * own, bytes_accessed=rows * width * 6 + own * (rows + width) * 10, transcendentals=0
+            flops=8 * rows * width * own, bytes_accessed=rows * width * 6 + own * (rows + width) * 10, transcendentals=0
         ),
         name="exit_products",
-    )(normed, back_out, weights, back_branch, back_inner, mixed)
+    )(normed, weights, back_branch, back_inner)
 
 
 def shards(
@@ -1761,7 +1819,7 @@
     )
     vectors = jnp.pad(vectors.T, ((0, 0), (0, LANES - 2 * WIDTH)))
     out_pack = jnp.concatenate([output_weight, rate_weight, entry_weight, vectors], axis=1)
-    fast = place.n_x == 2
+    fast = place.n_x == 2 and place.n_q == 4
     if fast:
         in_all, out_all, group_x, cot_c, cot_o = gather_all(place, in_pack, out_pack, tokens, cotangent)
         in_all = in_all.reshape(n_dp * n_seq * d_rows, -1)
@@ -1836,16 +1894,16 @@
     units = gate_weight.shape[1] // 2
 
     n_q = place.n_q
-    grad_down_part, grad_gate_part, grad_up_part = mlp_grads(rows, pair_cot, hidden, back_gate, back_up, GRAD_TILE)
-    grad_gate_part, grad_up_part = (a.reshape(n_q, -1, units) for a in (grad_gate_part, grad_up_part))
     if fast:
         plane = (2, 2, 2, tok, width)
-        back_middle, back_out, grad_mlp_gain, result, down_sum, gate_sum = sum_back_middle(
-            place, back_part.reshape(plane), down_part.reshape(plane), middle, cotangent, gain_mid,
-            [grad_down_part, grad_gate_part],
+        back_middle, back_out, grad_mlp_gain, result, grad_up_part, down_sum, gate_sum = sum_back_middle(
+            place, back_part.reshape(plane), down_part.reshape(plane), rows, pair_cot, middle, cotangent, gain_mid,
+            hidden, back_gate, back_up,
         )
         grad_mlp_gain = grad_mlp_gain[0]
     else:
+        grad_down_part, grad_gate_part, grad_up_part = mlp_grads(rows, pair_cot, hidden, back_gate, back_up, GRAD_TILE)
+        grad_gate_part, grad_up_part = (a.reshape(n_q, -1, units) for a in (grad_gate_part, grad_up_part))
         plane = (2, n_seq, tok, width)
         result = (middle + scatter_plane(place, down_part.reshape(plane))).astype(BF16)
         back_norm, grad_mlp_gain = rms_back(middle, gain_mid, scatter_plane(place, back_part.reshape(plane)))
@@ -1866,6 +1924,7 @@
     back_out = back_out.reshape(count, width)
 
     back_mixed = contract_cols(back_out, w_out)
+    grad_output_part = contract_rows(mixed, back_out).astype(BF16)
     if fast:
         back_branch, back_gates, direct, gate_sums = by_block(
             backward_gates_kernel, gate_first, gate_ins + [("own", states), ("own", back_mixed)],
@@ -1906,29 +1965,27 @@
         )
         for a in (back_gates[0], back_gates[1])
     )
-    grad_branch_part, grad_inner_part, grad_output_part, normed_part = exit_products(
-        normed, back_out, in_all, back_branch, back_inner, mixed, EXIT_TILE
-    )
-    normed_part = normed_part.reshape(n_seq, tok, width)
 
     sums = jnp.concatenate([conv_sums[: WIDTH + 1], gate_sums[:3]], axis=0).T
     sums = jnp.pad(sums, ((0, 0), (0, LANES - 2 * WIDTH))).astype(BF16)
     gate_grads = jnp.concatenate([grad_rate_part.astype(BF16), grad_entry_part.astype(BF16), sums], axis=1)
-    parts = [
-        a.reshape(n_dp, -1, a.shape[1]) for a in (grad_output_part, grad_branch_part, gate_grads, grad_inner_part)
-    ]
+    by_dp = lambda a: a.reshape(n_dp, -1, a.shape[1])
     if fast:
         grad_tokens, gains, up_sum, output_sum, branch_sum, gates_sum, inner_sum = weight_sums(
-            place, normed_part, tokens, back_middle, gain_in, grad_mlp_gain[None], [grad_up_part] + parts,
-            (("rows", 4), ("turn", 1), ("seq", 2), ("turn", 1), ("seq", 2)),
+            place, normed, in_all, back_branch, back_inner, tokens, back_middle, gain_in, grad_mlp_gain[None],
+            grad_up_part, by_dp(grad_output_part), by_dp(gate_grads),
         )
         gains = lax.dynamic_slice_in_dim(gains[:2], (place.dp * n_seq + place.seq) * d_rows, d_rows, axis=1)
     else:
-        back_x, grad_norm_gain = rms_back(whole_x, gain_in, scatter_seq(place, normed_part))
+        grad_branch_part, grad_inner_part, normed_part = exit_products(normed, in_all, back_branch, back_inner, EXIT_TILE)
+        back_x, grad_norm_gain = rms_back(
+            whole_x, gain_in, scatter_seq(place, normed_part.reshape(n_seq, tok, width))
+        )
         grad_tokens = back_middle + back_x
         gains = lax.psum_scatter(
             jnp.stack([grad_norm_gain, grad_mlp_gain]), BOTH, scatter_dimension=1, tiled=True
         )
+        parts = [by_dp(a) for a in (grad_output_part, grad_branch_part, gate_grads, grad_inner_part)]
         totals = [sum_dp(place, a) for a in parts]
         output_sum, gates_sum = (turned(place, totals[i], True) for i in (0, 2))
         branch_sum, inner_sum = (

time: 671 us -> 624 us (0.930)
  Pallas kernels: 596 us -> 543 us
    pallas_call x4 -> x2, Pallas kernels: 325 us -> 283 us  [the longest x1 154 us: weight_sums(): pl.pallas_call(partial(weight_sums_kernel, cuts), in_specs=[vmem] * 11, o...]
    pallas_call x1, Pallas kernels: 99.2 us -> 88.6 us  [sum_middle(): pl.pallas_call(middle_kernel, in_specs=[vmem] * 4 + [kept] * 6, out_specs...]
  transfers between devices with their start and end apart: 4 -> 4, of which waited for: 1 -> 1; matrix products, arithmetic and copies ran while one was open for 2% -> 3% of each run, Pallas kernels for 5% -> 5%
where the time goes in v3:
time: 624 us; the launch traced here: 613 us
  Pallas kernels  543 us (87%)
  local copies, waits for them, and re-layouts  25.7 us (4%)
  other arithmetic  18.9 us (3%)
  matrix products  14.3 us (2%)
  starting transfers between devices  8.51 us (1%)
    pallas_call x1, Pallas kernels, weight_sums(): pl.pallas_call(partial(weight_sums_kernel, cuts), in_specs=[vmem] * 11, o...  154 us
    pallas_call x1, Pallas kernels, sum_back_middle(): pl.pallas_call(partial(back_middle_kernel, cuts), in_specs=[kept] * 4 + [...  129 us
    pallas_call x1, Pallas kernels, gather_all(): pl.pallas_call(gather_kernel, in_specs=[pl.BlockSpec(memory_space=pltpu.V...  115 us
    pallas_call x1, Pallas kernels, sum_middle(): pl.pallas_call(middle_kernel, in_specs=[vmem] * 4 + [kept] * 6, out_specs...  88.6 us
    pallas_call x4, Pallas kernels, by_block(): pl.pallas_call(kernel, grid_spec=pltpu.PrefetchScalarGridSpec(num_scalar_...  44.4 us
  transfers between devices with their start and end apart: 4, of which 1 were waited for; matrix products, arithmetic and copies ran while one was open for 3% of the time, Pallas kernels for 5%

profile of v3, /device:TPU:19, one launch (start us, length us, event | category | flops | bytes accessed | tf_op | source)
XLA Modules:
  0.0 613.3 jit_solution(17939122574671775438)
XLA Ops:
  5.3 114.8 %gather_all.1 = (bf16[8,4,64,1408]{3,2,1,0:T(8,128)(2,1)}, bf16[8,80,2688]{2,1,0:T(8,128)(2,1)}, bf16[4,256,2048]{2,1,0:T(8,128)(2,1)}, bf16[2,256,2048]{2,1,0:T(8,128)(2,1)}, bf16[2,256,2048]{2,1,0:T(8,128)(2,1)}) custom-call(bf16[4,64,1408]{2,1,0:T(8,128)(2,1)} %pad_maximum_fusion.in_pack, bf16[80,2688]{1,0:T(8,128)(2,1)} %fusion.27.out_pack, ...), custom_call_target="tpu_custom_call" | custom-call | tf_op jit(solution)/shard_map/gather_all/pallas_call | solution.py:763
  120.1 1.6 slice_select_fusion
  121.7 5.5 collective-permute-start.2
  130.3 12.4 %entry_products.1 = (bf16[1024,2048]{1,0:T(8,128)(2,1)}, f32[1024,640]{1,0:T(8,128)}, bf16[1024,640]{1,0:T(8,128)(2,1)}, f32[8,2048]{1,0:T(8,128)}) custom-call(bf16[1024,2048]{1,0:T(8,128)(2,1)} %bitcast.86, bf16[2048,1408]{1,0:T(8,128)(2,1)} %bitcast.63), custom_call_target="tpu_custom_call" | custom-call | flops 5368709120 | bytes 18087936 | tf_op jit(solution)/shard_map/entry_products/pallas_call | solution.py:1682
  142.7 6.2 %shard_map.305 = bf16[1024,768]{1,0:T(8,128)(2,1)} custom-call(s32[1]{0:T(128)} %bitcast.first_ref, bf16[1024,640]{1,0:T(8,128)(2,1)} %get-tuple-element.60.inner_ref, f32[8,640]{1,0:T(8,128)} %broadcast_select_fusion.taps_ref, s32[1024,1]{1,0:T(8,128)} %iota_subtract_fusion.offset_ref), custom_call_target="tpu_custom_call" | custom-call | flops 39321600 | bytes 2670592 | tf_op jit(solution)/shard_map/pallas_call | solution.py:500
  148.9 1.7 constant_dynamic-slice_fusion.2
  151.8 1.9 slice.154.w_out
  153.7 1.5 fusion.32
  155.8 1.6 maximum_select_fusion
  158.4 1.7 constant_dynamic-update-slice_fusion.1.block_ref.conv_ref
  160.1 12.2 %shard_map.306 = (f32[1024,640]{1,0:T(8,128)}, bf16[1024,640]{1,0:T(8,128)(2,1)}) custom-call(s32[1]{0:T(128)} %bitcast.first_ref, bf16[1024,768]{1,0:T(8,128)(2,1)} %constant_dynamic-update-slice_fusion.1.block_ref.conv_ref, bf16[768,256]{1,0:T(8,128)(2,1)} %get-tuple-element.174.w_rate_ref, bf16[768,256]{1,0:T(8,128)(2,1)} %get-tuple-element.173.w_entry_ref, ...), custom_call_target="tpu_custom_call" | custom-call | flops 39321600 | bytes 13156352 | tf_op jit(solution)/shard_map/pallas_call | solution.py:500
  173.5 88.6 %sum_middle.1 = (f32[256,2048]{1,0:T(8,128)}, bf16[8,256,2048]{2,1,0:T(8,128)(2,1)}, bf16[8,256,2048]{2,1,0:T(8,128)(2,1)}, bf16[8,256,768]{2,1,0:T(8,128)(2,1)}...) custom-call(bf16[4,256,640]{2,1,0:T(8,128)(2,1)} %bitcast.77, ...), custom_call_target="tpu_custom_call" | custom-call | tf_op jit(solution)/shard_map/sum_middle/pallas_call | solution.py:964
  262.1 129.3 %sum_back_middle.1 = (f32[256,2048]{1,0:T(8,128)}, bf16[4,256,2048]{2,1,0:T(8,128)(2,1)}, f32[1,2048]{1,0:T(1,128)}, bf16[256,2048]{1,0:T(8,128)(2,1)}, bf16[4,5...) custom-call(bf16[2,2,2,256,2048]{4,3,2,1,0:T(8,128)(2,1)} %bitcast.62, ...), custom_call_target="tpu_custom_call" | custom-call | tf_op jit(solution)/shard_map/sum_back_middle/pallas_call | solution.py:1626
  391.4 8.1 %fusion.28.back_ref = f32[1024,640]{1,0:T(8,128)} fusion(bf16[1024,2048]{1,0:T(8,128)(2,1)} %bitcast.87, bf16[640,2688]{1,0:T(8,128)(2,1)} %bitcast.67), kind=kOutput, calls=%fused_computation.67 | convolution fusion | flops 2684354560 | bytes 9437184 | tf_op jit(solution)/shard_map/dot_general | solution.py:34
  399.5 4.2 convolution_convert_fusion
  403.7 16.5 %shard_map.307 = (bf16[1024,640]{1,0:T(8,128)(2,1)}, bf16[2,1024,768]{2,1,0:T(8,128)(2,1)}, f32[1024,640]{1,0:T(8,128)}, f32[8,640]{1,0:T(8,128)}) custom-call(s32[1]{0:T(128)} %bitcast.first_ref, bf16[1024,768]{1,0:T(8,128)(2,1)} %constant_dynamic-update-slice_fusion.1.block_ref.conv_ref, bf16[768,256]{1,0:T(8,128)(2,1)} %get-tuple-element.174.w_rate_ref, ...), custom_call_target="tpu_custom_call" | custom-call | flops 39321600 | bytes 23642112 | tf_op jit(solution)/shard_map/pallas_call | solution.py:500
  422.1 2.8 collective-permute-start.3
  424.8 1.3 convert_element_type.52
  427.8 1.4 copy-done.2
  432.3 9.5 %shard_map.308 = (bf16[1024,640]{1,0:T(8,128)(2,1)}, f32[8,640]{1,0:T(8,128)}) custom-call(s32[1]{0:T(128)} %bitcast.first_ref, bf16[2,1024,768]{2,1,0:T(8,128)(2,1)} %copy-done.2, bf16[768,256]{1,0:T(8,128)(2,1)} %get-tuple-element.174.w_rate_ref, bf16[768,256]{1,0:T(8,128)(2,1)} %get-tuple-element.173.w_entry_ref, ...), custom_call_target="tpu_custom_call" | custom-call | flops 39321600 | bytes 15777792 | tf_op jit(solution)/shard_map/pallas_call | solution.py:500
  445.5 154.0 %weight_sums.1 = (f32[256,2048]{1,0:T(8,128)}, f32[8,2048]{1,0:T(8,128)}, bf16[256,1536]{1,0:T(8,128)(2,1)}, bf16[80,2048]{1,0:T(8,128)(2,1)}, bf16[64,2560]{1,0...) custom-call(bf16[1024,2048]{1,0:T(8,128)(2,1)} %get-tuple-element.78.refs_0_, ...), custom_call_target="tpu_custom_call" | custom-call | tf_op jit(solution)/shard_map/weight_sums/pallas_call | solution.py:1392
  599.5 1.5 fusion.31
  604.8 1.9 convert_element_type.48
  608.5 1.3 convert_element_type.53
  (91 shorter events, 30.6 us)
Async XLA Ops:
  0.7 3.8 copy-start.13
  0.7 3.8 copy-start.14
  0.7 3.8 copy-start.10
  5.3 122.8 %copy-start.17 = (s32[1,4]{1,0:T(1,128)S(1)}, s32[1,4]{1,0:T(1,128)}, u32[]{:S(2)}) copy-start(s32[1,4]{1,0:T(1,128)} %param.19) | copy-start | bytes 52
  5.3 123.1 %copy-start.15 = (pred[8]{0:T(512)(128)(4,1)S(1)}, pred[8]{0:T(512)(128)(4,1)}, u32[]{:S(2)}) copy-start(pred[8]{0:T(512)(128)(4,1)} %constant.71.clone.1) | copy-start | bytes 28
  121.7 34.1 %collective-permute-start.1 = (bf16[128,512]{1,0:T(8,128)(2,1)}, bf16[128,512]{1,0:T(8,128)(2,1)}, u32[]{:S(2)}, u32[]{:S(2)}) collective-permute-start(bf16[128,512]{1,0:T(8,128)(2,1)} %slice_select_fusion), channel_id=1, source_target_pairs={{0,1},{1,0},{2,3},{3,2},{4,5},{5,4},{6,7},{7,6},{8,9},{9,8},{10,11... | collective-permute-start | bytes 393224 | tf_op jit(solution)/shard_map/ppermute | solution.py:51
  121.7 51.8 %collective-permute-start.2 = (bf16[2,256,2048]{2,1,0:T(8,128)(2,1)}, bf16[2,256,2048]{2,1,0:T(8,128)(2,1)}, u32[]{:S(2)}, u32[]{:S(2)}) collective-permute-start(bf16[2,256,2048]{2,1,0:T(8,128)(2,1)} %get-tuple-element.64.cot_c), channel_id=1, source_target_pairs={{0,4},{4,0},{8,12},{12,8},{16,20},{20,16},{24,28},{28,24},{1,5},{5... | collective-permute-start | bytes 6291464 | tf_op jit(solution)/shard_map/ppermute | solution.py:54
  142.7 8.2 %copy-start.3 = (bf16[8,80,2688]{2,1,0:T(8,128)(2,1)S(1)}, bf16[8,80,2688]{2,1,0:T(8,128)(2,1)}, u32[]{:S(2)}) copy-start(bf16[8,80,2688]{2,1,0:T(8,128)(2,1)} %get-tuple-element.61) | copy-start | bytes 10321924
  150.6 7.8 %collective-permute-start = (bf16[1024,128]{1,0:T(8,128)(2,1)}, bf16[1024,128]{1,0:T(8,128)(2,1)}, u32[]{:S(2)}, u32[]{:S(2)}) collective-permute-start(bf16[1024,128]{1,0:T(8,128)(2,1)} %constant_dynamic-slice_fusion.2), channel_id=1, source_target_pairs={{0,1},{1,0},{2,3},{3,2},{4,5},{5,4},{6,7},{7,6},{8,9},{9,8},{10,11... | collective-permute-start | bytes 786440 | tf_op jit(solution)/shard_map/ppermute | solution.py:51
  391.4 8.1 %copy-start.5 = (bf16[1024,640]{1,0:T(8,128)(2,1)S(1)}, bf16[1024,640]{1,0:T(8,128)(2,1)}, u32[]{:S(2)}) copy-start(bf16[1024,640]{1,0:T(8,128)(2,1)} %get-tuple-element.65) | copy-start | bytes 3932164
  391.4 8.1 %copy-start.16 = (bf16[4,256,2048]{2,1,0:T(8,128)(2,1)S(1)}, bf16[4,256,2048]{2,1,0:T(8,128)(2,1)}, u32[]{:S(2)}) copy-start(bf16[4,256,2048]{2,1,0:T(8,128)(2,1)} %get-tuple-element.80) | copy-start | bytes 12582916
  403.7 21.2 %copy-start.9 = (bf16[256,1536]{1,0:T(8,128)(2,1)S(1)}, bf16[256,1536]{1,0:T(8,128)(2,1)}, u32[]{:S(2)}) copy-start(bf16[256,1536]{1,0:T(8,128)(2,1)} %get-tuple-element.96) | copy-start | bytes 2359300
  420.9 5.3 copy-start.8
  422.1 5.4 collective-permute-start.3
  424.8 2.6 copy-start.1
  427.6 1.7 copy-start.2
  427.6 2.5 copy-start
  599.5 7.2 %copy-start.12 = (bf16[64,2560]{1,0:T(8,128)(2,1)S(1)}, bf16[64,2560]{1,0:T(8,128)(2,1)}, u32[]{:S(2)}) copy-start(bf16[64,2560]{1,0:T(8,128)(2,1)} %get-tuple-element.92) | copy-start | bytes 983044
  599.5 8.1 %copy-start.11 = (bf16[80,2048]{1,0:T(8,128)(2,1)S(1)}, bf16[80,2048]{1,0:T(8,128)(2,1)}, u32[]{:S(2)}) copy-start(bf16[80,2048]{1,0:T(8,128)(2,1)} %get-tuple-element.93) | copy-start | bytes 983044
  602.0 6.5 %copy-start.7 = (bf16[256,1536]{1,0:T(8,128)(2,1)S(1)}, bf16[256,1536]{1,0:T(8,128)(2,1)}, u32[]{:S(2)}) copy-start(bf16[256,1536]{1,0:T(8,128)(2,1)} %get-tuple-element.97) | copy-start | bytes 2359300
  607.6 2.2 copy-start.6
  609.8 2.0 copy-start.4
